TPU v7x, 128 devices: a whole 4x4x4 slice. The times are simulated.
128 devices in a mesh: store: 16 (over x, y), section: 4 (over z), tp: 2 (over core).
Axes of the slice: x: 4, y: 4, z: 4, core: 2. Of those that a mesh axis runs over, the one named last changes fastest.
Arguments:
- tokens: bfloat16 [8192, 2048], P(('store', 'section')), may hold values from -32 to 32
- attn_gain: bfloat16 [2048], replicated, may hold values from 0.099609375 to 1.8984375
- w_query: bfloat16 [2048, 3072], P(None, 'tp'), may hold values from -0.125 to 0.125
- w_latent: bfloat16 [2048, 576], replicated, may hold values from -0.125 to 0.125
- kv_gain: bfloat16 [512], replicated, may hold values from 0.099609375 to 1.8984375
- w_key_up: bfloat16 [16, 512, 128], P('tp'), may hold values from -0.5 to 0.5
- w_value_up: bfloat16 [16, 512, 128], P('tp'), may hold values from -0.25 to 0.25
- w_out: bfloat16 [2048, 2048], P('tp'), may hold values from -0.125 to 0.125
- mlp_gain: bfloat16 [2048], replicated, may hold values from 0.099609375 to 1.8984375
- w_gate: bfloat16 [2048, 1408], P(None, 'tp'), may hold values from -0.125 to 0.125
- w_up: bfloat16 [2048, 1408], P(None, 'tp'), may hold values from -0.125 to 0.125
- w_down: bfloat16 [1408, 2048], P('tp'), may hold values from -0.15625 to 0.15625
- page_pool: bfloat16 [128, 256, 576], P('store'), may hold values from -96 to 96
- hit_owner: int32 [16, 24, 1], replicated, may hold values from 0 to 15; in each aligned block of 24 rows (0 to 23, 24 to 47, ..., all dimensions but the last counted through in order) at most 2 rows name the same one
- hit_slot: int32 [16, 24], replicated, may hold values from 0 to 7
- fetch_count: int32 [16], replicated, may hold values from 1 to 24, 240 in all
Outputs:
- layer_out: bfloat16 [8192, 2048], P(('store', 'section'), 'tp')
- new_latent: bfloat16 [8192, 576], P(('store', 'section'))
Inputs may be any that keep to these rules, and one draw needn't show every extreme that they name: `hit_owner`: no store device holds more than 2 of the pages listed for one request. Only the first fetch_count[g] entries of request g's lists are its cached prefix, the rest are padding; the largest count is 24.
All inputs are finite; a program needn't handle non-finite values.
Results may differ from a plain program's by a relative error of at most 0.015.
Values may be sent and summed in bfloat16 or wider, within the bound.
No kernel may reach another device: no remote copies, remote signals or barrier semaphores. Data moves between devices by JAX's collectives and lax.ppermute only.
A program may use at most 128 MiB of HBM per device.

v0:
```python
import jax
import jax.numpy as jnp
from jax import lax
from jax.sharding import PartitionSpec as P

NOPE = 128
ROPE = 64
KVR = 512
PAGE = 256
PB = 4


EPSILON = 1e-06
ROTARY_BASE = 10000.0
MASKED_SCORE = -1e30


def rms_scale(values, gain_vec):
    mean_sq = jnp.mean(values * values, axis=-1, keepdims=True)
    return values * lax.rsqrt(mean_sq + EPSILON) * gain_vec.astype(values.dtype)


def angles(position, rot_width):
    half_dim = rot_width // 2
    freq_table = ROTARY_BASE ** (-(jnp.arange(half_dim, dtype=jnp.float32) / half_dim))
    return position[:, None] * freq_table[None, :]


def rotate(values, angle_table):
    half_dim = values.shape[-1] // 2
    lower_half = values[..., :half_dim]
    upper_half = values[..., half_dim:]
    cosine = jnp.cos(angle_table)
    sine_val = jnp.sin(angle_table)
    return jnp.concatenate(
        [lower_half * cosine - upper_half * sine_val, lower_half * sine_val + upper_half * cosine],
        axis=-1,
    )


def fetch_plan(owner_row, slot_row, live_count, source, capacity):
    matched = (owner_row == source).astype(jnp.int32)
    rank_pos = jnp.cumsum(matched) - 1
    live_flag = (jnp.arange(owner_row.shape[0], dtype=jnp.int32) < live_count).astype(jnp.int32)
    pick_table = matched[None, :] * (
        rank_pos[None, :] == jnp.arange(capacity, dtype=jnp.int32)[:, None]
    ).astype(jnp.int32)
    slot_ids = jnp.sum(pick_table * slot_row[None, :], axis=1)
    is_valid = jnp.sum(pick_table * live_flag[None, :], axis=1) > 0
    return (slot_ids, is_valid)


def on_device(
    tokens,
    attn_gain,
    w_query,
    w_latent,
    kv_gain,
    w_key_up,
    w_value_up,
    w_out,
    mlp_gain,
    w_gate,
    w_up,
    w_down,
    page_pool,
    hit_owner,
    hit_slot,
    fetch_count,
):
    n_store = lax.axis_size("store")
    n_tp = lax.axis_size("tp")
    group_index = lax.axis_index("store")
    section_index = lax.axis_index("section")
    tp_index = lax.axis_index("tp")
    tok_rows = tokens.shape[0]
    head_count = w_key_up.shape[0]
    hit_count = hit_owner.shape[1]
    capacity = max(2, 3 * hit_count // (2 * n_store))
    score_scale = (NOPE + ROPE) ** (-0.5)
    owners = hit_owner[:, :, 0]
    prefix_pages = fetch_count[group_index]
    offset = section_index * tok_rows + jnp.arange(tok_rows, dtype=jnp.int32)
    position = (prefix_pages * PAGE + offset).astype(jnp.float32)
    normed = rms_scale(tokens.astype(jnp.float32), attn_gain).astype(jnp.bfloat16)
    queries = jnp.dot(normed, w_query, preferred_element_type=jnp.float32).astype(jnp.bfloat16)
    queries = queries.reshape(tok_rows, head_count, NOPE + ROPE)
    query_rot = rotate(
        queries[:, :, NOPE:].astype(jnp.float32), angles(position, ROPE)[:, None, :]
    ).astype(jnp.bfloat16)
    query_lat = jnp.einsum(
        "thn,hcn->thc", queries[:, :, :NOPE], w_key_up, preferred_element_type=jnp.float32
    ).astype(jnp.bfloat16)
    probes = jnp.concatenate([query_lat, query_rot], axis=-1).reshape(
        tok_rows * head_count, KVR + ROPE
    )
    latent_raw = jnp.dot(normed, w_latent, preferred_element_type=jnp.float32)
    latent = rms_scale(latent_raw[:, :KVR], kv_gain)
    key_rot = rotate(latent_raw[:, KVR:], angles(position, ROPE))
    new_latent = jnp.concatenate([latent, key_rot], axis=-1).astype(jnp.bfloat16)

    def attend(attn_state, key_block, key_mask):
        row_top, row_total, row_acc = attn_state
        scores = (
            jnp.einsum("rc,kc->rk", probes, key_block, preferred_element_type=jnp.float32)
            * score_scale
        )
        scores = jnp.where(key_mask, scores, MASKED_SCORE)
        new_top = jnp.maximum(row_top, jnp.max(scores, axis=1))
        weight = jnp.where(key_mask, jnp.exp(scores - new_top[:, None]), 0.0)
        fade_factor = jnp.exp(row_top - new_top)
        new_total = row_total * fade_factor + jnp.sum(weight, axis=1)
        summed = jnp.dot(
            weight.astype(jnp.bfloat16), key_block[:, :KVR], preferred_element_type=jnp.float32
        )
        return (new_top, new_total, row_acc * fade_factor[:, None] + summed)

    n_query = tok_rows * head_count
    attn_state = (
        jnp.full((n_query,), MASKED_SCORE, jnp.float32),
        jnp.zeros((n_query,), jnp.float32),
        jnp.zeros((n_query, KVR), jnp.float32),
    )
    send_slots, _ = jax.vmap(
        lambda owner_row, slot_row, live_count: fetch_plan(
            owner_row, slot_row, live_count, group_index, capacity
        )
    )(owners, hit_slot, fetch_count)
    _, recv_valid = jax.vmap(
        lambda source: fetch_plan(
            owners[group_index], hit_slot[group_index], prefix_pages, source, capacity
        )
    )(jnp.arange(n_store, dtype=jnp.int32))
    flat_valid = recv_valid.reshape(n_store * capacity)
    outgoing = page_pool[send_slots]
    incoming = lax.all_to_all(outgoing, "store", split_axis=0, concat_axis=0, tiled=True)
    attend_attn_state = attn_state
    page_block = incoming.reshape(n_store * capacity, PAGE, KVR + ROPE)
    n_pages = page_block.shape[0]
    page_rows = page_block.shape[1]
    n_blocks = n_pages // PB
    key_blocks = page_block.reshape(n_blocks, PB * page_rows, KVR + ROPE)
    live_mask = jnp.repeat(flat_valid.reshape(n_blocks, PB), page_rows, axis=1)

    def scan_block(carried, scan_item):
        key_block, block_live = scan_item
        carried = attend(carried, key_block, block_live[None, :])
        return (carried, None)

    attend_attn_state, _ = lax.scan(scan_block, attend_attn_state, (key_blocks, live_mask))
    attn_state = attend_attn_state
    query_pos = jnp.repeat(offset, head_count)
    piece_block = lax.all_gather(new_latent, "section", axis=0, tiled=True)
    key_pos = jnp.arange(piece_block.shape[0], dtype=jnp.int32)
    attn_state = attend(attn_state, piece_block, key_pos[None, :] <= query_pos[:, None])
    row_top, row_total, row_acc = attn_state
    mixed = (row_acc / row_total[:, None]).astype(jnp.bfloat16).reshape(tok_rows, head_count, KVR)
    per_head = jnp.einsum(
        "thc,hcv->thv", mixed, w_value_up, preferred_element_type=jnp.float32
    ).astype(jnp.bfloat16)
    per_head = per_head.reshape(tok_rows, head_count * w_value_up.shape[2])
    partial_value = jnp.dot(per_head, w_out, preferred_element_type=jnp.float32)
    attended = lax.psum(partial_value.astype(jnp.bfloat16), "tp").astype(jnp.float32)
    middle = (tokens.astype(jnp.float32) + attended).astype(jnp.bfloat16)
    mlp_in = rms_scale(middle.astype(jnp.float32), mlp_gain).astype(jnp.bfloat16)
    gate_act = jnp.dot(mlp_in, w_gate, preferred_element_type=jnp.float32)
    up_act = jnp.dot(mlp_in, w_up, preferred_element_type=jnp.float32)
    hidden = (jax.nn.silu(gate_act) * up_act).astype(jnp.bfloat16)
    down_part = jnp.dot(hidden, w_down, preferred_element_type=jnp.float32)
    out_width = down_part.shape[1] // n_tp
    reduced = lax.psum_scatter(
        down_part.astype(jnp.bfloat16), "tp", scatter_dimension=1, tiled=True
    ).astype(jnp.float32)
    own_part = lax.dynamic_slice_in_dim(middle, tp_index * out_width, out_width, 1)
    layer_out = (own_part.astype(jnp.float32) + reduced).astype(jnp.bfloat16)
    return (layer_out, new_latent)


def solution(mesh):
    in_specs = (
        P(("store", "section"), None),
        P(),
        P(None, "tp"),
        P(),
        P(),
        P("tp", None, None),
        P("tp", None, None),
        P("tp", None),
        P(),
        P(None, "tp"),
        P(None, "tp"),
        P("tp", None),
        P("store", None, None),
        P(),
        P(),
        P(),
    )
    out_specs = (P(("store", "section"), "tp"), P(("store", "section"), None))
    return jax.shard_map(
        on_device, mesh=mesh, in_specs=in_specs, out_specs=out_specs, check_vma=False
    )
```

profile of v0, /device:TPU:1, one launch (start us, length us, event | category | flops | bytes accessed | tf_op | source)
XLA Modules:
  0.0 387.1 jit_solution(5195139103866843342)
XLA Ops:
  9.2 7.0 %gather_fusion = bf16[32,256,576]{1,2,0:T(8,128)(2,1)} fusion(bf16[8,256,576]{1,2,0:T(8,128)(2,1)} %param.30, s32[1024]{0:T(1024)S(1)} %pad_clamp_fusion), kind=kCustom, calls=%fused_computation | custom fusion | bytes 18874496 | tf_op jit(solution)/shard_map/gather | solution.py:135
  16.3 7.6 %all-to-all-start = ((bf16[16,2,256,576]{2,3,1,0:T(8,128)(2,1)}), bf16[16,2,256,576]{2,3,1,0:T(8,128)(2,1)}, u32[]{:S(2)}, u32[]{:S(2)}) async-start(bf16[16,2,256,576]{2,3,1,0:T(8,128)(2,1)} %bitcast.45), calls=%async_computation | async-start | bytes 18874368 | tf_op jit(solution)/shard_map/all_to_all | solution.py:136
  31.5 4.6 %convolution_convert_fusion.2 = bf16[128,1536]{1,0:T(8,128)(2,1)} fusion(bf16[2048,1536]{1,0:T(8,128)(2,1)} %param.20, bf16[128,2048]{1,0:T(8,128)(2,1)S(1)} %copy-done.3, f32[2048]{0:T(1024)S(1)} %convert_element_type.121, f32[128]{0:T(128)S(1)} %add_rsqrt_fusion.2), kind=kOutput, calls=%fused_computation.26 | convolution fusion | flops 806551552 | bytes 7217664 | tf_op jit(solution)/shard_map/dot_general | solution.py:86
  50.7 14.5 %all_gather.3 = bf16[512,576]{0,1:T(8,128)(2,1)S(1)} all-gather(bf16[128,576]{0,1:T(8,128)(2,1)S(1)} %pad_maximum_fusion.1), channel_id=1, replica_groups=mesh['store'=16,'section'=4,'tp'=2] {'section'}, dimensions={0}, use_global_device_ids=true | all-gather | bytes 737280 | tf_op jit(solution)/shard_map/all_gather | solution.py:153
  69.9 117.5 %all-to-all-done = bf16[16,2,256,576]{2,3,1,0:T(8,128)(2,1)} async-done(((bf16[16,2,256,576]{2,3,1,0:T(8,128)(2,1)}), bf16[16,2,256,576]{2,3,1,0:T(8,128)(2,1)}, u32[]{:S(2)}, u32[]{:S(2)}) %all-to-all-start) | async-done | bytes 9437216 | tf_op jit(solution)/shard_map/all_to_all | solution.py:136
  187.5 14.1 %copy.74 = bf16[16,2,256,576]{3,2,1,0:T(8,128)(2,1)} copy(bf16[16,2,256,576]{2,3,1,0:T(8,128)(2,1)} %all-to-all-done) | data formatting | bytes 18874368
  201.6 112.8 %while.15 = (s32[]{:T(128)}, f32[1024]{0:T(1024)S(1)}, f32[1024]{0:T(1024)S(1)}, f32[1024,512]{1,0:T(8,128)}, pred[8,1024]{1,0:T(8,128)(4,1)S(1)}, /*index=5*/bf...) while((s32[]{:T(128)}, f32[1024]{0:T(1024)S(1)}, ...), condition=%wide.region_8.9_spmd.clone, body=%wide.region_5.8_spmd.clone.sunk | while | flops 2296910848 | bytes 48829636 | solution.py:150
  203.4 4.0 %fusion.84 = (f32[1024]{0:T(1024)S(1)}, f32[1024,1024]{1,0:T(8,128)}) fusion(pred[1024]{0:T(1024)(128)(4,1)S(1)} %dynamic-slice_reduce_fusion.2, bf16[1024,576]{1,0:T(8,128)(2,1)S(1)} %dynamic-slice_bitcast_fusion.3, bf16[1024,576]{1,0:T(8,128)(2,1)S(1)} %copy-done.11), kind=kOutput, calls=%fused_computation.3.clone.1 | convolution fusion | flops 1211104256 | bytes 6558720 | tf_op jit(solution)/shard_map/while/body/eval_jaxpr/rc,kc->rk/dot_general | solution.py:105
  210.8 4.3 %fusion.87 = f32[1024,512]{1,0:T(8,128)} fusion(f32[1024,512]{1,0:T(8,128)} %get-tuple-element.177, f32[1024,1024]{1,0:T(8,128)S(1)} %copy-done.1, f32[1024]{0:T(1024)S(1)} %select_maximum_fusion.2, pred[1024]{0:T(1024)(128)(4,1)S(1)} %dynamic-slice_reduce_fusion.2, bf16[1024,576]{1,0:T(8,128)(2,1)} %copy-done.2, f32[1024]{0:T(1024)S(1)} %get-tuple-element.164, ...), kind=kOutput, calls=%fused_computation.8.clone.1 | convolution fusion | flops 1080557568 | bytes 9446401 | tf_op jit(solution)/shard_map/while/body/eval_jaxpr/dot_general | solution.py:113
  216.8 4.0 %fusion.84 = (f32[1024]{0:T(1024)S(1)}, f32[1024,1024]{1,0:T(8,128)}) fusion(pred[1024]{0:T(1024)(128)(4,1)S(1)} %dynamic-slice_reduce_fusion.2, bf16[1024,576]{1,0:T(8,128)(2,1)S(1)} %dynamic-slice_bitcast_fusion.3, bf16[1024,576]{1,0:T(8,128)(2,1)S(1)} %copy-done.11), kind=kOutput, calls=%fused_computation.3.clone.1 | convolution fusion | flops 1211104256 | bytes 6558720 | tf_op jit(solution)/shard_map/while/body/eval_jaxpr/rc,kc->rk/dot_general | solution.py:105
  224.3 5.0 %fusion.87 = f32[1024,512]{1,0:T(8,128)} fusion(f32[1024,512]{1,0:T(8,128)} %get-tuple-element.177, f32[1024,1024]{1,0:T(8,128)S(1)} %copy-done.1, f32[1024]{0:T(1024)S(1)} %select_maximum_fusion.2, pred[1024]{0:T(1024)(128)(4,1)S(1)} %dynamic-slice_reduce_fusion.2, bf16[1024,576]{1,0:T(8,128)(2,1)} %copy-done.2, f32[1024]{0:T(1024)S(1)} %get-tuple-element.164, ...), kind=kOutput, calls=%fused_computation.8.clone.1 | convolution fusion | flops 1080557568 | bytes 9446401 | tf_op jit(solution)/shard_map/while/body/eval_jaxpr/dot_general | solution.py:113
  231.0 4.0 %fusion.84 = (f32[1024]{0:T(1024)S(1)}, f32[1024,1024]{1,0:T(8,128)}) fusion(pred[1024]{0:T(1024)(128)(4,1)S(1)} %dynamic-slice_reduce_fusion.2, bf16[1024,576]{1,0:T(8,128)(2,1)S(1)} %dynamic-slice_bitcast_fusion.3, bf16[1024,576]{1,0:T(8,128)(2,1)S(1)} %copy-done.11), kind=kOutput, calls=%fused_computation.3.clone.1 | convolution fusion | flops 1211104256 | bytes 6558720 | tf_op jit(solution)/shard_map/while/body/eval_jaxpr/rc,kc->rk/dot_general | solution.py:105
  238.5 5.0 %fusion.87 = f32[1024,512]{1,0:T(8,128)} fusion(f32[1024,512]{1,0:T(8,128)} %get-tuple-element.177, f32[1024,1024]{1,0:T(8,128)S(1)} %copy-done.1, f32[1024]{0:T(1024)S(1)} %select_maximum_fusion.2, pred[1024]{0:T(1024)(128)(4,1)S(1)} %dynamic-slice_reduce_fusion.2, bf16[1024,576]{1,0:T(8,128)(2,1)} %copy-done.2, f32[1024]{0:T(1024)S(1)} %get-tuple-element.164, ...), kind=kOutput, calls=%fused_computation.8.clone.1 | convolution fusion | flops 1080557568 | bytes 9446401 | tf_op jit(solution)/shard_map/while/body/eval_jaxpr/dot_general | solution.py:113
  245.2 4.0 %fusion.84 = (f32[1024]{0:T(1024)S(1)}, f32[1024,1024]{1,0:T(8,128)}) fusion(pred[1024]{0:T(1024)(128)(4,1)S(1)} %dynamic-slice_reduce_fusion.2, bf16[1024,576]{1,0:T(8,128)(2,1)S(1)} %dynamic-slice_bitcast_fusion.3, bf16[1024,576]{1,0:T(8,128)(2,1)S(1)} %copy-done.11), kind=kOutput, calls=%fused_computation.3.clone.1 | convolution fusion | flops 1211104256 | bytes 6558720 | tf_op jit(solution)/shard_map/while/body/eval_jaxpr/rc,kc->rk/dot_general | solution.py:105
  252.6 5.0 %fusion.87 = f32[1024,512]{1,0:T(8,128)} fusion(f32[1024,512]{1,0:T(8,128)} %get-tuple-element.177, f32[1024,1024]{1,0:T(8,128)S(1)} %copy-done.1, f32[1024]{0:T(1024)S(1)} %select_maximum_fusion.2, pred[1024]{0:T(1024)(128)(4,1)S(1)} %dynamic-slice_reduce_fusion.2, bf16[1024,576]{1,0:T(8,128)(2,1)} %copy-done.2, f32[1024]{0:T(1024)S(1)} %get-tuple-element.164, ...), kind=kOutput, calls=%fused_computation.8.clone.1 | convolution fusion | flops 1080557568 | bytes 9446401 | tf_op jit(solution)/shard_map/while/body/eval_jaxpr/dot_general | solution.py:113
  259.4 4.0 %fusion.84 = (f32[1024]{0:T(1024)S(1)}, f32[1024,1024]{1,0:T(8,128)}) fusion(pred[1024]{0:T(1024)(128)(4,1)S(1)} %dynamic-slice_reduce_fusion.2, bf16[1024,576]{1,0:T(8,128)(2,1)S(1)} %dynamic-slice_bitcast_fusion.3, bf16[1024,576]{1,0:T(8,128)(2,1)S(1)} %copy-done.11), kind=kOutput, calls=%fused_computation.3.clone.1 | convolution fusion | flops 1211104256 | bytes 6558720 | tf_op jit(solution)/shard_map/while/body/eval_jaxpr/rc,kc->rk/dot_general | solution.py:105
  266.8 5.0 %fusion.87 = f32[1024,512]{1,0:T(8,128)} fusion(f32[1024,512]{1,0:T(8,128)} %get-tuple-element.177, f32[1024,1024]{1,0:T(8,128)S(1)} %copy-done.1, f32[1024]{0:T(1024)S(1)} %select_maximum_fusion.2, pred[1024]{0:T(1024)(128)(4,1)S(1)} %dynamic-slice_reduce_fusion.2, bf16[1024,576]{1,0:T(8,128)(2,1)} %copy-done.2, f32[1024]{0:T(1024)S(1)} %get-tuple-element.164, ...), kind=kOutput, calls=%fused_computation.8.clone.1 | convolution fusion | flops 1080557568 | bytes 9446401 | tf_op jit(solution)/shard_map/while/body/eval_jaxpr/dot_general | solution.py:113
  281.0 5.0 %fusion.87 = f32[1024,512]{1,0:T(8,128)} fusion(f32[1024,512]{1,0:T(8,128)} %get-tuple-element.177, f32[1024,1024]{1,0:T(8,128)S(1)} %copy-done.1, f32[1024]{0:T(1024)S(1)} %select_maximum_fusion.2, pred[1024]{0:T(1024)(128)(4,1)S(1)} %dynamic-slice_reduce_fusion.2, bf16[1024,576]{1,0:T(8,128)(2,1)} %copy-done.2, f32[1024]{0:T(1024)S(1)} %get-tuple-element.164, ...), kind=kOutput, calls=%fused_computation.8.clone.1 | convolution fusion | flops 1080557568 | bytes 9446401 | tf_op jit(solution)/shard_map/while/body/eval_jaxpr/dot_general | solution.py:113
  295.2 5.0 %fusion.87 = f32[1024,512]{1,0:T(8,128)} fusion(f32[1024,512]{1,0:T(8,128)} %get-tuple-element.177, f32[1024,1024]{1,0:T(8,128)S(1)} %copy-done.1, f32[1024]{0:T(1024)S(1)} %select_maximum_fusion.2, pred[1024]{0:T(1024)(128)(4,1)S(1)} %dynamic-slice_reduce_fusion.2, bf16[1024,576]{1,0:T(8,128)(2,1)} %copy-done.2, f32[1024]{0:T(1024)S(1)} %get-tuple-element.164, ...), kind=kOutput, calls=%fused_computation.8.clone.1 | convolution fusion | flops 1080557568 | bytes 9446401 | tf_op jit(solution)/shard_map/while/body/eval_jaxpr/dot_general | solution.py:113
  301.9 4.0 %fusion.84 = (f32[1024]{0:T(1024)S(1)}, f32[1024,1024]{1,0:T(8,128)}) fusion(pred[1024]{0:T(1024)(128)(4,1)S(1)} %dynamic-slice_reduce_fusion.2, bf16[1024,576]{1,0:T(8,128)(2,1)S(1)} %dynamic-slice_bitcast_fusion.3, bf16[1024,576]{1,0:T(8,128)(2,1)S(1)} %copy-done.11), kind=kOutput, calls=%fused_computation.3.clone.1 | convolution fusion | flops 1211104256 | bytes 6558720 | tf_op jit(solution)/shard_map/while/body/eval_jaxpr/rc,kc->rk/dot_general | solution.py:105
  309.4 5.0 %fusion.87 = f32[1024,512]{1,0:T(8,128)} fusion(f32[1024,512]{1,0:T(8,128)} %get-tuple-element.177, f32[1024,1024]{1,0:T(8,128)S(1)} %copy-done.1, f32[1024]{0:T(1024)S(1)} %select_maximum_fusion.2, pred[1024]{0:T(1024)(128)(4,1)S(1)} %dynamic-slice_reduce_fusion.2, bf16[1024,576]{1,0:T(8,128)(2,1)} %copy-done.2, f32[1024]{0:T(1024)S(1)} %get-tuple-element.164, ...), kind=kOutput, calls=%fused_computation.8.clone.1 | convolution fusion | flops 1080557568 | bytes 9446401 | tf_op jit(solution)/shard_map/while/body/eval_jaxpr/dot_general | solution.py:113
  322.7 33.0 %all-reduce.2.cloned.1.call-done = bf16[128,2048]{1,0:T(8,128)(2,1)} async-done(((bf16[128,2048]{1,0:T(8,128)(2,1)}), bf16[128,2048]{1,0:T(8,128)(2,1)}) %all-reduce.2.cloned.1.call-update) | async-done | bytes 524304 | tf_op jit(solution)/shard_map/psum | solution.py:163
  361.3 5.1 %convolution_convert_fusion = bf16[128,2048]{1,0:T(8,128)(2,1)} fusion(bf16[704,2048]{1,0:T(8,128)(2,1)S(1)} %copy-done, bf16[2048,704]{0,1:T(8,128)(2,1)} %param.28, f32[128,704]{0,1:T(8,128)} %fusion.51, bf16[128,2048]{1,0:T(8,128)(2,1)} %copy-done.4, f32[2048]{0:T(1024)S(1)} %convert_element_type.138, f32[128]{0:T(128)S(1)} %add_rsqrt_fusion), kind=kOutput, calls=%fused_computation.24 | convolution fusion | flops 740048896 | bytes 7184896 | tf_op jit(solution)/shard_map/dot_general | solution.py:169
  366.4 12.2 %reduce-scatter.2.cloned.1.call-done = bf16[128,1024]{1,0:T(8,128)(2,1)} async-done(((bf16[128,2048]{1,0:T(8,128)(2,1)}), bf16[128,1024]{1,0:T(8,128)(2,1)}) %reduce-scatter.2.cloned.1.call-update) | async-done | bytes 262160 | tf_op jit(solution)/shard_map/reduce_scatter | solution.py:171
  (199 shorter events, 92.7 us)
Async XLA Ops:
  7.2 354.1 %copy-start = (bf16[704,2048]{1,0:T(8,128)(2,1)S(1)}, bf16[704,2048]{1,0:T(8,128)(2,1)}, u32[]{:S(2)}) copy-start(bf16[704,2048]{1,0:T(8,128)(2,1)} %param.29) | copy-start | bytes 8650756
  16.3 7.7 %copy-start.17 = (bf16[2048]{0:T(1024)(128)(2,1)S(1)}, bf16[2048]{0:T(1024)(128)(2,1)}, u32[]{:S(2)}) copy-start(bf16[2048]{0:T(1024)(128)(2,1)} %param.19) | copy-start | bytes 12292
  16.3 7.7 %copy-start.21 = (s32[16]{0:T(128)S(1)}, s32[16]{0:T(128)}, u32[]{:S(2)}) copy-start(s32[16]{0:T(128)} %param.33) | copy-start | bytes 196
  16.3 9.6 %copy-start.3 = (bf16[128,2048]{1,0:T(8,128)(2,1)S(1)}, bf16[128,2048]{1,0:T(8,128)(2,1)}, u32[]{:S(2)}) copy-start(bf16[128,2048]{1,0:T(8,128)(2,1)} %param.18) | copy-start | bytes 1572868
  16.3 171.2 %all-to-all-start = ((bf16[16,2,256,576]{2,3,1,0:T(8,128)(2,1)}), bf16[16,2,256,576]{2,3,1,0:T(8,128)(2,1)}, u32[]{:S(2)}, u32[]{:S(2)}) async-start(bf16[16,2,256,576]{2,3,1,0:T(8,128)(2,1)} %bitcast.45), calls=%async_computation | async-start | bytes 18874368 | tf_op jit(solution)/shard_map/all_to_all | solution.py:136
  23.9 331.7 %all-reduce.2.cloned.1.call-start = ((), (), s32[]{:S(2)}) async-start(), calls=%async_computation.2 | async-start | bytes 1048576 | tf_op jit(solution)/shard_map/psum | solution.py:163
  42.5 5.1 %copy-start.20 = (bf16[512]{0:T(512)(128)(2,1)S(1)}, bf16[512]{0:T(512)(128)(2,1)}, u32[]{:S(2)}) copy-start(bf16[512]{0:T(512)(128)(2,1)} %param.22) | copy-start | bytes 3076
  42.5 5.1 %copy-start.19 = (s32[128]{0:T(128)S(1)}, s32[128]{0:T(128)}, u32[]{:S(2)}) copy-start(s32[128]{0:T(128)} %get-tuple-element.113) | copy-start | bytes 1540
  43.9 6.1 %copy-start.16 = (bf16[128,32]{0,1:T(8,128)(2,1)S(1)}, bf16[128,32]{0,1:T(8,128)(2,1)}, u32[]{:S(2)}) copy-start(bf16[128,32]{0,1:T(8,128)(2,1)} %get-tuple-element.107) | copy-start | bytes 24580
  203.2 4.1 %copy-start.2 = (bf16[1024,576]{1,0:T(8,128)(2,1)}, bf16[1024,576]{1,0:T(8,128)(2,1)S(1)}, u32[]{:S(2)}) copy-start(bf16[1024,576]{1,0:T(8,128)(2,1)S(1)} %dynamic-slice_bitcast_fusion.3) | copy-start | bytes 3538948 | tf_op jit(solution)/shard_map/while
  207.3 3.4 copy-start.1
  216.7 4.1 %copy-start.2 = (bf16[1024,576]{1,0:T(8,128)(2,1)}, bf16[1024,576]{1,0:T(8,128)(2,1)S(1)}, u32[]{:S(2)}) copy-start(bf16[1024,576]{1,0:T(8,128)(2,1)S(1)} %dynamic-slice_bitcast_fusion.3) | copy-start | bytes 3538948 | tf_op jit(solution)/shard_map/while
  220.8 3.4 copy-start.1
  230.9 4.1 %copy-start.2 = (bf16[1024,576]{1,0:T(8,128)(2,1)}, bf16[1024,576]{1,0:T(8,128)(2,1)S(1)}, u32[]{:S(2)}) copy-start(bf16[1024,576]{1,0:T(8,128)(2,1)S(1)} %dynamic-slice_bitcast_fusion.3) | copy-start | bytes 3538948 | tf_op jit(solution)/shard_map/while
  245.1 4.1 %copy-start.2 = (bf16[1024,576]{1,0:T(8,128)(2,1)}, bf16[1024,576]{1,0:T(8,128)(2,1)S(1)}, u32[]{:S(2)}) copy-start(bf16[1024,576]{1,0:T(8,128)(2,1)S(1)} %dynamic-slice_bitcast_fusion.3) | copy-start | bytes 3538948 | tf_op jit(solution)/shard_map/while
  249.2 3.4 copy-start.1
  259.2 4.1 %copy-start.2 = (bf16[1024,576]{1,0:T(8,128)(2,1)}, bf16[1024,576]{1,0:T(8,128)(2,1)S(1)}, u32[]{:S(2)}) copy-start(bf16[1024,576]{1,0:T(8,128)(2,1)S(1)} %dynamic-slice_bitcast_fusion.3) | copy-start | bytes 3538948 | tf_op jit(solution)/shard_map/while
  263.4 3.4 copy-start.1
  273.4 4.1 %copy-start.2 = (bf16[1024,576]{1,0:T(8,128)(2,1)}, bf16[1024,576]{1,0:T(8,128)(2,1)S(1)}, u32[]{:S(2)}) copy-start(bf16[1024,576]{1,0:T(8,128)(2,1)S(1)} %dynamic-slice_bitcast_fusion.3) | copy-start | bytes 3538948 | tf_op jit(solution)/shard_map/while
  287.6 4.1 %copy-start.2 = (bf16[1024,576]{1,0:T(8,128)(2,1)}, bf16[1024,576]{1,0:T(8,128)(2,1)S(1)}, u32[]{:S(2)}) copy-start(bf16[1024,576]{1,0:T(8,128)(2,1)S(1)} %dynamic-slice_bitcast_fusion.3) | copy-start | bytes 3538948 | tf_op jit(solution)/shard_map/while
  301.8 4.1 %copy-start.2 = (bf16[1024,576]{1,0:T(8,128)(2,1)}, bf16[1024,576]{1,0:T(8,128)(2,1)S(1)}, u32[]{:S(2)}) copy-start(bf16[1024,576]{1,0:T(8,128)(2,1)S(1)} %dynamic-slice_bitcast_fusion.3) | copy-start | bytes 3538948 | tf_op jit(solution)/shard_map/while
  316.8 4.0 %copy-start.7 = (bf16[1024,2048]{1,0:T(8,128)(2,1)S(1)}, bf16[1024,2048]{1,0:T(8,128)(2,1)}, u32[]{:S(2)}) copy-start(bf16[1024,2048]{1,0:T(8,128)(2,1)} %param.25) | copy-start | bytes 12582916
  322.4 56.2 %reduce-scatter.2.cloned.1.call-start = ((), (), s32[]{:S(2)}) async-start(), calls=%async_computation.3 | async-start | bytes 786432 | tf_op jit(solution)/shard_map/reduce_scatter | solution.py:171
  361.3 17.3 %copy-start.5 = (bf16[128,2048]{1,0:T(8,128)(2,1)S(1)}, bf16[128,2048]{1,0:T(8,128)(2,1)}, u32[]{:S(2)}) copy-start(bf16[128,2048]{1,0:T(8,128)(2,1)} %copy-done.4) | copy-start | bytes 1572868
  (22 other events, 43.4 us)
Sparse Core Ops, SparseCore 0:
  322.5 33.0 all-reduce.1
  366.5 11.9 reduce-scatter.1
where the time goes:
time: 389 us; the launch traced here: 387 us
  waiting for transfers between devices  163 us (42%)
  matrix products  97 us (25%)
  local copies, waits for them, and re-layouts  48.1 us (12%)
  other arithmetic  41.5 us (11%)
  between operations  15.1 us (4%)
  blocking collectives  14.5 us (4%)
  starting transfers between devices  7.91 us (2%)
    all_to_all x1, waiting for transfers between devices, on_device(): lax.all_to_all(outgoing, 'store', split_axis=0, concat_axis=0, tiled=True)  118 us
    dot_general x9, matrix products, attend(): jnp.dot(weight.astype(jnp.bfloat16), key_block[:, :KVR], preferred_elemen...  42.7 us
    dot_general x9, matrix products, attend(): jnp.einsum('rc,kc->rk', probes, key_block, preferred_element_type=jnp.flo...  35.7 us
    psum x1, waiting for transfers between devices, on_device(): lax.psum(partial_value.astype(jnp.bfloat16), 'tp').astype(jnp.float32)  33 us
    reduce_sum x9, other arithmetic, attend(): new_total = row_total * fade_factor + jnp.sum(weight, axis=1)  29.4 us
    unnamed x40, local copies, waits for them, and re-layouts  19.1 us
    all_gather x1, blocking collectives, on_device(): piece_block = lax.all_gather(new_latent, 'section', axis=0, tiled=True)  14.5 us
    squeeze x8, local copies, waits for them, and re-layouts, on_device(): lax.scan(scan_block, attend_attn_state, (key_blocks, live_mask))  12.2 us
  transfers between devices with their start and end apart: 3, of which 3 were waited for; matrix products, arithmetic and copies ran while one was open for 7% of the time, Pallas kernels for 0%

commit v1 on v0

v1 whole, which is shorter than its diff:
```python
import functools
import math

import jax
import jax.numpy as jnp
import numpy as np
from jax import lax
from jax.experimental import pallas as pl
from jax.experimental.pallas import tpu as pltpu
from jax.sharding import PartitionSpec as P

NOPE = 128
ROPE = 64
KVR = 512
PAGE = 256
LAT = KVR + ROPE
WIDE = KVR + 2 * ROPE
MSG = 2 * LAT
VDIM = 128
EPSILON = 1e-06
ROTARY_BASE = 10000.0
MASKED_SCORE = -1e30
SCALE = (NOPE + ROPE) ** (-0.5) / math.log(2.0)
F32 = jnp.float32
BF16 = jnp.bfloat16
MB = 1024 * 1024

VMEM = pl.BlockSpec(memory_space=pltpu.VMEM)
SMEM = pl.BlockSpec(memory_space=pltpu.SMEM)
HBM = pl.BlockSpec(memory_space=pltpu.HBM)


def params(mb):
    return pltpu.CompilerParams(vmem_limit_bytes=mb * MB)


def dot(a, b):
    return jnp.dot(a, b, preferred_element_type=F32)


def dot_nt(a, b):
    return lax.dot_general(a, b, (((1,), (1,)), ((), ())), preferred_element_type=F32)


def rms(values, gain):
    mean_sq = jnp.mean(values * values, axis=-1, keepdims=True)
    return values * lax.rsqrt(mean_sq + EPSILON) * gain


def turn(values, cosine, sine):
    lane = lax.broadcasted_iota(jnp.int32, values.shape, 1)
    low = (lane & (ROPE // 2)) == 0
    partner = jnp.where(
        low, pltpu.roll(values, 128 - ROPE // 2, axis=1), pltpu.roll(values, ROPE // 2, axis=1)
    )
    return values * cosine + partner * sine


def pack_kernel(
    place, owner_src, slot_src, pool_src, out, owner, slot, pool, sems
):
    n_pages, width, page = pool.shape
    n_store, rows, _ = out.shape
    window = 128
    per = window // rows
    pairs = [(owner_src, owner), (slot_src, slot)]
    strip = n_pages // 4
    for k in range(4):
        at = pl.ds(k * strip, strip)
        pairs.append((pool_src.at[at], pool.at[at]))
    copies = [
        pltpu.make_async_copy(src, dst, sems.at[i]) for i, (src, dst) in enumerate(pairs)
    ]
    for copy in copies:
        copy.start()
    for copy in copies:
        copy.wait()
    upper = place[1] >= per
    first = (place[1] % per) * rows
    lane = lax.broadcasted_iota(jnp.int32, (width, window), 1)
    joined = []
    for at in range(0, n_pages, per):
        part = None
        for k in range(per):
            both = pool[at + k]
            moved = jnp.where(upper, both[:, window:], both[:, :window]).astype(F32)
            moved = pltpu.roll(moved, (k * rows - first + window) % window, axis=1)
            part = moved if part is None else jnp.where(lane >= k * rows, moved, part)
        joined.append(part.astype(BF16))
    stage = jnp.concatenate(joined, axis=1)
    total = n_store * rows
    n_list = owner.shape[1]
    held = owner[...] == place[0]
    entry = lax.broadcasted_iota(jnp.int32, held.shape, 1)
    low = jnp.min(jnp.where(held, entry, n_list), axis=1, keepdims=True)
    high = jnp.max(jnp.where(held, entry, -1), axis=1, keepdims=True)
    row = lax.broadcasted_iota(jnp.int32, (rows, 1), 0)
    column = lax.broadcasted_iota(jnp.int32, (total, n_pages * rows), 1)
    taken = []
    for which in (low, high):
        page = jnp.sum(jnp.where(entry == which, slot[...], 0), axis=1, keepdims=True) * rows
        wanted = [jnp.broadcast_to(page[g : g + 1], (rows, 1)) + row for g in range(n_store)]
        wanted = jnp.concatenate(wanted, axis=0)
        choose = jnp.where(column == wanted, 1.0, 0.0).astype(BF16)
        taken.append(dot_nt(choose, stage))
    ropes = jnp.concatenate([part[:, KVR:] for part in taken], axis=1)
    for which, part in enumerate(taken):
        out[:, :, which * KVR : (which + 1) * KVR] = (
            part[:, :KVR].astype(BF16).reshape(n_store, rows, KVR)
        )
    out[:, :, 2 * KVR :] = ropes.astype(BF16).reshape(n_store, rows, 2 * ROPE)


def pack_pages(place, owner, slot, pool_t, rows):
    n_store = owner.shape[0]
    return pl.pallas_call(
        pack_kernel,
        out_shape=jax.ShapeDtypeStruct((n_store, rows, MSG), BF16),
        in_specs=[SMEM] + [HBM] * 3,
        out_specs=VMEM,
        scratch_shapes=[
            pltpu.VMEM(owner.shape, jnp.int32),
            pltpu.VMEM(slot.shape, jnp.int32),
            pltpu.VMEM(pool_t.shape, BF16),
            pltpu.SemaphoreType.DMA((6,)),
        ],
        compiler_params=params(60),
        name="pack_pages",
    )(place, owner, slot, pool_t)


def keys_kernel(place, owner, count, pages, out, seen):
    rows = pages.shape[1]
    group = place[0]
    lane = lax.broadcasted_iota(jnp.int32, (rows, 128), 1)
    for k in range(pages.shape[0]):
        seen[k] = 0
    for j in range(owner.shape[1]):
        source = owner[group, j]
        second = seen[source] > 0
        seen[source] = 1
        bias = jnp.where(j < count[group], 0.0, MASKED_SCORE)
        row = pages[source]
        at = pl.ds(j * rows, rows)
        out[at, :KVR] = jnp.where(second, row[:, KVR : 2 * KVR], row[:, :KVR])
        pair = row[:, 2 * KVR :].astype(F32)
        rot = jnp.where(second, pltpu.roll(pair, ROPE, axis=1), pair)
        last = jnp.where(lane == ROPE, bias, 0.0)
        out[at, KVR:] = jnp.where(lane < ROPE, rot, last).astype(BF16)


def build_keys(place, owner, count, pages):
    n_keys = owner.shape[1] * pages.shape[1]
    return pl.pallas_call(
        keys_kernel,
        out_shape=jax.ShapeDtypeStruct((n_keys, WIDE), BF16),
        in_specs=[SMEM, SMEM, SMEM, VMEM],
        out_specs=VMEM,
        scratch_shapes=[pltpu.SMEM((pages.shape[0],), jnp.int32)],
        compiler_params=params(24),
        name="build_keys",
    )(place, owner, count, pages)


def rotation_table(n_rows):
    half = ROPE // 2
    freq = np.float32(ROTARY_BASE) ** (-(np.arange(half, dtype=np.float32) / np.float32(half)))
    angle = np.arange(n_rows, dtype=np.float32)[:, None] * freq.astype(np.float32)[None, :]
    angle = angle.astype(np.float64)
    parts = [np.cos(angle), np.cos(angle), -np.sin(angle), np.sin(angle)]
    return np.concatenate(parts, axis=1).astype(np.float32)


def project_kernel(
    place, count, tokens_src, gain, table, w_query_src, w_latent_src, kv_gain, query, new_latent, span,
    tokens, turns, w_query, w_latent_t, total, sems
):
    rows = tokens.shape[0]
    start = pl.multiple_of(count[place[0]] * PAGE + place[2] * rows, rows)
    pairs = [(tokens_src, tokens), (table.at[pl.ds(start, rows), :], turns)]
    pieces = 8
    depth = w_query.shape[0] // pieces
    for k in range(pieces):
        at = pl.ds(k * depth, depth)
        pairs.append((w_query_src.at[at, :], w_query.at[at, :]))
    strip = w_latent_t.shape[0] // 4
    for k in range(4):
        at = pl.ds(k * strip, strip)
        pairs.append((w_latent_src.at[at, :], w_latent_t.at[at, :]))
    copies = [
        pltpu.make_async_copy(src, dst, sems.at[i]) for i, (src, dst) in enumerate(pairs)
    ]
    for copy in copies:
        copy.start()
    copies[0].wait()
    normed = rms(tokens[...].astype(F32), gain[...].astype(F32)).astype(BF16)
    copies[1].wait()
    cosine, sine = turns[:, :ROPE], turns[:, ROPE:]
    cosine = jnp.concatenate([cosine, cosine], axis=1)
    sine = jnp.concatenate([sine, sine], axis=1)
    for k in range(0, pieces, 2):
        copies[2 + k].wait()
        copies[3 + k].wait()
        at = slice(k * depth, (k + 2) * depth)
        part = dot(normed[:, at], w_query[at, :])
        total[...] = part if k == 0 else total[...] + part
    head = NOPE + ROPE
    for at in range(0, query.shape[1], 2 * head):
        part = total[:, at : at + 2 * head].astype(BF16).astype(F32)
        query[:, at : at + NOPE] = part[:, :NOPE].astype(BF16)
        query[:, at + NOPE : at + 2 * NOPE] = part[:, head : head + NOPE].astype(BF16)
        pair = jnp.concatenate([part[:, NOPE:head], part[:, head + NOPE :]], axis=1)
        query[:, at + 2 * NOPE : at + 2 * head] = (turn(pair, cosine, sine) * SCALE).astype(BF16)
    for copy in copies[2 + pieces :]:
        copy.wait()
    raw = dot_nt(normed, w_latent_t[...])
    latent = rms(raw[:, :KVR], kv_gain[...].astype(F32)).astype(BF16)
    pair = jnp.concatenate([raw[:, KVR:], raw[:, KVR:]], axis=1)
    turned = turn(pair, cosine, sine)
    new_latent[:KVR, :] = latent.astype(F32).T.astype(BF16)
    new_latent[KVR:, :] = turned.T[:ROPE].astype(BF16)
    lane = lax.broadcasted_iota(jnp.int32, turned.shape, 1)
    span[:, :KVR] = latent
    span[:, KVR:] = jnp.where(lane < ROPE, turned, 0.0).astype(BF16)


def project(place, count, tokens, gain, table, w_query, w_latent_t, kv_gain):
    rows, width = tokens.shape
    cols = w_query.shape[1]
    return pl.pallas_call(
        project_kernel,
        out_shape=[
            jax.ShapeDtypeStruct((rows, cols), BF16),
            jax.ShapeDtypeStruct((LAT, rows), BF16),
            jax.ShapeDtypeStruct((rows, WIDE), BF16),
        ],
        in_specs=[SMEM] * 2 + [HBM, VMEM] + [HBM] * 3 + [VMEM],
        out_specs=[VMEM] * 3,
        scratch_shapes=[
            pltpu.VMEM(tokens.shape, BF16),
            pltpu.VMEM((rows, 2 * ROPE), F32),
            pltpu.VMEM(w_query.shape, BF16),
            pltpu.VMEM(w_latent_t.shape, BF16),
            pltpu.VMEM((rows, cols), F32),
            pltpu.SemaphoreType.DMA((14,)),
        ],
        compiler_params=params(60),
        cost_estimate=pl.CostEstimate(
            flops=2 * rows * width * (cols + LAT),
            bytes_accessed=2 * width * (cols + LAT),
            transcendentals=0,
        ),
        name="project",
    )(place, count, tokens, gain, table, w_query, w_latent_t, kv_gain)


def attend_kernel(by, n_section, place, query, key_up, value_up, near, *refs):
    n_head, rows = key_up.shape[0], query.shape[0]
    if len(refs) == 5:
        arrived, span, out, far, probes = refs
        far[...] = arrived[...]
    else:
        far, span, out, probes = refs
    blocks = (near, far, span)
    lane = lax.broadcasted_iota(jnp.int32, (rows, 128), 1)
    head_pair = 2 * (NOPE + ROPE)
    at_once = 2
    tile = at_once * rows
    steps = n_head // at_once
    width = n_head * NOPE
    for h in range(n_head):
        at = pl.ds(h * rows, rows)
        base = (h // 2) * head_pair
        nope = query[:, base + (h % 2) * NOPE : base + (h % 2 + 1) * NOPE]
        probes[at, :KVR] = (dot_nt(nope, key_up[h]) * SCALE).astype(BF16)
        pair = query[:, base + 2 * NOPE : base + head_pair].astype(F32)
        if h % 2 == 1:
            pair = pltpu.roll(pair, ROPE, axis=1)
        one = jnp.where(lane == ROPE, 1.0, 0.0)
        probes[at, KVR:] = jnp.where(lane < ROPE, pair, one).astype(BF16)

    if by == 0:
        row_of = lax.broadcasted_iota(jnp.int32, (tile, rows), 0) & (rows - 1)
        key_of = lax.broadcasted_iota(jnp.int32, (tile, rows), 1)
        hide = jnp.where(key_of <= row_of, 0.0, MASKED_SCORE)
    else:
        hide = jnp.where(place[2] + by < n_section, 0.0, MASKED_SCORE)

    def score(i):
        probe = probes[i * tile : (i + 1) * tile, :]
        parts = [dot_nt(probe, block[...]) for block in blocks]
        parts[2] = parts[2] + hide
        return parts

    def finish(i, parts, stats):
        tops = [jnp.max(part, axis=1, keepdims=True) for part in parts]
        top = functools.reduce(jnp.maximum, tops)
        total, summed = 0.0, 0.0
        for part, block in zip(parts, blocks):
            weight = jnp.exp2(part - top)
            total = total + jnp.sum(weight, axis=1, keepdims=True)
            summed = summed + dot(weight.astype(BF16), block[:, :KVR])
        mixed = (summed * (1.0 / total)).astype(BF16)
        level = top + jnp.log2(total)
        for k in range(at_once):
            h = i * at_once + k
            value = dot(mixed[k * rows : (k + 1) * rows], value_up[h])
            out[:, h * VDIM : (h + 1) * VDIM] = value.astype(BF16)
            stats = jnp.where(lane == h, level[k * rows : (k + 1) * rows], stats)
        return stats

    stats = jnp.zeros((rows, 128), F32)
    parts = score(0)
    for i in range(steps):
        following = score(i + 1) if i + 1 < steps else None
        stats = finish(i, parts, stats)
        parts = following
    high = stats.astype(BF16).astype(F32)
    rest = stats - high
    mid = rest.astype(BF16).astype(F32)
    joined = high + pltpu.roll(mid, n_head, axis=1) + pltpu.roll(rest - mid, 2 * n_head, axis=1)
    out[:, width:] = joined.astype(BF16)


def attend(by, n_section, place, query, key_up, value_up, near, far, span, keep_far):
    rows, n_head = query.shape[0], key_up.shape[0]
    n_keys = 2 * near.shape[0] + rows
    out_shape = [jax.ShapeDtypeStruct((rows, n_head * VDIM + 128), BF16)]
    if keep_far:
        out_shape.append(jax.ShapeDtypeStruct(far.shape, BF16))
    return pl.pallas_call(
        functools.partial(attend_kernel, by, n_section),
        out_shape=out_shape,
        in_specs=[SMEM] + [VMEM] * 6,
        out_specs=[VMEM] * len(out_shape),
        scratch_shapes=[pltpu.VMEM((n_head * rows, WIDE), BF16)],
        compiler_params=params(28),
        cost_estimate=pl.CostEstimate(
            flops=2 * rows * n_head * n_keys * (WIDE + KVR),
            bytes_accessed=2 * n_keys * WIDE,
            transcendentals=rows * n_head * n_keys,
        ),
        name="attend_%d" % by,
    )(place, query, key_up, value_up, near, far, span)


def output_kernel(n_head, own, one, two, three, weight, exact, send):
    parts = (own, one, two, three)
    width = n_head * VDIM
    levels = []
    for part in parts:
        stat = part[:, width:].astype(F32)
        rest = pltpu.roll(stat, 128 - n_head, axis=1) + pltpu.roll(stat, 128 - 2 * n_head, axis=1)
        levels.append(stat + rest)
    top = functools.reduce(jnp.maximum, levels)
    shares = [jnp.exp2(level - top) for level in levels]
    total = functools.reduce(jnp.add, shares)
    head_of = lax.broadcasted_iota(jnp.int32, (128, width), 0)
    lane_of = lax.broadcasted_iota(jnp.int32, (128, width), 1)
    begin = head_of * VDIM
    spread = jnp.where((lane_of >= begin) & (lane_of < begin + VDIM), 1.0, 0.0).astype(BF16)
    mixed = 0.0
    for part, share in zip(parts, shares):
        share = share / total
        high = share.astype(BF16)
        low = (share - high.astype(F32)).astype(BF16)
        factor = dot(high, spread) + dot(low, spread)
        mixed = mixed + part[:, :width].astype(F32) * factor
    per_head = mixed.astype(BF16)
    block = 512
    for at in range(0, weight.shape[1], block):
        part = dot(per_head, weight[:, at : at + block])
        exact[:, at : at + block] = part
        send[:, at : at + block] = part.astype(BF16)


def project_output(own, one, two, three, w_out):
    rows = own.shape[0]
    depth, cols = w_out.shape
    return pl.pallas_call(
        functools.partial(output_kernel, depth // VDIM),
        out_shape=[
            jax.ShapeDtypeStruct((rows, cols), F32),
            jax.ShapeDtypeStruct((rows, cols), BF16),
        ],
        in_specs=[VMEM] * 5,
        out_specs=[VMEM] * 2,
        compiler_params=params(16),
        name="project_output",
    )(own, one, two, three, w_out)


def expert_kernel(place, tokens, exact, other, gain, w_gate_t, w_up_t, w_down, keep, send):
    half = keep.shape[1]
    middle = tokens[...].astype(F32) + (exact[...] + other[...].astype(F32))
    middle = middle.astype(BF16).astype(F32)
    mlp_in = rms(middle, gain[...].astype(F32)).astype(BF16)
    gate = dot_nt(mlp_in, w_gate_t[...])
    up = dot_nt(mlp_in, w_up_t[...])
    hidden = (gate / (1.0 + jnp.exp(-gate)) * up).astype(BF16)
    low = dot(hidden, w_down[:, :half])
    high = dot(hidden, w_down[:, half:])
    first = place[3] == 0
    keep[...] = jnp.where(first, middle[:, :half] + low, middle[:, half:] + high)
    send[...] = jnp.where(first, high, low).astype(BF16)


def expert(place, tokens, exact, other, gain, w_gate_t, w_up_t, w_down):
    rows, width = tokens.shape
    half = width // 2
    return pl.pallas_call(
        expert_kernel,
        out_shape=[
            jax.ShapeDtypeStruct((rows, half), F32),
            jax.ShapeDtypeStruct((rows, half), BF16),
        ],
        in_specs=[SMEM] + [VMEM] * 7,
        out_specs=[VMEM] * 2,
        compiler_params=params(24),
        name="expert",
    )(place, tokens, exact, other, gain, w_gate_t, w_up_t, w_down)


def on_device(
    tokens,
    attn_gain,
    w_query,
    w_latent,
    kv_gain,
    w_key_up,
    w_value_up,
    w_out,
    mlp_gain,
    w_gate,
    w_up,
    w_down,
    page_pool,
    hit_owner,
    hit_slot,
    fetch_count,
):
    n_store = lax.axis_size("store")
    n_section = lax.axis_size("section")
    n_tp = lax.axis_size("tp")
    group = lax.axis_index("store")
    section = lax.axis_index("section")
    core = lax.axis_index("tp")
    rows = tokens.shape[0]
    share = PAGE // (n_section * n_tp)

    swap = [(0, 1), (1, 0)]
    place = jnp.stack([group, section * n_tp + core, section, core]).astype(jnp.int32)
    owner = hit_owner[:, :, 0]
    outgoing = pack_pages(place, owner, hit_slot, jnp.swapaxes(page_pool, 1, 2), share)
    outgoing, early_tokens = lax.optimization_barrier((outgoing, tokens))
    outgoing = outgoing.reshape(n_store, 2, share // 2, MSG)
    arrived = lax.all_to_all(outgoing, "store", split_axis=0, concat_axis=0, tiled=True)
    arrived = arrived.reshape(n_store, share, MSG)

    def shift(value, by):
        pairs = [((z + by) % n_section, z) for z in range(n_section)]
        return lax.ppermute(value, "section", pairs)

    table = rotation_table((hit_owner.shape[1]) * PAGE + n_section * rows)
    query, new_latent, span = project(
        place,
        fetch_count,
        early_tokens,
        attn_gain.reshape(1, -1),
        jnp.asarray(table),
        w_query,
        w_latent.T,
        kv_gain.reshape(1, -1),
    )
    next_query, last_query = shift(query, 1), shift(query, -1)
    arrived, next_query, last_query, span = lax.optimization_barrier(
        (arrived, next_query, last_query, span)
    )
    cut = rows // 2
    far_low, far_high = shift(next_query[:cut], 1), shift(last_query[cut:], -1)

    near = build_keys(place, owner, fetch_count, arrived)
    far = lax.ppermute(near, "tp", swap)

    def partial_for(by, query, far, keep_far=False):
        return attend(
            by, n_section, place, query, w_key_up, w_value_up, near, far, span, keep_far
        )

    one, far = partial_for(1, next_query, far, True)
    _, far_low, far_high = lax.optimization_barrier((one, far_low, far_high))
    one = shift(one, -1)
    (two,) = partial_for(2, jnp.concatenate([far_low, far_high], axis=0), far)
    _, last_query = lax.optimization_barrier((two, last_query))
    two = shift(two, -2)
    (three,) = partial_for(3, last_query, far)
    _, query = lax.optimization_barrier((three, query))
    three = shift(three, -3)
    (own,) = partial_for(0, query, far)
    exact, send = project_output(own, one, two, three, w_out)
    incoming = lax.ppermute(send, "tp", swap)
    keep, send = expert(
        place,
        tokens,
        exact,
        incoming,
        mlp_gain.reshape(1, -1),
        w_gate.T,
        w_up.T,
        w_down,
    )
    layer_out = (keep + lax.ppermute(send, "tp", swap).astype(F32)).astype(BF16)
    return (layer_out, new_latent.T)


def solution(mesh):
    in_specs = (
        P(("store", "section"), None),
        P(),
        P(None, "tp"),
        P(),
        P(),
        P("tp", None, None),
        P("tp", None, None),
        P("tp", None),
        P(),
        P(None, "tp"),
        P(None, "tp"),
        P("tp", None),
        P("store", None, None),
        P(),
        P(),
        P(),
    )
    out_specs = (P(("store", "section"), "tp"), P(("store", "section"), None))
    return jax.shard_map(
        on_device, mesh=mesh, in_specs=in_specs, out_specs=out_specs, check_vma=False
    )
```

time: 389 us -> 89.1 us (0.23)
  waiting for transfers between devices: 163 us -> 23.2 us
  matrix products: 97 us -> 0 us
  local copies, waits for them, and re-layouts: 48.1 us -> 1.3 us
  Pallas kernels: 0 us -> 44 us
  other arithmetic: 41.5 us -> 1.42 us
  blocking collectives: 14.5 us -> 0 us
  between operations: 15.1 us -> 0.86 us
  starting transfers between devices: 7.91 us -> 18.1 us
    all_to_all x1, waiting for transfers between devices: 118 us -> 0.01 us  [on_device(): lax.all_to_all(outgoing, 'store', split_axis=0, concat_axis=0, tiled=True)]
    dot_general x25 -> x0, matrix products: 97 us -> none  [the longest x9 42.7 us: attend(): jnp.dot(weight.astype(jnp.bfloat16), key_block[:, :KVR], preferred_elemen...]
    pallas_call x0 -> x9, Pallas kernels: none -> 44 us  [the longest x4 27.1 us: attend(): pl.pallas_call(functools.partial(attend_kernel, by, n_section), out_shape...]
    psum x1 -> x0, waiting for transfers between devices: 33 us -> none  [on_device(): lax.psum(partial_value.astype(jnp.bfloat16), 'tp').astype(jnp.float32)]
    reduce_sum x14 -> x0, other arithmetic: 32.9 us -> none  [the longest x9 29.4 us: attend(): new_total = row_total * fade_factor + jnp.sum(weight, axis=1)]
    ppermute x0 -> x10, waiting for transfers between devices: none -> 23.2 us  [the longest x7 20.1 us: shift(): return lax.ppermute(value, 'section', pairs)]
    unnamed x40 -> x30, local copies, waits for them, and re-layouts: 19.1 us -> 0.07 us
    all_gather x1 -> x0, blocking collectives: 14.5 us -> none  [on_device(): piece_block = lax.all_gather(new_latent, 'section', axis=0, tiled=True)]
  transfers between devices with their start and end apart: 3 -> 11, of which waited for: 3 -> 7; matrix products, arithmetic and copies ran while one was open for 7% -> 1% of each run, Pallas kernels for 0% -> 23%
where the time goes in v1:
time: 89.1 us; the launch traced here: 88.8 us
  Pallas kernels  44 us (49%)
  waiting for transfers between devices  23.2 us (26%)
  starting transfers between devices  18.1 us (20%)
  other arithmetic  1.42 us (2%)
  local copies, waits for them, and re-layouts  1.3 us (1%)
    pallas_call x4, Pallas kernels, attend(): pl.pallas_call(functools.partial(attend_kernel, by, n_section), out_shape...  27.1 us
    ppermute x7, waiting for transfers between devices, shift(): return lax.ppermute(value, 'section', pairs)  20.1 us
    all_to_all x1, starting transfers between devices, on_device(): lax.all_to_all(outgoing, 'store', split_axis=0, concat_axis=0, tiled=True)  7.6 us
    ppermute x7, starting transfers between devices, shift(): return lax.ppermute(value, 'section', pairs)  7.21 us
    pallas_call x1, Pallas kernels, project(): pl.pallas_call(project_kernel, out_shape=[jax.ShapeDtypeStruct((rows, col...  6.54 us
    pallas_call x1, Pallas kernels, pack_pages(): pl.pallas_call(pack_kernel, out_shape=jax.ShapeDtypeStruct((n_store, rows...  4.84 us
    pallas_call x1, Pallas kernels, expert(): pl.pallas_call(expert_kernel, out_shape=[jax.ShapeDtypeStruct((rows, half...  3.14 us
    ppermute x1, starting transfers between devices, on_device(): far = lax.ppermute(near, 'tp', swap)  2.24 us
  transfers between devices with their start and end apart: 11, of which 7 were waited for; matrix products, arithmetic and copies ran while one was open for 1% of the time, Pallas kernels for 23%

profile of v1, /device:TPU:1, one launch (start us, length us, event | category | flops | bytes accessed | tf_op | source)
XLA Modules:
  0.0 88.8 jit_solution(8156460742381224493)
XLA Ops:
  0.6 0.6 pad_add_fusion.place
  1.3 4.8 %pack_pages.1 = bf16[16,32,1152]{2,1,0:T(8,128)(2,1)} custom-call(s32[4]{0:T(128)} %pad_add_fusion.place, s32[16,24]{1,0:T(8,128)} %bitcast.15, s32[16,24]{1,0:T(8,128)} %slot_src.1, bf16[8,576,256]{2,1,0:T(8,128)(2,1)} %bitcast.18), custom_call_target="tpu_custom_call" | custom-call | tf_op jit(solution)/shard_map/pack_pages/pallas_call | solution.py:116
  6.1 7.6 %all-to-all-start = ((bf16[16,2,16,1152]{3,2,1,0:T(8,128)(2,1)}), bf16[16,2,16,1152]{3,2,1,0:T(8,128)(2,1)S(1)}, u32[]{:S(2)}, u32[]{:S(2)}) async-start(bf16[16,2,16,1152]{3,2,1,0:T(8,128)(2,1)} %bitcast.17), calls=%async_computation | async-start | bytes 2359296 | tf_op jit(solution)/shard_map/all_to_all | solution.py:457
  13.7 0.6 reshape.21.gain
  14.3 0.6 reshape.22.kv_gain
  14.9 6.5 %project.1 = (bf16[128,1536]{1,0:T(8,128)(2,1)}, bf16[576,128]{1,0:T(8,128)(2,1)}, bf16[128,640]{1,0:T(8,128)(2,1)}) custom-call(s32[4]{0:T(128)} %pad_add_fusion.place, s32[16]{0:T(128)} %count.3, bf16[128,2048]{1,0:T(8,128)(2,1)} %tokens.1, bf16[1,2048]{1,0:T(2,128)(2,1)} %reshape.21.gain, f32[6656,128]{1,0:T(8,128)} %constant.17.clone.table, ...), custom_call_target="tpu_custom_call" | custom-call | flops 1107296256 | bytes 8650752 | tf_op jit(solution)/shard_map/project/pallas_call | solution.py:230
  21.5 3.8 %collective-permute-start = (bf16[128,1536]{1,0:T(8,128)(2,1)}, bf16[128,1536]{1,0:T(8,128)(2,1)S(1)}, u32[]{:S(2)}, u32[]{:S(2)}) collective-permute-start(bf16[128,1536]{1,0:T(8,128)(2,1)} %get-tuple-element.34.query), channel_id=1, source_target_pairs={{2,0},{4,2},{6,4},{0,6},{3,1},{5,3},{7,5},{1,7},{10,8},{12,10},{14... | collective-permute-start | bytes 1179656 | tf_op jit(solution)/shard_map/ppermute | solution.py:462
  25.3 7.8 %collective-permute-done.query = bf16[128,1536]{1,0:T(8,128)(2,1)S(1)} collective-permute-done((bf16[128,1536]{1,0:T(8,128)(2,1)}, bf16[128,1536]{1,0:T(8,128)(2,1)S(1)}, u32[]{:S(2)}, u32[]{:S(2)}) %collective-permute-start) | collective-permute-done | bytes 393248 | tf_op jit(solution)/shard_map/ppermute | solution.py:462
  33.1 3.0 %collective-permute-done.1.query = bf16[128,1536]{1,0:T(8,128)(2,1)S(1)} collective-permute-done((bf16[128,1536]{1,0:T(8,128)(2,1)}, bf16[128,1536]{1,0:T(8,128)(2,1)S(1)}, u32[]{:S(2)}, u32[]{:S(2)}) %collective-permute-start.1) | collective-permute-done | bytes 393248 | tf_op jit(solution)/shard_map/ppermute | solution.py:462
  36.1 0.9 build_keys.1.near
  37.0 2.2 %collective-permute-start.2 = (bf16[768,640]{1,0:T(8,128)(2,1)S(1)}, bf16[768,640]{1,0:T(8,128)(2,1)S(1)}, u32[]{:S(2)}, u32[]{:S(2)}) collective-permute-start(bf16[768,640]{1,0:T(8,128)(2,1)S(1)} %build_keys.1.near), channel_id=1, source_target_pairs={{0,1},{1,0},{2,3},{3,2},{4,5},{5,4},{6,7},{7,6},{8,9},{9,8},{10,11... | collective-permute-start | bytes 2949128 | tf_op jit(solution)/shard_map/ppermute | solution.py:483
  39.4 1.7 %collective-permute-start.4 = (bf16[64,1536]{1,0:T(8,128)(2,1)S(1)}, bf16[64,1536]{1,0:T(8,128)(2,1)S(1)}, u32[]{:S(2)}, u32[]{:S(2)}) collective-permute-start(bf16[64,1536]{1,0:T(8,128)(2,1)S(1)} %slice.7), channel_id=1, source_target_pairs={{6,0},{0,2},{2,4},{4,6},{7,1},{1,3},{3,5},{5,7},{14,8},{8,10},{10,... | collective-permute-start | bytes 589832 | tf_op jit(solution)/shard_map/ppermute | solution.py:462
  41.5 6.7 %attend_1.1 = (bf16[128,1152]{1,0:T(8,128)(2,1)S(1)}, bf16[768,640]{1,0:T(8,128)(2,1)S(1)}) custom-call(s32[4]{0:T(128)S(1)} %copy-done.6, bf16[128,1536]{1,0:T(8,128)(2,1)S(1)} %collective-permute-done.query, bf16[8,512,128]{2,1,0:T(8,128)(2,1)S(1)} %copy-done.8, bf16[8,512,128]{2,1,0:T(8,128)(2,1)S(1)} %copy-done.9, bf16[768,640]{1,0:T(8,128)(2,1)S(1)} %build_keys.1.near, ...), custom_call_target="tpu_custom_call" | custom-call | flops 3925868544 | bytes 2129920 | tf_op jit(solution)/shard_map/attend_1/pallas_call | solution.py:331
  48.3 6.7 %attend_2.1 = bf16[128,1152]{1,0:T(8,128)(2,1)S(1)} custom-call(s32[4]{0:T(128)S(1)} %copy-done.6, bf16[128,1536]{1,0:T(8,128)(2,1)S(1)} %pad_maximum_fusion.query, bf16[8,512,128]{2,1,0:T(8,128)(2,1)S(1)} %copy-done.8, bf16[8,512,128]{2,1,0:T(8,128)(2,1)S(1)} %copy-done.9, bf16[768,640]{1,0:T(8,128)(2,1)S(1)} %build_keys.1.near, ...), custom_call_target="tpu_custom_call" | custom-call | flops 3925868544 | bytes 2129920 | tf_op jit(solution)/shard_map/attend_2/pallas_call | solution.py:331
  55.0 6.9 %attend_3.1 = bf16[128,1152]{1,0:T(8,128)(2,1)S(1)} custom-call(s32[4]{0:T(128)S(1)} %copy-done.6, bf16[128,1536]{1,0:T(8,128)(2,1)S(1)} %collective-permute-done.1.query, bf16[8,512,128]{2,1,0:T(8,128)(2,1)S(1)} %copy-done.8, bf16[8,512,128]{2,1,0:T(8,128)(2,1)S(1)} %copy-done.9, bf16[768,640]{1,0:T(8,128)(2,1)S(1)} %build_keys.1.near, ...), custom_call_target="tpu_custom_call" | custom-call | flops 3925868544 | bytes 2129920 | tf_op jit(solution)/shard_map/attend_3/pallas_call | solution.py:331
  61.9 0.9 %collective-permute-start.7 = (bf16[128,1152]{1,0:T(8,128)(2,1)S(1)}, bf16[128,1152]{1,0:T(8,128)(2,1)S(1)}, u32[]{:S(2)}, u32[]{:S(2)}) collective-permute-start(bf16[128,1152]{1,0:T(8,128)(2,1)S(1)} %attend_3.1), channel_id=1, source_target_pairs={{2,0},{4,2},{6,4},{0,6},{3,1},{5,3},{7,5},{1,7},{10,8},{12,10},{14... | collective-permute-start | bytes 884744 | tf_op jit(solution)/shard_map/ppermute | solution.py:462
  63.5 6.7 %attend_0.1.own = bf16[128,1152]{1,0:T(8,128)(2,1)S(1)} custom-call(s32[4]{0:T(128)S(1)} %copy-done.6, bf16[128,1536]{1,0:T(8,128)(2,1)S(1)} %copy-done.10, bf16[8,512,128]{2,1,0:T(8,128)(2,1)S(1)} %copy-done.8, bf16[8,512,128]{2,1,0:T(8,128)(2,1)S(1)} %copy-done.9, bf16[768,640]{1,0:T(8,128)(2,1)S(1)} %build_keys.1.near, ...), custom_call_target="tpu_custom_call" | custom-call | flops 3925868544 | bytes 2129920 | tf_op jit(solution)/shard_map/attend_0/pallas_call | solution.py:331
  70.3 1.8 %collective-permute-done.6.two = bf16[128,1152]{1,0:T(8,128)(2,1)S(1)} collective-permute-done((bf16[128,1152]{1,0:T(8,128)(2,1)S(1)}, bf16[128,1152]{1,0:T(8,128)(2,1)S(1)}, u32[]{:S(2)}, u32[]{:S(2)}) %collective-permute-start.6) | collective-permute-done | bytes 294944 | tf_op jit(solution)/shard_map/ppermute | solution.py:462
  72.1 7.5 %collective-permute-done.5.one = bf16[128,1152]{1,0:T(8,128)(2,1)S(1)} collective-permute-done((bf16[128,1152]{1,0:T(8,128)(2,1)S(1)}, bf16[128,1152]{1,0:T(8,128)(2,1)S(1)}, u32[]{:S(2)}, u32[]{:S(2)}) %collective-permute-start.5) | collective-permute-done | bytes 294944 | tf_op jit(solution)/shard_map/ppermute | solution.py:462
  79.6 1.5 %project_output.1 = (f32[128,2048]{1,0:T(8,128)S(1)}, bf16[128,2048]{1,0:T(8,128)(2,1)S(1)}) custom-call(bf16[128,1152]{1,0:T(8,128)(2,1)S(1)} %attend_0.1.own, bf16[128,1152]{1,0:T(8,128)(2,1)S(1)} %collective-permute-done.5.one, bf16[128,1152]{1,0:T(8,128)(2,1)S(1)} %collective-permute-done.6.two, bf16[128,1152]{1,0:T(8,128)(2,1)S(1)} %collective-permute-done.7.three, ...), custom_call_target="tpu_custom_call" | custom-call | tf_op jit(solution)/shard_map/project_output/pallas_call | solution.py:380
  81.8 1.5 %collective-permute-done.8.other = bf16[128,2048]{1,0:T(8,128)(2,1)S(1)} collective-permute-done((bf16[128,2048]{1,0:T(8,128)(2,1)S(1)}, bf16[128,2048]{1,0:T(8,128)(2,1)S(1)}, u32[]{:S(2)}, u32[]{:S(2)}) %collective-permute-start.8) | collective-permute-done | bytes 524320 | tf_op jit(solution)/shard_map/ppermute | solution.py:501
  83.3 3.1 %expert.1 = (f32[128,1024]{1,0:T(8,128)S(1)}, bf16[128,1024]{1,0:T(8,128)(2,1)S(1)}) custom-call(s32[4]{0:T(128)S(1)} %copy-done.6, bf16[128,2048]{1,0:T(8,128)(2,1)S(1)} %copy-done.4, f32[128,2048]{1,0:T(8,128)S(1)} %get-tuple-element.35.exact, bf16[128,2048]{1,0:T(8,128)(2,1)S(1)} %collective-permute-done.8.other, bf16[1,2048]{1,0:T(2,128)(2,1)S(1)} %reshape.23.gain, ...), custom_call_target="tpu_custom_call" | custom-call | tf_op jit(solution)/shard_map/expert/pallas_call | solution.py:411
  86.9 1.2 %collective-permute-done.9 = bf16[128,1024]{1,0:T(8,128)(2,1)S(1)} collective-permute-done((bf16[128,1024]{1,0:T(8,128)(2,1)S(1)}, bf16[128,1024]{1,0:T(8,128)(2,1)S(1)}, u32[]{:S(2)}, u32[]{:S(2)}) %collective-permute-start.9) | collective-permute-done | bytes 262176 | tf_op jit(solution)/shard_map/ppermute | solution.py:512
  88.1 0.8 add_convert_fusion
  (45 shorter events, 2.3 us)
Async XLA Ops:
  1.3 12.5 %copy-start.12 = (bf16[2048]{0:T(1024)(128)(2,1)S(1)}, bf16[2048]{0:T(1024)(128)(2,1)}, u32[]{:S(2)}) copy-start(bf16[2048]{0:T(1024)(128)(2,1)} %param.18) | copy-start | bytes 12292
  1.3 13.1 %copy-start.14 = (bf16[512]{0:T(512)(128)(2,1)S(1)}, bf16[512]{0:T(512)(128)(2,1)}, u32[]{:S(2)}) copy-start(bf16[512]{0:T(512)(128)(2,1)} %param.21) | copy-start | bytes 3076
  6.1 30.0 %all-to-all-start = ((bf16[16,2,16,1152]{3,2,1,0:T(8,128)(2,1)}), bf16[16,2,16,1152]{3,2,1,0:T(8,128)(2,1)S(1)}, u32[]{:S(2)}, u32[]{:S(2)}) async-start(bf16[16,2,16,1152]{3,2,1,0:T(8,128)(2,1)} %bitcast.17), calls=%async_computation | async-start | bytes 2359296 | tf_op jit(solution)/shard_map/all_to_all | solution.py:457
  14.9 21.2 %copy-start.5 = (s32[16,24,1]{1,2,0:T(1,128)S(1)}, s32[16,24,1]{1,2,0:T(1,128)}, u32[]{:S(2)}) copy-start(s32[16,24,1]{1,2,0:T(1,128)} %param.30) | copy-start | bytes 4612
  14.9 21.2 %copy-start.6 = (s32[4]{0:T(128)S(1)}, s32[4]{0:T(128)}, u32[]{:S(2)}) copy-start(s32[4]{0:T(128)} %pad_add_fusion.place) | copy-start | bytes 52
  14.9 21.2 %copy-start.7 = (s32[16]{0:T(128)S(1)}, s32[16]{0:T(128)}, u32[]{:S(2)}) copy-start(s32[16]{0:T(128)} %count.3) | copy-start | bytes 196
  21.5 20.0 %copy-start.8 = (bf16[8,512,128]{2,1,0:T(8,128)(2,1)S(1)}, bf16[8,512,128]{2,1,0:T(8,128)(2,1)}, u32[]{:S(2)}) copy-start(bf16[8,512,128]{2,1,0:T(8,128)(2,1)} %key_up.7) | copy-start | bytes 3145732
  21.5 20.0 %copy-start.11 = (bf16[128,640]{1,0:T(8,128)(2,1)S(1)}, bf16[128,640]{1,0:T(8,128)(2,1)}, u32[]{:S(2)}) copy-start(bf16[128,640]{1,0:T(8,128)(2,1)} %get-tuple-element.27.refs_1_) | copy-start | bytes 491524
  21.5 11.6 %collective-permute-start = (bf16[128,1536]{1,0:T(8,128)(2,1)}, bf16[128,1536]{1,0:T(8,128)(2,1)S(1)}, u32[]{:S(2)}, u32[]{:S(2)}) collective-permute-start(bf16[128,1536]{1,0:T(8,128)(2,1)} %get-tuple-element.34.query), channel_id=1, source_target_pairs={{2,0},{4,2},{6,4},{0,6},{3,1},{5,3},{7,5},{1,7},{10,8},{12,10},{14... | collective-permute-start | bytes 1179656 | tf_op jit(solution)/shard_map/ppermute | solution.py:462
  25.3 10.8 %collective-permute-start.1 = (bf16[128,1536]{1,0:T(8,128)(2,1)}, bf16[128,1536]{1,0:T(8,128)(2,1)S(1)}, u32[]{:S(2)}, u32[]{:S(2)}) collective-permute-start(bf16[128,1536]{1,0:T(8,128)(2,1)} %get-tuple-element.34.query), channel_id=1, source_target_pairs={{6,0},{0,2},{2,4},{4,6},{7,1},{1,3},{3,5},{5,7},{14,8},{8,10},{10,... | collective-permute-start | bytes 1179656 | tf_op jit(solution)/shard_map/ppermute | solution.py:462
  37.0 4.4 %collective-permute-start.2 = (bf16[768,640]{1,0:T(8,128)(2,1)S(1)}, bf16[768,640]{1,0:T(8,128)(2,1)S(1)}, u32[]{:S(2)}, u32[]{:S(2)}) collective-permute-start(bf16[768,640]{1,0:T(8,128)(2,1)S(1)} %build_keys.1.near), channel_id=1, source_target_pairs={{0,1},{1,0},{2,3},{3,2},{4,5},{5,4},{6,7},{7,6},{8,9},{9,8},{10,11... | collective-permute-start | bytes 2949128 | tf_op jit(solution)/shard_map/ppermute | solution.py:483
  39.3 8.9 %collective-permute-start.3 = (bf16[64,1536]{1,0:T(8,128)(2,1)S(1)}, bf16[64,1536]{1,0:T(8,128)(2,1)S(1)}, u32[]{:S(2)}, u32[]{:S(2)}) collective-permute-start(bf16[64,1536]{1,0:T(8,128)(2,1)S(1)} %slice.6), channel_id=1, source_target_pairs={{2,0},{4,2},{6,4},{0,6},{3,1},{5,3},{7,5},{1,7},{10,8},{12,10},{14... | collective-permute-start | bytes 589832 | tf_op jit(solution)/shard_map/ppermute | solution.py:462
  39.4 8.8 %collective-permute-start.4 = (bf16[64,1536]{1,0:T(8,128)(2,1)S(1)}, bf16[64,1536]{1,0:T(8,128)(2,1)S(1)}, u32[]{:S(2)}, u32[]{:S(2)}) collective-permute-start(bf16[64,1536]{1,0:T(8,128)(2,1)S(1)} %slice.7), channel_id=1, source_target_pairs={{6,0},{0,2},{2,4},{4,6},{7,1},{1,3},{3,5},{5,7},{14,8},{8,10},{10,... | collective-permute-start | bytes 589832 | tf_op jit(solution)/shard_map/ppermute | solution.py:462
  61.9 8.4 %collective-permute-start.7 = (bf16[128,1152]{1,0:T(8,128)(2,1)S(1)}, bf16[128,1152]{1,0:T(8,128)(2,1)S(1)}, u32[]{:S(2)}, u32[]{:S(2)}) collective-permute-start(bf16[128,1152]{1,0:T(8,128)(2,1)S(1)} %attend_3.1), channel_id=1, source_target_pairs={{2,0},{4,2},{6,4},{0,6},{3,1},{5,3},{7,5},{1,7},{10,8},{12,10},{14... | collective-permute-start | bytes 884744 | tf_op jit(solution)/shard_map/ppermute | solution.py:462
  62.9 9.2 %collective-permute-start.6 = (bf16[128,1152]{1,0:T(8,128)(2,1)S(1)}, bf16[128,1152]{1,0:T(8,128)(2,1)S(1)}, u32[]{:S(2)}, u32[]{:S(2)}) collective-permute-start(bf16[128,1152]{1,0:T(8,128)(2,1)S(1)} %attend_2.1), channel_id=1, source_target_pairs={{4,0},{6,2},{0,4},{2,6},{5,1},{7,3},{1,5},{3,7},{12,8},{14,10},{8,... | collective-permute-start | bytes 884744 | tf_op jit(solution)/shard_map/ppermute | solution.py:462
  63.4 16.2 %collective-permute-start.5 = (bf16[128,1152]{1,0:T(8,128)(2,1)S(1)}, bf16[128,1152]{1,0:T(8,128)(2,1)S(1)}, u32[]{:S(2)}, u32[]{:S(2)}) collective-permute-start(bf16[128,1152]{1,0:T(8,128)(2,1)S(1)} %get-tuple-element.28), channel_id=1, source_target_pairs={{6,0},{0,2},{2,4},{4,6},{7,1},{1,3},{3,5},{5,7},{14,8},{8,10},{10,... | collective-permute-start | bytes 884744 | tf_op jit(solution)/shard_map/ppermute | solution.py:462
  63.5 16.1 %copy-start = (bf16[1024,2048]{1,0:T(8,128)(2,1)S(1)}, bf16[1024,2048]{1,0:T(8,128)(2,1)}, u32[]{:S(2)}) copy-start(bf16[1024,2048]{1,0:T(8,128)(2,1)} %weight.1) | copy-start | bytes 12582916
  63.5 19.7 %copy-start.2 = (bf16[2048,704]{0,1:T(8,128)(2,1)S(1)}, bf16[2048,704]{0,1:T(8,128)(2,1)}, u32[]{:S(2)}) copy-start(bf16[2048,704]{0,1:T(8,128)(2,1)} %param.27) | copy-start | bytes 8650756
  63.5 19.7 %copy-start.3 = (bf16[704,2048]{1,0:T(8,128)(2,1)S(1)}, bf16[704,2048]{1,0:T(8,128)(2,1)}, u32[]{:S(2)}) copy-start(bf16[704,2048]{1,0:T(8,128)(2,1)} %w_down.1) | copy-start | bytes 8650756
  70.3 11.5 %copy-start.13 = (bf16[2048]{0:T(1024)(128)(2,1)S(1)}, bf16[2048]{0:T(1024)(128)(2,1)}, u32[]{:S(2)}) copy-start(bf16[2048]{0:T(1024)(128)(2,1)} %param.25) | copy-start | bytes 12292
  70.3 13.0 %copy-start.1 = (bf16[2048,704]{0,1:T(8,128)(2,1)S(1)}, bf16[2048,704]{0,1:T(8,128)(2,1)}, u32[]{:S(2)}) copy-start(bf16[2048,704]{0,1:T(8,128)(2,1)} %param.26) | copy-start | bytes 8650756
  70.3 13.0 %copy-start.4 = (bf16[128,2048]{1,0:T(8,128)(2,1)S(1)}, bf16[128,2048]{1,0:T(8,128)(2,1)}, u32[]{:S(2)}) copy-start(bf16[128,2048]{1,0:T(8,128)(2,1)} %tokens.1) | copy-start | bytes 1572868
  81.2 2.1 %collective-permute-start.8 = (bf16[128,2048]{1,0:T(8,128)(2,1)S(1)}, bf16[128,2048]{1,0:T(8,128)(2,1)S(1)}, u32[]{:S(2)}, u32[]{:S(2)}) collective-permute-start(bf16[128,2048]{1,0:T(8,128)(2,1)S(1)} %get-tuple-element.36), channel_id=1, source_target_pairs={{0,1},{1,0},{2,3},{3,2},{4,5},{5,4},{6,7},{7,6},{8,9},{9,8},{10,11... | collective-permute-start | bytes 1572872 | tf_op jit(solution)/shard_map/ppermute | solution.py:501
  86.4 1.6 %collective-permute-start.9 = (bf16[128,1024]{1,0:T(8,128)(2,1)S(1)}, bf16[128,1024]{1,0:T(8,128)(2,1)S(1)}, u32[]{:S(2)}, u32[]{:S(2)}) collective-permute-start(bf16[128,1024]{1,0:T(8,128)(2,1)S(1)} %get-tuple-element.38), channel_id=1, source_target_pairs={{0,1},{1,0},{2,3},{3,2},{4,5},{5,4},{6,7},{7,6},{8,9},{9,8},{10,11... | collective-permute-start | bytes 786440 | tf_op jit(solution)/shard_map/ppermute | solution.py:512
  (2 other events, 13.9 us)

commit v2 on v1

--- a/solution.py
+++ b/solution.py
@@ -59,15 +59,15 @@
 def pack_kernel(
     place, owner_src, slot_src, pool_src, out, owner, slot, pool, sems
 ):
-    n_pages, width, page = pool.shape
+    n_pages, width, window = pool.shape
     n_store, rows, _ = out.shape
-    window = 128
     per = window // rows
     pairs = [(owner_src, owner), (slot_src, slot)]
+    part = pl.ds(pl.multiple_of((place[1] // per) * window, window), window)
     strip = n_pages // 4
     for k in range(4):
         at = pl.ds(k * strip, strip)
-        pairs.append((pool_src.at[at], pool.at[at]))
+        pairs.append((pool_src.at[at, :, part], pool.at[at]))
     copies = [
         pltpu.make_async_copy(src, dst, sems.at[i]) for i, (src, dst) in enumerate(pairs)
     ]
@@ -75,16 +75,13 @@
         copy.start()
     for copy in copies:
         copy.wait()
-    upper = place[1] >= per
     first = (place[1] % per) * rows
     lane = lax.broadcasted_iota(jnp.int32, (width, window), 1)
     joined = []
     for at in range(0, n_pages, per):
         part = None
         for k in range(per):
-            both = pool[at + k]
-            moved = jnp.where(upper, both[:, window:], both[:, :window]).astype(F32)
-            moved = pltpu.roll(moved, (k * rows - first + window) % window, axis=1)
+            moved = pltpu.roll(pool[at + k].astype(F32), (k * rows - first + window) % window, axis=1)
             part = moved if part is None else jnp.where(lane >= k * rows, moved, part)
         joined.append(part.astype(BF16))
     stage = jnp.concatenate(joined, axis=1)
@@ -121,7 +118,7 @@
         scratch_shapes=[
             pltpu.VMEM(owner.shape, jnp.int32),
             pltpu.VMEM(slot.shape, jnp.int32),
-            pltpu.VMEM(pool_t.shape, BF16),
+            pltpu.VMEM((*pool_t.shape[:2], 128), BF16),
             pltpu.SemaphoreType.DMA((6,)),
         ],
         compiler_params=params(60),
@@ -172,8 +169,7 @@
 
 
 def project_kernel(
-    place, count, tokens_src, gain, table, w_query_src, w_latent_src, kv_gain, query, new_latent, span,
-    tokens, turns, w_query, w_latent_t, total, sems
+    place, count, tokens_src, gain, table, w_query_src, query, normed, turns, tokens, w_query, total, sems
 ):
     rows = tokens.shape[0]
     start = pl.multiple_of(count[place[0]] * PAGE + place[2] * rows, rows)
@@ -183,17 +179,13 @@
     for k in range(pieces):
         at = pl.ds(k * depth, depth)
         pairs.append((w_query_src.at[at, :], w_query.at[at, :]))
-    strip = w_latent_t.shape[0] // 4
-    for k in range(4):
-        at = pl.ds(k * strip, strip)
-        pairs.append((w_latent_src.at[at, :], w_latent_t.at[at, :]))
     copies = [
         pltpu.make_async_copy(src, dst, sems.at[i]) for i, (src, dst) in enumerate(pairs)
     ]
     for copy in copies:
         copy.start()
     copies[0].wait()
-    normed = rms(tokens[...].astype(F32), gain[...].astype(F32)).astype(BF16)
+    normed[...] = rms(tokens[...].astype(F32), gain[...].astype(F32).reshape(1, -1)).astype(BF16)
     copies[1].wait()
     cosine, sine = turns[:, :ROPE], turns[:, ROPE:]
     cosine = jnp.concatenate([cosine, cosine], axis=1)
@@ -211,10 +203,37 @@
         query[:, at + NOPE : at + 2 * NOPE] = part[:, head : head + NOPE].astype(BF16)
         pair = jnp.concatenate([part[:, NOPE:head], part[:, head + NOPE :]], axis=1)
         query[:, at + 2 * NOPE : at + 2 * head] = (turn(pair, cosine, sine) * SCALE).astype(BF16)
-    for copy in copies[2 + pieces :]:
-        copy.wait()
-    raw = dot_nt(normed, w_latent_t[...])
-    latent = rms(raw[:, :KVR], kv_gain[...].astype(F32)).astype(BF16)
+
+
+def project(place, count, tokens, gain, table, w_query):
+    rows, width = tokens.shape
+    cols = w_query.shape[1]
+    return pl.pallas_call(
+        project_kernel,
+        out_shape=[
+            jax.ShapeDtypeStruct((rows, cols), BF16),
+            jax.ShapeDtypeStruct(tokens.shape, BF16),
+            jax.ShapeDtypeStruct((rows, 2 * ROPE), F32),
+        ],
+        in_specs=[SMEM] * 2 + [HBM, VMEM] + [HBM] * 2,
+        out_specs=[VMEM] * 3,
+        scratch_shapes=[
+            pltpu.VMEM(tokens.shape, BF16),
+            pltpu.VMEM(w_query.shape, BF16),
+            pltpu.VMEM((rows, cols), F32),
+            pltpu.SemaphoreType.DMA((10,)),
+        ],
+        compiler_params=params(60),
+        name="project",
+    )(place, count, tokens, gain, table, w_query)
+
+
+def latent_kernel(normed, turns, w_latent_t, kv_gain, new_latent, span):
+    cosine, sine = turns[:, :ROPE], turns[:, ROPE:]
+    cosine = jnp.concatenate([cosine, cosine], axis=1)
+    sine = jnp.concatenate([sine, sine], axis=1)
+    raw = dot_nt(normed[...], w_latent_t[...])
+    latent = rms(raw[:, :KVR], kv_gain[...].astype(F32).reshape(1, -1)).astype(BF16)
     pair = jnp.concatenate([raw[:, KVR:], raw[:, KVR:]], axis=1)
     turned = turn(pair, cosine, sine)
     new_latent[:KVR, :] = latent.astype(F32).T.astype(BF16)
@@ -224,44 +243,31 @@
     span[:, KVR:] = jnp.where(lane < ROPE, turned, 0.0).astype(BF16)
 
 
-def project(place, count, tokens, gain, table, w_query, w_latent_t, kv_gain):
-    rows, width = tokens.shape
-    cols = w_query.shape[1]
-    return pl.pallas_call(
-        project_kernel,
+def project_latent(normed, turns, w_latent_t, kv_gain):
+    rows = normed.shape[0]
+    return pl.pallas_call(
+        latent_kernel,
         out_shape=[
-            jax.ShapeDtypeStruct((rows, cols), BF16),
             jax.ShapeDtypeStruct((LAT, rows), BF16),
             jax.ShapeDtypeStruct((rows, WIDE), BF16),
         ],
-        in_specs=[SMEM] * 2 + [HBM, VMEM] + [HBM] * 3 + [VMEM],
-        out_specs=[VMEM] * 3,
-        scratch_shapes=[
-            pltpu.VMEM(tokens.shape, BF16),
-            pltpu.VMEM((rows, 2 * ROPE), F32),
-            pltpu.VMEM(w_query.shape, BF16),
-            pltpu.VMEM(w_latent_t.shape, BF16),
-            pltpu.VMEM((rows, cols), F32),
-            pltpu.SemaphoreType.DMA((14,)),
-        ],
-        compiler_params=params(60),
-        cost_estimate=pl.CostEstimate(
-            flops=2 * rows * width * (cols + LAT),
-            bytes_accessed=2 * width * (cols + LAT),
-            transcendentals=0,
-        ),
-        name="project",
-    )(place, count, tokens, gain, table, w_query, w_latent_t, kv_gain)
+        in_specs=[VMEM] * 4,
+        out_specs=[VMEM] * 2,
+        compiler_params=params(16),
+        name="project_latent",
+    )(normed, turns, w_latent_t, kv_gain)
 
 
 def attend_kernel(by, n_section, place, query, key_up, value_up, near, *refs):
     n_head, rows = key_up.shape[0], query.shape[0]
     if len(refs) == 5:
-        arrived, span, out, far, probes = refs
-        far[...] = arrived[...]
+        far, span, out, keys, probes = refs
+        keys[: near.shape[0], :] = near[...]
+        keys[near.shape[0] :, :] = far[...]
     else:
-        far, span, out, probes = refs
-    blocks = (near, far, span)
+        keys = near
+        span, out, probes = refs
+    blocks = (keys, span)
     lane = lax.broadcasted_iota(jnp.int32, (rows, 128), 1)
     head_pair = 2 * (NOPE + ROPE)
     at_once = 2
@@ -289,7 +295,7 @@
     def score(i):
         probe = probes[i * tile : (i + 1) * tile, :]
         parts = [dot_nt(probe, block[...]) for block in blocks]
-        parts[2] = parts[2] + hide
+        parts[1] = parts[1] + hide
         return parts
 
     def finish(i, parts, stats):
@@ -322,26 +328,20 @@
     out[:, width:] = joined.astype(BF16)
 
 
-def attend(by, n_section, place, query, key_up, value_up, near, far, span, keep_far):
+def attend(by, n_section, place, query, key_up, value_up, *keys):
     rows, n_head = query.shape[0], key_up.shape[0]
-    n_keys = 2 * near.shape[0] + rows
     out_shape = [jax.ShapeDtypeStruct((rows, n_head * VDIM + 128), BF16)]
-    if keep_far:
-        out_shape.append(jax.ShapeDtypeStruct(far.shape, BF16))
+    if len(keys) == 3:
+        out_shape.append(jax.ShapeDtypeStruct((2 * keys[0].shape[0], WIDE), BF16))
     return pl.pallas_call(
         functools.partial(attend_kernel, by, n_section),
         out_shape=out_shape,
-        in_specs=[SMEM] + [VMEM] * 6,
+        in_specs=[SMEM] + [VMEM] * (3 + len(keys)),
         out_specs=[VMEM] * len(out_shape),
         scratch_shapes=[pltpu.VMEM((n_head * rows, WIDE), BF16)],
         compiler_params=params(28),
-        cost_estimate=pl.CostEstimate(
-            flops=2 * rows * n_head * n_keys * (WIDE + KVR),
-            bytes_accessed=2 * n_keys * WIDE,
-            transcendentals=rows * n_head * n_keys,
-        ),
         name="attend_%d" % by,
-    )(place, query, key_up, value_up, near, far, span)
+    )(place, query, key_up, value_up, *keys)
 
 
 def output_kernel(n_head, own, one, two, three, weight, exact, send):
@@ -394,7 +394,7 @@
     half = keep.shape[1]
     middle = tokens[...].astype(F32) + (exact[...] + other[...].astype(F32))
     middle = middle.astype(BF16).astype(F32)
-    mlp_in = rms(middle, gain[...].astype(F32)).astype(BF16)
+    mlp_in = rms(middle, gain[...].astype(F32).reshape(1, -1)).astype(BF16)
     gate = dot_nt(mlp_in, w_gate_t[...])
     up = dot_nt(mlp_in, w_up_t[...])
     hidden = (gate / (1.0 + jnp.exp(-gate)) * up).astype(BF16)
@@ -462,17 +462,11 @@
         return lax.ppermute(value, "section", pairs)
 
     table = rotation_table((hit_owner.shape[1]) * PAGE + n_section * rows)
-    query, new_latent, span = project(
-        place,
-        fetch_count,
-        early_tokens,
-        attn_gain.reshape(1, -1),
-        jnp.asarray(table),
-        w_query,
-        w_latent.T,
-        kv_gain.reshape(1, -1),
+    query, normed, turns = project(
+        place, fetch_count, early_tokens, attn_gain, jnp.asarray(table), w_query
     )
     next_query, last_query = shift(query, 1), shift(query, -1)
+    new_latent, span = project_latent(normed, turns, w_latent.T, kv_gain)
     arrived, next_query, last_query, span = lax.optimization_barrier(
         (arrived, next_query, last_query, span)
     )
@@ -482,21 +476,20 @@
     near = build_keys(place, owner, fetch_count, arrived)
     far = lax.ppermute(near, "tp", swap)
 
-    def partial_for(by, query, far, keep_far=False):
-        return attend(
-            by, n_section, place, query, w_key_up, w_value_up, near, far, span, keep_far
-        )
-
-    one, far = partial_for(1, next_query, far, True)
-    _, far_low, far_high = lax.optimization_barrier((one, far_low, far_high))
+    def partial_for(by, query, *keys):
+        return attend(by, n_section, place, query, w_key_up, w_value_up, *keys, span)
+
+    one, keys = partial_for(1, next_query, near, far)
+    one, far_low, far_high = lax.optimization_barrier((one, far_low, far_high))
     one = shift(one, -1)
-    (two,) = partial_for(2, jnp.concatenate([far_low, far_high], axis=0), far)
-    _, last_query = lax.optimization_barrier((two, last_query))
-    two = shift(two, -2)
-    (three,) = partial_for(3, last_query, far)
-    _, query = lax.optimization_barrier((three, query))
+    (two,) = partial_for(2, jnp.concatenate([far_low, far_high], axis=0), keys)
+    two, last_query, one = lax.optimization_barrier((two, last_query, one))
+    two = shift(two, -1)
+    (three,) = partial_for(3, last_query, keys)
+    three, query, two = lax.optimization_barrier((three, query, two))
     three = shift(three, -3)
-    (own,) = partial_for(0, query, far)
+    two = shift(two, -1)
+    (own,) = partial_for(0, query, keys)
     exact, send = project_output(own, one, two, three, w_out)
     incoming = lax.ppermute(send, "tp", swap)
     keep, send = expert(
@@ -504,7 +497,7 @@
         tokens,
         exact,
         incoming,
-        mlp_gain.reshape(1, -1),
+        mlp_gain,
         w_gate.T,
         w_up.T,
         w_down,

time: 89.1 us -> 87.7 us (0.984)
  waiting for transfers between devices: 23.2 us -> 8.86 us
  local copies, waits for them, and re-layouts: 1.3 us -> 6.24 us
  starting transfers between devices: 18.1 us -> 22.3 us
  Pallas kernels: 44 us -> 47.5 us
    ppermute x7 -> x8, waiting for transfers between devices: 20.1 us -> 6.15 us  [shift(): return lax.ppermute(value, 'section', pairs)]
    unnamed x30 -> x36, local copies, waits for them, and re-layouts: 0.07 us -> 4.36 us
    pallas_call x4, Pallas kernels: 27.1 us -> 30.6 us  [attend(): pl.pallas_call(functools.partial(attend_kernel, by, n_section), out_shape...]
    ppermute x1, starting transfers between devices: 0.57 us -> 2.77 us  [on_device(): incoming = lax.ppermute(send, 'tp', swap)]
    ppermute x7 -> x8, starting transfers between devices: 7.21 us -> 9.23 us  [shift(): return lax.ppermute(value, 'section', pairs)]
    pallas_call x0 -> x1, Pallas kernels: none -> 1.95 us  [project_latent(): pl.pallas_call(latent_kernel, out_shape=[jax.ShapeDtypeStruct((LAT, rows)...]
    pallas_call x1, Pallas kernels: 6.54 us -> 5.11 us  [project(): pl.pallas_call(project_kernel, out_shape=[jax.ShapeDtypeStruct((rows, col...]
    reshape x3 -> x0, local copies, waits for them, and re-layouts: 1.2 us -> none  [the longest x1 0.6 us: on_device(): attn_gain.reshape(1, -1)]
  transfers between devices with their start and end apart: 11 -> 12, of which waited for: 7 -> 5; matrix products, arithmetic and copies ran while one was open for 1% -> 2% of each run, Pallas kernels for 23% -> 43%
where the time goes in v2:
time: 87.7 us; the launch traced here: 87.2 us
  Pallas kernels  47.5 us (54%)
  starting transfers between devices  22.3 us (25%)
  waiting for transfers between devices  8.86 us (10%)
  local copies, waits for them, and re-layouts  6.24 us (7%)
  other arithmetic  1.38 us (2%)
  between operations  0.93 us (1%)
    pallas_call x4, Pallas kernels, attend(): pl.pallas_call(functools.partial(attend_kernel, by, n_section), out_shape...  30.6 us
    ppermute x8, starting transfers between devices, shift(): return lax.ppermute(value, 'section', pairs)  9.23 us
    all_to_all x1, starting transfers between devices, on_device(): lax.all_to_all(outgoing, 'store', split_axis=0, concat_axis=0, tiled=True)  7.6 us
    ppermute x8, waiting for transfers between devices, shift(): return lax.ppermute(value, 'section', pairs)  6.15 us
    pallas_call x1, Pallas kernels, project(): pl.pallas_call(project_kernel, out_shape=[jax.ShapeDtypeStruct((rows, col...  5.11 us
    unnamed x36, local copies, waits for them, and re-layouts  4.36 us
    pallas_call x1, Pallas kernels, pack_pages(): pl.pallas_call(pack_kernel, out_shape=jax.ShapeDtypeStruct((n_store, rows...  4.34 us
    pallas_call x1, Pallas kernels, expert(): pl.pallas_call(expert_kernel, out_shape=[jax.ShapeDtypeStruct((rows, half...  3.16 us
  transfers between devices with their start and end apart: 12, of which 5 were waited for; matrix products, arithmetic and copies ran while one was open for 2% of the time, Pallas kernels for 43%

profile of v2, /device:TPU:1, one launch (start us, length us, event | category | flops | bytes accessed | tf_op | source)
XLA Modules:
  0.0 87.2 jit_solution(12051768678468786017)
XLA Ops:
  1.2 4.3 %pack_pages.1 = bf16[16,32,1152]{2,1,0:T(8,128)(2,1)} custom-call(s32[4]{0:T(128)} %pad_add_fusion.place, s32[16,24]{1,0:T(8,128)} %bitcast.16, s32[16,24]{1,0:T(8,128)} %slot_src.1, bf16[8,576,256]{2,1,0:T(8,128)(2,1)} %bitcast.19), custom_call_target="tpu_custom_call" | custom-call | tf_op jit(solution)/shard_map/pack_pages/pallas_call | solution.py:113
  5.6 7.6 %all-to-all-start = ((bf16[16,2,16,1152]{3,2,1,0:T(8,128)(2,1)}), bf16[16,2,16,1152]{3,2,1,0:T(8,128)(2,1)S(1)}, u32[]{:S(2)}, u32[]{:S(2)}) async-start(bf16[16,2,16,1152]{3,2,1,0:T(8,128)(2,1)} %bitcast.18), calls=%async_computation | async-start | bytes 2359296 | tf_op jit(solution)/shard_map/all_to_all | solution.py:457
  13.2 5.1 %project.1 = (bf16[128,1536]{1,0:T(8,128)(2,1)}, bf16[128,2048]{1,0:T(8,128)(2,1)}, f32[128,128]{1,0:T(8,128)}) custom-call(s32[4]{0:T(128)} %pad_add_fusion.place, s32[16]{0:T(128)} %count.3, bf16[128,2048]{1,0:T(8,128)(2,1)} %tokens.1, bf16[2048]{0:T(1024)(128)(2,1)} %gain.2, f32[6656,128]{1,0:T(8,128)} %constant.17.clone.table, bf16[2048,1536]{1,0:T(8,128)(2,1)} %w_query_src.1), custom_call_target="tpu_custom_call" | custom-call | tf_op jit(solution)/shard_map/project/pallas_call | solution.py:211
  18.3 3.8 %collective-permute-start = (bf16[128,1536]{1,0:T(8,128)(2,1)}, bf16[128,1536]{1,0:T(8,128)(2,1)S(1)}, u32[]{:S(2)}, u32[]{:S(2)}) collective-permute-start(bf16[128,1536]{1,0:T(8,128)(2,1)} %get-tuple-element.45.query), channel_id=1, source_target_pairs={{2,0},{4,2},{6,4},{0,6},{3,1},{5,3},{7,5},{1,7},{10,8},{12,10},{14... | collective-permute-start | bytes 1179656 | tf_op jit(solution)/shard_map/ppermute | solution.py:462
  22.2 1.7 %copy-done.6 = bf16[2048,576]{0,1:T(8,128)(2,1)S(1)} copy-done((bf16[2048,576]{0,1:T(8,128)(2,1)S(1)}, bf16[2048,576]{0,1:T(8,128)(2,1)}, u32[]{:S(2)}) %copy-start.6) | copy-done | bytes 2359320
  23.8 1.0 %copy-done.10 = bf16[128,2048]{1,0:T(8,128)(2,1)S(1)} copy-done((bf16[128,2048]{1,0:T(8,128)(2,1)S(1)}, bf16[128,2048]{1,0:T(8,128)(2,1)}, u32[]{:S(2)}) %copy-start.10) | copy-done | bytes 524312
  25.7 1.9 %project_latent.1 = (bf16[576,128]{1,0:T(8,128)(2,1)}, bf16[128,640]{1,0:T(8,128)(2,1)S(1)}) custom-call(bf16[128,2048]{1,0:T(8,128)(2,1)S(1)} %copy-done.10, f32[128,128]{1,0:T(8,128)S(1)} %copy-done.12, bf16[576,2048]{1,0:T(8,128)(2,1)S(1)} %bitcast.15, bf16[512]{0:T(512)(128)(2,1)S(1)} %copy-done.17), custom_call_target="tpu_custom_call" | custom-call | tf_op jit(solution)/shard_map/project_latent/pallas_call | solution.py:248
  27.7 2.3 %collective-permute-done.query = bf16[128,1536]{1,0:T(8,128)(2,1)S(1)} collective-permute-done((bf16[128,1536]{1,0:T(8,128)(2,1)}, bf16[128,1536]{1,0:T(8,128)(2,1)S(1)}, u32[]{:S(2)}, u32[]{:S(2)}) %collective-permute-start) | collective-permute-done | bytes 393248 | tf_op jit(solution)/shard_map/ppermute | solution.py:462
  30.7 2.4 %collective-permute-done.1.query = bf16[128,1536]{1,0:T(8,128)(2,1)} collective-permute-done((bf16[128,1536]{1,0:T(8,128)(2,1)}, bf16[128,1536]{1,0:T(8,128)(2,1)}, u32[]{:S(2)}, u32[]{:S(2)}) %collective-permute-start.1) | collective-permute-done | bytes 393248 | tf_op jit(solution)/shard_map/ppermute | solution.py:462
  34.0 2.2 %collective-permute-start.2 = (bf16[768,640]{1,0:T(8,128)(2,1)S(1)}, bf16[768,640]{1,0:T(8,128)(2,1)S(1)}, u32[]{:S(2)}, u32[]{:S(2)}) collective-permute-start(bf16[768,640]{1,0:T(8,128)(2,1)S(1)} %build_keys.1.near), channel_id=1, source_target_pairs={{0,1},{1,0},{2,3},{3,2},{4,5},{5,4},{6,7},{7,6},{8,9},{9,8},{10,11... | collective-permute-start | bytes 2949128 | tf_op jit(solution)/shard_map/ppermute | solution.py:477
  36.2 0.9 %slice.6 = bf16[64,1536]{1,0:T(8,128)(2,1)S(1)} slice(bf16[128,1536]{1,0:T(8,128)(2,1)} %copy-done.8), slice={[0:64], [0:1536]} | slice | bytes 393216 | tf_op jit(solution)/shard_map/slice | solution.py:474
  37.2 2.0 %collective-permute-start.3 = (bf16[64,1536]{1,0:T(8,128)(2,1)S(1)}, bf16[64,1536]{1,0:T(8,128)(2,1)S(1)}, u32[]{:S(2)}, u32[]{:S(2)}) collective-permute-start(bf16[64,1536]{1,0:T(8,128)(2,1)S(1)} %slice.6), channel_id=1, source_target_pairs={{2,0},{4,2},{6,4},{0,6},{3,1},{5,3},{7,5},{1,7},{10,8},{12,10},{14... | collective-permute-start | bytes 589832 | tf_op jit(solution)/shard_map/ppermute | solution.py:462
  39.2 0.9 %slice.7 = bf16[64,1536]{1,0:T(8,128)(2,1)S(1)} slice(bf16[128,1536]{1,0:T(8,128)(2,1)} %collective-permute-done.1.query), slice={[64:128], [0:1536]} | slice | bytes 393216 | tf_op jit(solution)/shard_map/slice | solution.py:474
  40.3 7.5 %attend_1.1 = (bf16[128,1152]{1,0:T(8,128)(2,1)S(1)}, bf16[1536,640]{1,0:T(8,128)(2,1)S(1)}) custom-call(s32[4]{0:T(128)S(1)} %copy-done.13, bf16[128,1536]{1,0:T(8,128)(2,1)S(1)} %copy-done.9, bf16[8,512,128]{2,1,0:T(8,128)(2,1)S(1)} %copy-done, bf16[8,512,128]{2,1,0:T(8,128)(2,1)S(1)} %copy-done.1, bf16[768,640]{1,0:T(8,128)(2,1)S(1)} %build_keys.1.near, ...), custom_call_target="tpu_custom_call" | custom-call | tf_op jit(solution)/shard_map/attend_1/pallas_call | solution.py:336
  48.1 7.5 %attend_2.1 = bf16[128,1152]{1,0:T(8,128)(2,1)S(1)} custom-call(s32[4]{0:T(128)S(1)} %copy-done.13, bf16[128,1536]{1,0:T(8,128)(2,1)S(1)} %pad_maximum_fusion.query, bf16[8,512,128]{2,1,0:T(8,128)(2,1)S(1)} %copy-done, bf16[8,512,128]{2,1,0:T(8,128)(2,1)S(1)} %copy-done.1, bf16[1536,640]{1,0:T(8,128)(2,1)S(1)} %get-tuple-element.41.near, ...), custom_call_target="tpu_custom_call" | custom-call | tf_op jit(solution)/shard_map/attend_2/pallas_call | solution.py:336
  55.6 1.5 %collective-permute-done.5.one = bf16[128,1152]{1,0:T(8,128)(2,1)S(1)} collective-permute-done((bf16[128,1152]{1,0:T(8,128)(2,1)S(1)}, bf16[128,1152]{1,0:T(8,128)(2,1)S(1)}, u32[]{:S(2)}, u32[]{:S(2)}) %collective-permute-start.5) | collective-permute-done | bytes 294944 | tf_op jit(solution)/shard_map/ppermute | solution.py:462
  57.1 8.1 %attend_3.1 = bf16[128,1152]{1,0:T(8,128)(2,1)S(1)} custom-call(s32[4]{0:T(128)S(1)} %copy-done.13, bf16[128,1536]{1,0:T(8,128)(2,1)} %collective-permute-done.1.query, bf16[8,512,128]{2,1,0:T(8,128)(2,1)S(1)} %copy-done, bf16[8,512,128]{2,1,0:T(8,128)(2,1)S(1)} %copy-done.1, bf16[1536,640]{1,0:T(8,128)(2,1)S(1)} %get-tuple-element.41.near, ...), custom_call_target="tpu_custom_call" | custom-call | tf_op jit(solution)/shard_map/attend_3/pallas_call | solution.py:336
  65.2 2.1 %collective-permute-start.7 = (bf16[128,1152]{1,0:T(8,128)(2,1)S(1)}, bf16[128,1152]{1,0:T(8,128)(2,1)S(1)}, u32[]{:S(2)}, u32[]{:S(2)}) collective-permute-start(bf16[128,1152]{1,0:T(8,128)(2,1)S(1)} %collective-permute-done.6), channel_id=1, source_target_pairs={{6,0},{0,2},{2,4},{4,6},{7,1},{1,3},{3,5},{5,7},{14,8},{8,10},{10,... | collective-permute-start | bytes 884744 | tf_op jit(solution)/shard_map/ppermute | solution.py:462
  68.3 7.5 %attend_0.1.own = bf16[128,1152]{1,0:T(8,128)(2,1)S(1)} custom-call(s32[4]{0:T(128)S(1)} %copy-done.13, bf16[128,1536]{1,0:T(8,128)(2,1)S(1)} %copy-done.11, bf16[8,512,128]{2,1,0:T(8,128)(2,1)S(1)} %copy-done, bf16[8,512,128]{2,1,0:T(8,128)(2,1)S(1)} %copy-done.1, bf16[1536,640]{1,0:T(8,128)(2,1)S(1)} %get-tuple-element.41.near, ...), custom_call_target="tpu_custom_call" | custom-call | tf_op jit(solution)/shard_map/attend_0/pallas_call | solution.py:336
  75.8 1.5 %project_output.1 = (f32[128,2048]{1,0:T(8,128)S(1)}, bf16[128,2048]{1,0:T(8,128)(2,1)S(1)}) custom-call(bf16[128,1152]{1,0:T(8,128)(2,1)S(1)} %attend_0.1.own, bf16[128,1152]{1,0:T(8,128)(2,1)S(1)} %collective-permute-done.5.one, bf16[128,1152]{1,0:T(8,128)(2,1)S(1)} %collective-permute-done.7.two, bf16[128,1152]{1,0:T(8,128)(2,1)S(1)} %collective-permute-done.8.three, ...), custom_call_target="tpu_custom_call" | custom-call | tf_op jit(solution)/shard_map/project_output/pallas_call | solution.py:380
  77.4 2.8 %collective-permute-start.9 = (bf16[128,2048]{1,0:T(8,128)(2,1)S(1)}, bf16[128,2048]{1,0:T(8,128)(2,1)S(1)}, u32[]{:S(2)}, u32[]{:S(2)}) collective-permute-start(bf16[128,2048]{1,0:T(8,128)(2,1)S(1)} %get-tuple-element.50), channel_id=1, source_target_pairs={{0,1},{1,0},{2,3},{3,2},{4,5},{5,4},{6,7},{7,6},{8,9},{9,8},{10,11... | collective-permute-start | bytes 1572872 | tf_op jit(solution)/shard_map/ppermute | solution.py:494
  80.1 1.5 %collective-permute-done.9.other = bf16[128,2048]{1,0:T(8,128)(2,1)S(1)} collective-permute-done((bf16[128,2048]{1,0:T(8,128)(2,1)S(1)}, bf16[128,2048]{1,0:T(8,128)(2,1)S(1)}, u32[]{:S(2)}, u32[]{:S(2)}) %collective-permute-start.9) | collective-permute-done | bytes 524320 | tf_op jit(solution)/shard_map/ppermute | solution.py:494
  81.7 3.2 %expert.1 = (f32[128,1024]{1,0:T(8,128)S(1)}, bf16[128,1024]{1,0:T(8,128)(2,1)S(1)}) custom-call(s32[4]{0:T(128)S(1)} %copy-done.13, bf16[128,2048]{1,0:T(8,128)(2,1)S(1)} %copy-done.7, f32[128,2048]{1,0:T(8,128)S(1)} %get-tuple-element.49.exact, bf16[128,2048]{1,0:T(8,128)(2,1)S(1)} %collective-permute-done.9.other, bf16[2048]{0:T(1024)(128)(2,1)S(1)} %copy-done.15, ...), custom_call_target="tpu_custom_call" | custom-call | tf_op jit(solution)/shard_map/expert/pallas_call | solution.py:411
  85.3 1.2 %collective-permute-done.10 = bf16[128,1024]{1,0:T(8,128)(2,1)S(1)} collective-permute-done((bf16[128,1024]{1,0:T(8,128)(2,1)S(1)}, bf16[128,1024]{1,0:T(8,128)(2,1)S(1)}, u32[]{:S(2)}, u32[]{:S(2)}) %collective-permute-start.10) | collective-permute-done | bytes 262176 | tf_op jit(solution)/shard_map/ppermute | solution.py:505
  (51 shorter events, 5.6 us)
Async XLA Ops:
  5.6 27.5 %all-to-all-start = ((bf16[16,2,16,1152]{3,2,1,0:T(8,128)(2,1)}), bf16[16,2,16,1152]{3,2,1,0:T(8,128)(2,1)S(1)}, u32[]{:S(2)}, u32[]{:S(2)}) async-start(bf16[16,2,16,1152]{3,2,1,0:T(8,128)(2,1)} %bitcast.18), calls=%async_computation | async-start | bytes 2359296 | tf_op jit(solution)/shard_map/all_to_all | solution.py:457
  13.2 9.0 %copy-start.17 = (bf16[512]{0:T(512)(128)(2,1)S(1)}, bf16[512]{0:T(512)(128)(2,1)}, u32[]{:S(2)}) copy-start(bf16[512]{0:T(512)(128)(2,1)} %kv_gain.1) | copy-start | bytes 3076
  13.2 19.9 %copy-start.14 = (s32[16,24,1]{1,2,0:T(1,128)S(1)}, s32[16,24,1]{1,2,0:T(1,128)}, u32[]{:S(2)}) copy-start(s32[16,24,1]{1,2,0:T(1,128)} %param.30) | copy-start | bytes 4612
  18.3 14.8 %copy-start.13 = (s32[4]{0:T(128)S(1)}, s32[4]{0:T(128)}, u32[]{:S(2)}) copy-start(s32[4]{0:T(128)} %pad_add_fusion.place) | copy-start | bytes 52
  18.3 14.8 %copy-start.16 = (s32[16]{0:T(128)S(1)}, s32[16]{0:T(128)}, u32[]{:S(2)}) copy-start(s32[16]{0:T(128)} %count.3) | copy-start | bytes 196
  18.3 11.6 %collective-permute-start = (bf16[128,1536]{1,0:T(8,128)(2,1)}, bf16[128,1536]{1,0:T(8,128)(2,1)S(1)}, u32[]{:S(2)}, u32[]{:S(2)}) collective-permute-start(bf16[128,1536]{1,0:T(8,128)(2,1)} %get-tuple-element.45.query), channel_id=1, source_target_pairs={{2,0},{4,2},{6,4},{0,6},{3,1},{5,3},{7,5},{1,7},{10,8},{12,10},{14... | collective-permute-start | bytes 1179656 | tf_op jit(solution)/shard_map/ppermute | solution.py:462
  22.2 10.9 %collective-permute-start.1 = (bf16[128,1536]{1,0:T(8,128)(2,1)}, bf16[128,1536]{1,0:T(8,128)(2,1)}, u32[]{:S(2)}, u32[]{:S(2)}) collective-permute-start(bf16[128,1536]{1,0:T(8,128)(2,1)} %get-tuple-element.45.query), channel_id=1, source_target_pairs={{6,0},{0,2},{2,4},{4,6},{7,1},{1,3},{3,5},{5,7},{14,8},{8,10},{10,... | collective-permute-start | bytes 1179656 | tf_op jit(solution)/shard_map/ppermute | solution.py:462
  25.7 14.5 %copy-start = (bf16[8,512,128]{2,1,0:T(8,128)(2,1)S(1)}, bf16[8,512,128]{2,1,0:T(8,128)(2,1)}, u32[]{:S(2)}) copy-start(bf16[8,512,128]{2,1,0:T(8,128)(2,1)} %key_up.7) | copy-start | bytes 3145732
  25.7 14.5 %copy-start.1 = (bf16[8,512,128]{2,1,0:T(8,128)(2,1)S(1)}, bf16[8,512,128]{2,1,0:T(8,128)(2,1)}, u32[]{:S(2)}) copy-start(bf16[8,512,128]{2,1,0:T(8,128)(2,1)} %value_up.7) | copy-start | bytes 3145732
  33.1 7.2 %copy-start.9 = (bf16[128,1536]{1,0:T(8,128)(2,1)S(1)}, bf16[128,1536]{1,0:T(8,128)(2,1)}, u32[]{:S(2)}) copy-start(bf16[128,1536]{1,0:T(8,128)(2,1)} %copy-done.8) | copy-start | bytes 1179652
  34.0 6.2 %collective-permute-start.2 = (bf16[768,640]{1,0:T(8,128)(2,1)S(1)}, bf16[768,640]{1,0:T(8,128)(2,1)S(1)}, u32[]{:S(2)}, u32[]{:S(2)}) collective-permute-start(bf16[768,640]{1,0:T(8,128)(2,1)S(1)} %build_keys.1.near), channel_id=1, source_target_pairs={{0,1},{1,0},{2,3},{3,2},{4,5},{5,4},{6,7},{7,6},{8,9},{9,8},{10,11... | collective-permute-start | bytes 2949128 | tf_op jit(solution)/shard_map/ppermute | solution.py:477
  37.2 10.6 %collective-permute-start.3 = (bf16[64,1536]{1,0:T(8,128)(2,1)S(1)}, bf16[64,1536]{1,0:T(8,128)(2,1)S(1)}, u32[]{:S(2)}, u32[]{:S(2)}) collective-permute-start(bf16[64,1536]{1,0:T(8,128)(2,1)S(1)} %slice.6), channel_id=1, source_target_pairs={{2,0},{4,2},{6,4},{0,6},{3,1},{5,3},{7,5},{1,7},{10,8},{12,10},{14... | collective-permute-start | bytes 589832 | tf_op jit(solution)/shard_map/ppermute | solution.py:462
  40.1 7.6 %collective-permute-start.4 = (bf16[64,1536]{1,0:T(8,128)(2,1)S(1)}, bf16[64,1536]{1,0:T(8,128)(2,1)S(1)}, u32[]{:S(2)}, u32[]{:S(2)}) collective-permute-start(bf16[64,1536]{1,0:T(8,128)(2,1)S(1)} %slice.7), channel_id=1, source_target_pairs={{6,0},{0,2},{2,4},{4,6},{7,1},{1,3},{3,5},{5,7},{14,8},{8,10},{10,... | collective-permute-start | bytes 589832 | tf_op jit(solution)/shard_map/ppermute | solution.py:462
  47.8 9.3 %collective-permute-start.5 = (bf16[128,1152]{1,0:T(8,128)(2,1)S(1)}, bf16[128,1152]{1,0:T(8,128)(2,1)S(1)}, u32[]{:S(2)}, u32[]{:S(2)}) collective-permute-start(bf16[128,1152]{1,0:T(8,128)(2,1)S(1)} %get-tuple-element.42), channel_id=1, source_target_pairs={{6,0},{0,2},{2,4},{4,6},{7,1},{1,3},{3,5},{5,7},{14,8},{8,10},{10,... | collective-permute-start | bytes 884744 | tf_op jit(solution)/shard_map/ppermute | solution.py:462
  55.6 12.7 %copy-start.11 = (bf16[128,1536]{1,0:T(8,128)(2,1)S(1)}, bf16[128,1536]{1,0:T(8,128)(2,1)}, u32[]{:S(2)}) copy-start(bf16[128,1536]{1,0:T(8,128)(2,1)} %get-tuple-element.45.query) | copy-start | bytes 1179652
  57.1 8.1 %collective-permute-start.6 = (bf16[128,1152]{1,0:T(8,128)(2,1)S(1)}, bf16[128,1152]{1,0:T(8,128)(2,1)S(1)}, u32[]{:S(2)}, u32[]{:S(2)}) collective-permute-start(bf16[128,1152]{1,0:T(8,128)(2,1)S(1)} %attend_2.1), channel_id=1, source_target_pairs={{6,0},{0,2},{2,4},{4,6},{7,1},{1,3},{3,5},{5,7},{14,8},{8,10},{10,... | collective-permute-start | bytes 884744 | tf_op jit(solution)/shard_map/ppermute | solution.py:462
  57.1 24.6 %copy-start.5 = (bf16[704,2048]{1,0:T(8,128)(2,1)S(1)}, bf16[704,2048]{1,0:T(8,128)(2,1)}, u32[]{:S(2)}) copy-start(bf16[704,2048]{1,0:T(8,128)(2,1)} %w_down.1) | copy-start | bytes 8650756
  57.1 24.6 %copy-start.7 = (bf16[128,2048]{1,0:T(8,128)(2,1)S(1)}, bf16[128,2048]{1,0:T(8,128)(2,1)}, u32[]{:S(2)}) copy-start(bf16[128,2048]{1,0:T(8,128)(2,1)} %tokens.1) | copy-start | bytes 1572868
  65.2 10.6 %copy-start.2 = (bf16[1024,2048]{1,0:T(8,128)(2,1)S(1)}, bf16[1024,2048]{1,0:T(8,128)(2,1)}, u32[]{:S(2)}) copy-start(bf16[1024,2048]{1,0:T(8,128)(2,1)} %weight.1) | copy-start | bytes 12582916
  65.2 10.6 %collective-permute-start.7 = (bf16[128,1152]{1,0:T(8,128)(2,1)S(1)}, bf16[128,1152]{1,0:T(8,128)(2,1)S(1)}, u32[]{:S(2)}, u32[]{:S(2)}) collective-permute-start(bf16[128,1152]{1,0:T(8,128)(2,1)S(1)} %collective-permute-done.6), channel_id=1, source_target_pairs={{6,0},{0,2},{2,4},{4,6},{7,1},{1,3},{3,5},{5,7},{14,8},{8,10},{10,... | collective-permute-start | bytes 884744 | tf_op jit(solution)/shard_map/ppermute | solution.py:462
  67.3 8.4 %collective-permute-start.8 = (bf16[128,1152]{1,0:T(8,128)(2,1)S(1)}, bf16[128,1152]{1,0:T(8,128)(2,1)S(1)}, u32[]{:S(2)}, u32[]{:S(2)}) collective-permute-start(bf16[128,1152]{1,0:T(8,128)(2,1)S(1)} %attend_3.1), channel_id=1, source_target_pairs={{2,0},{4,2},{6,4},{0,6},{3,1},{5,3},{7,5},{1,7},{10,8},{12,10},{14... | collective-permute-start | bytes 884744 | tf_op jit(solution)/shard_map/ppermute | solution.py:462
  68.3 13.4 %copy-start.4 = (bf16[2048,704]{0,1:T(8,128)(2,1)S(1)}, bf16[2048,704]{0,1:T(8,128)(2,1)}, u32[]{:S(2)}) copy-start(bf16[2048,704]{0,1:T(8,128)(2,1)} %param.27) | copy-start | bytes 8650756
  77.4 4.3 %collective-permute-start.9 = (bf16[128,2048]{1,0:T(8,128)(2,1)S(1)}, bf16[128,2048]{1,0:T(8,128)(2,1)S(1)}, u32[]{:S(2)}, u32[]{:S(2)}) collective-permute-start(bf16[128,2048]{1,0:T(8,128)(2,1)S(1)} %get-tuple-element.50), channel_id=1, source_target_pairs={{0,1},{1,0},{2,3},{3,2},{4,5},{5,4},{6,7},{7,6},{8,9},{9,8},{10,11... | collective-permute-start | bytes 1572872 | tf_op jit(solution)/shard_map/ppermute | solution.py:494
  84.9 1.6 %collective-permute-start.10 = (bf16[128,1024]{1,0:T(8,128)(2,1)S(1)}, bf16[128,1024]{1,0:T(8,128)(2,1)S(1)}, u32[]{:S(2)}, u32[]{:S(2)}) collective-permute-start(bf16[128,1024]{1,0:T(8,128)(2,1)S(1)} %get-tuple-element.52), channel_id=1, source_target_pairs={{0,1},{1,0},{2,3},{3,2},{4,5},{5,4},{6,7},{7,6},{8,9},{9,8},{10,11... | collective-permute-start | bytes 786440 | tf_op jit(solution)/shard_map/ppermute | solution.py:505
  (6 other events, 16.1 us)

commit v3 on v2

--- a/solution.py
+++ b/solution.py
@@ -261,13 +261,11 @@
 def attend_kernel(by, n_section, place, query, key_up, value_up, near, *refs):
     n_head, rows = key_up.shape[0], query.shape[0]
     if len(refs) == 5:
-        far, span, out, keys, probes = refs
-        keys[: near.shape[0], :] = near[...]
-        keys[near.shape[0] :, :] = far[...]
+        arrived, span, out, far, probes = refs
+        far[...] = arrived[...]
     else:
-        keys = near
-        span, out, probes = refs
-    blocks = (keys, span)
+        far, span, out, probes = refs
+    blocks = (near, far, span)
     lane = lax.broadcasted_iota(jnp.int32, (rows, 128), 1)
     head_pair = 2 * (NOPE + ROPE)
     at_once = 2
@@ -292,20 +290,25 @@
     else:
         hide = jnp.where(place[2] + by < n_section, 0.0, MASKED_SCORE)
 
-    def score(i):
-        probe = probes[i * tile : (i + 1) * tile, :]
-        parts = [dot_nt(probe, block[...]) for block in blocks]
-        parts[1] = parts[1] + hide
-        return parts
-
-    def finish(i, parts, stats):
-        tops = [jnp.max(part, axis=1, keepdims=True) for part in parts]
-        top = functools.reduce(jnp.maximum, tops)
-        total, summed = 0.0, 0.0
-        for part, block in zip(parts, blocks):
-            weight = jnp.exp2(part - top)
-            total = total + jnp.sum(weight, axis=1, keepdims=True)
-            summed = summed + dot(weight.astype(BF16), block[:, :KVR])
+    pieces, closing = [], []
+    for block in blocks:
+        step = min(256, block.shape[0])
+        for at in range(0, block.shape[0], step):
+            pieces.append((block, at, step))
+            closing.append(at + step == block.shape[0])
+
+    def lanes(value):
+        return [value[:, at : at + 128] for at in range(0, value.shape[1], 128)]
+
+    def score(i, p, peak):
+        block, at, step = pieces[p]
+        value = dot_nt(probes[i * tile : (i + 1) * tile, :], block[at : at + step, :])
+        if block is span:
+            value = value + hide
+        return value, functools.reduce(jnp.maximum, lanes(value), peak)
+
+    def finish(i, total, summed, stats, top):
+        total = jnp.sum(total, axis=1, keepdims=True)
         mixed = (summed * (1.0 / total)).astype(BF16)
         level = top + jnp.log2(total)
         for k in range(at_once):
@@ -316,11 +319,29 @@
         return stats
 
     stats = jnp.zeros((rows, 128), F32)
-    parts = score(0)
+    lowest = jnp.full((tile, 128), MASKED_SCORE, F32)
+    ready, peak = [], lowest
+    for p in range(len(pieces)):
+        value, peak = score(0, p, peak)
+        ready.append(value)
     for i in range(steps):
-        following = score(i + 1) if i + 1 < steps else None
-        stats = finish(i, parts, stats)
-        parts = following
+        top = jnp.max(peak, axis=1, keepdims=True)
+        shift = jnp.broadcast_to(top, (tile, 128))
+        total, summed = jnp.zeros((tile, 128), F32), 0.0
+        coming, peak, weights = [], lowest, []
+        for p in range(len(pieces)):
+            if i + 1 < steps:
+                value, peak = score(i + 1, p, peak)
+                coming.append(value)
+            for part in lanes(ready[p]):
+                weight = jnp.exp2(part - shift)
+                total = total + weight
+                weights.append(weight.astype(BF16))
+            if closing[p]:
+                summed = summed + dot(jnp.concatenate(weights, axis=1), pieces[p][0][:, :KVR])
+                weights = []
+        stats = finish(i, total, summed, stats, top)
+        ready = coming
     high = stats.astype(BF16).astype(F32)
     rest = stats - high
     mid = rest.astype(BF16).astype(F32)
@@ -328,20 +349,20 @@
     out[:, width:] = joined.astype(BF16)
 
 
-def attend(by, n_section, place, query, key_up, value_up, *keys):
+def attend(by, n_section, place, query, key_up, value_up, near, far, span, keep_far=False):
     rows, n_head = query.shape[0], key_up.shape[0]
     out_shape = [jax.ShapeDtypeStruct((rows, n_head * VDIM + 128), BF16)]
-    if len(keys) == 3:
-        out_shape.append(jax.ShapeDtypeStruct((2 * keys[0].shape[0], WIDE), BF16))
+    if keep_far:
+        out_shape.append(jax.ShapeDtypeStruct(far.shape, BF16))
     return pl.pallas_call(
         functools.partial(attend_kernel, by, n_section),
         out_shape=out_shape,
-        in_specs=[SMEM] + [VMEM] * (3 + len(keys)),
+        in_specs=[SMEM] + [VMEM] * 6,
         out_specs=[VMEM] * len(out_shape),
         scratch_shapes=[pltpu.VMEM((n_head * rows, WIDE), BF16)],
         compiler_params=params(28),
         name="attend_%d" % by,
-    )(place, query, key_up, value_up, *keys)
+    )(place, query, key_up, value_up, near, far, span)
 
 
 def output_kernel(n_head, own, one, two, three, weight, exact, send):
@@ -470,26 +491,25 @@
     arrived, next_query, last_query, span = lax.optimization_barrier(
         (arrived, next_query, last_query, span)
     )
-    cut = rows // 2
-    far_low, far_high = shift(next_query[:cut], 1), shift(last_query[cut:], -1)
+    far_query = shift(next_query, 1)
 
     near = build_keys(place, owner, fetch_count, arrived)
     far = lax.ppermute(near, "tp", swap)
 
-    def partial_for(by, query, *keys):
-        return attend(by, n_section, place, query, w_key_up, w_value_up, *keys, span)
-
-    one, keys = partial_for(1, next_query, near, far)
-    one, far_low, far_high = lax.optimization_barrier((one, far_low, far_high))
+    def partial_for(by, query, far, **flags):
+        return attend(by, n_section, place, query, w_key_up, w_value_up, near, far, span, **flags)
+
+    one, far = partial_for(1, next_query, far, keep_far=True)
+    one, far_query = lax.optimization_barrier((one, far_query))
     one = shift(one, -1)
-    (two,) = partial_for(2, jnp.concatenate([far_low, far_high], axis=0), keys)
+    (two,) = partial_for(2, far_query, far)
     two, last_query, one = lax.optimization_barrier((two, last_query, one))
     two = shift(two, -1)
-    (three,) = partial_for(3, last_query, keys)
+    (three,) = partial_for(3, last_query, far)
     three, query, two = lax.optimization_barrier((three, query, two))
     three = shift(three, -3)
     two = shift(two, -1)
-    (own,) = partial_for(0, query, keys)
+    (own,) = partial_for(0, query, far)
     exact, send = project_output(own, one, two, three, w_out)
     incoming = lax.ppermute(send, "tp", swap)
     keep, send = expert(

time: 87.7 us -> 86.7 us (0.989)
  waiting for transfers between devices: 8.86 us -> 12.1 us
  Pallas kernels: 47.5 us -> 44.3 us
  starting transfers between devices: 22.3 us -> 21.4 us
    pallas_call x4, Pallas kernels: 30.6 us -> 27.3 us  [attend(): pl.pallas_call(functools.partial(attend_kernel, by, n_section), out_shape...]
    ppermute x8 -> x7, waiting for transfers between devices: 6.15 us -> 8.52 us  [shift(): return lax.ppermute(value, 'section', pairs)]
    slice x2 -> x0, local copies, waits for them, and re-layouts: 1.88 us -> none  [the longest x1 0.94 us: on_device(): next_query[:cut]]
    unnamed x36 -> x40, local copies, waits for them, and re-layouts: 4.36 us -> 6.1 us
    ppermute x8 -> x7, starting transfers between devices: 9.23 us -> 7.82 us  [shift(): return lax.ppermute(value, 'section', pairs)]
    ppermute x1, waiting for transfers between devices: 0.01 us -> 0.88 us  [on_device(): far = lax.ppermute(near, 'tp', swap)]
  transfers between devices with their start and end apart: 12 -> 11, of which waited for: 5 -> 8; matrix products, arithmetic and copies ran while one was open for 2% -> 0% of each run, Pallas kernels for 43% -> 40%
where the time goes in v3:
time: 86.7 us; the launch traced here: 86.2 us
  Pallas kernels  44.3 us (51%)
  starting transfers between devices  21.4 us (25%)
  waiting for transfers between devices  12.1 us (14%)
  local copies, waits for them, and re-layouts  6.1 us (7%)
  other arithmetic  1.41 us (2%)
  between operations  0.87 us (1%)
    pallas_call x4, Pallas kernels, attend(): pl.pallas_call(functools.partial(attend_kernel, by, n_section), out_shape...  27.3 us
    ppermute x7, waiting for transfers between devices, shift(): return lax.ppermute(value, 'section', pairs)  8.52 us
    ppermute x7, starting transfers between devices, shift(): return lax.ppermute(value, 'section', pairs)  7.82 us
    all_to_all x1, starting transfers between devices, on_device(): lax.all_to_all(outgoing, 'store', split_axis=0, concat_axis=0, tiled=True)  7.6 us
    unnamed x40, local copies, waits for them, and re-layouts  6.1 us
    pallas_call x1, Pallas kernels, project(): pl.pallas_call(project_kernel, out_shape=[jax.ShapeDtypeStruct((rows, col...  5.1 us
    pallas_call x1, Pallas kernels, pack_pages(): pl.pallas_call(pack_kernel, out_shape=jax.ShapeDtypeStruct((n_store, rows...  4.37 us
    ppermute x1, starting transfers between devices, on_device(): incoming = lax.ppermute(send, 'tp', swap)  3.32 us
  transfers between devices with their start and end apart: 11, of which 8 were waited for; matrix products, arithmetic and copies ran while one was open for 0% of the time, Pallas kernels for 40%

profile of v3, /device:TPU:1, one launch (start us, length us, event | category | flops | bytes accessed | tf_op | source)
XLA Modules:
  0.0 86.2 jit_solution(6670511215504223037)
XLA Ops:
  1.3 4.4 %pack_pages.1 = bf16[16,32,1152]{2,1,0:T(8,128)(2,1)} custom-call(s32[4]{0:T(128)} %pad_add_fusion.place, s32[16,24]{1,0:T(8,128)} %bitcast.16, s32[16,24]{1,0:T(8,128)} %slot_src.1, bf16[8,576,256]{2,1,0:T(8,128)(2,1)} %bitcast.19), custom_call_target="tpu_custom_call" | custom-call | tf_op jit(solution)/shard_map/pack_pages/pallas_call | solution.py:113
  5.7 7.6 %all-to-all-start = ((bf16[16,2,16,1152]{3,2,1,0:T(8,128)(2,1)}), bf16[16,2,16,1152]{3,2,1,0:T(8,128)(2,1)S(1)}, u32[]{:S(2)}, u32[]{:S(2)}) async-start(bf16[16,2,16,1152]{3,2,1,0:T(8,128)(2,1)} %bitcast.18), calls=%async_computation | async-start | bytes 2359296 | tf_op jit(solution)/shard_map/all_to_all | solution.py:478
  13.3 5.1 %project.1 = (bf16[128,1536]{1,0:T(8,128)(2,1)}, bf16[128,2048]{1,0:T(8,128)(2,1)}, f32[128,128]{1,0:T(8,128)}) custom-call(s32[4]{0:T(128)} %pad_add_fusion.place, s32[16]{0:T(128)} %count.3, bf16[128,2048]{1,0:T(8,128)(2,1)} %tokens.1, bf16[2048]{0:T(1024)(128)(2,1)} %gain.2, f32[6656,128]{1,0:T(8,128)} %constant.17.clone.table, bf16[2048,1536]{1,0:T(8,128)(2,1)} %w_query_src.1), custom_call_target="tpu_custom_call" | custom-call | tf_op jit(solution)/shard_map/project/pallas_call | solution.py:211
  18.5 3.8 %collective-permute-start = (bf16[128,1536]{1,0:T(8,128)(2,1)}, bf16[128,1536]{1,0:T(8,128)(2,1)S(1)}, u32[]{:S(2)}, u32[]{:S(2)}) collective-permute-start(bf16[128,1536]{1,0:T(8,128)(2,1)} %get-tuple-element.43.query), channel_id=1, source_target_pairs={{2,0},{4,2},{6,4},{0,6},{3,1},{5,3},{7,5},{1,7},{10,8},{12,10},{14... | collective-permute-start | bytes 1179656 | tf_op jit(solution)/shard_map/ppermute | solution.py:483
  22.3 1.7 %copy-done.6 = bf16[2048,576]{0,1:T(8,128)(2,1)S(1)} copy-done((bf16[2048,576]{0,1:T(8,128)(2,1)S(1)}, bf16[2048,576]{0,1:T(8,128)(2,1)}, u32[]{:S(2)}) %copy-start.6) | copy-done | bytes 2359320
  24.0 1.0 %copy-done.8 = bf16[128,2048]{1,0:T(8,128)(2,1)S(1)} copy-done((bf16[128,2048]{1,0:T(8,128)(2,1)S(1)}, bf16[128,2048]{1,0:T(8,128)(2,1)}, u32[]{:S(2)}) %copy-start.8) | copy-done | bytes 524312
  25.8 1.9 %project_latent.1 = (bf16[576,128]{1,0:T(8,128)(2,1)}, bf16[128,640]{1,0:T(8,128)(2,1)S(1)}) custom-call(bf16[128,2048]{1,0:T(8,128)(2,1)S(1)} %copy-done.8, f32[128,128]{1,0:T(8,128)S(1)} %copy-done.14, bf16[576,2048]{1,0:T(8,128)(2,1)S(1)} %bitcast.15, bf16[512]{0:T(512)(128)(2,1)S(1)} %copy-done.19), custom_call_target="tpu_custom_call" | custom-call | tf_op jit(solution)/shard_map/project_latent/pallas_call | solution.py:248
  27.8 2.3 %collective-permute-done.query = bf16[128,1536]{1,0:T(8,128)(2,1)S(1)} collective-permute-done((bf16[128,1536]{1,0:T(8,128)(2,1)}, bf16[128,1536]{1,0:T(8,128)(2,1)S(1)}, u32[]{:S(2)}, u32[]{:S(2)}) %collective-permute-start) | collective-permute-done | bytes 393248 | tf_op jit(solution)/shard_map/ppermute | solution.py:483
  30.8 2.3 %collective-permute-done.1.query = bf16[128,1536]{1,0:T(8,128)(2,1)S(1)} collective-permute-done((bf16[128,1536]{1,0:T(8,128)(2,1)}, bf16[128,1536]{1,0:T(8,128)(2,1)S(1)}, u32[]{:S(2)}, u32[]{:S(2)}) %collective-permute-start.1) | collective-permute-done | bytes 393248 | tf_op jit(solution)/shard_map/ppermute | solution.py:483
  34.7 2.2 %collective-permute-start.2 = (bf16[768,640]{1,0:T(8,128)(2,1)S(1)}, bf16[768,640]{1,0:T(8,128)(2,1)S(1)}, u32[]{:S(2)}, u32[]{:S(2)}) collective-permute-start(bf16[768,640]{1,0:T(8,128)(2,1)S(1)} %build_keys.1.near), channel_id=1, source_target_pairs={{0,1},{1,0},{2,3},{3,2},{4,5},{5,4},{6,7},{7,6},{8,9},{9,8},{10,11... | collective-permute-start | bytes 2949128 | tf_op jit(solution)/shard_map/ppermute | solution.py:497
  37.0 1.3 %collective-permute-start.3 = (bf16[128,1536]{1,0:T(8,128)(2,1)}, bf16[128,1536]{1,0:T(8,128)(2,1)S(1)}, u32[]{:S(2)}, u32[]{:S(2)}) collective-permute-start(bf16[128,1536]{1,0:T(8,128)(2,1)} %copy-done.12), channel_id=1, source_target_pairs={{2,0},{4,2},{6,4},{0,6},{3,1},{5,3},{7,5},{1,7},{10,8},{12,10},{14... | collective-permute-start | bytes 1179656 | tf_op jit(solution)/shard_map/ppermute | solution.py:483
  39.2 1.0 %copy-done.13 = bf16[128,1536]{1,0:T(8,128)(2,1)S(1)} copy-done((bf16[128,1536]{1,0:T(8,128)(2,1)S(1)}, bf16[128,1536]{1,0:T(8,128)(2,1)}, u32[]{:S(2)}) %copy-start.13) | copy-done | bytes 393240
  40.2 6.8 %attend_1.1 = (bf16[128,1152]{1,0:T(8,128)(2,1)S(1)}, bf16[768,640]{1,0:T(8,128)(2,1)S(1)}) custom-call(s32[4]{0:T(128)S(1)} %copy-done.15, bf16[128,1536]{1,0:T(8,128)(2,1)S(1)} %copy-done.13, bf16[8,512,128]{2,1,0:T(8,128)(2,1)S(1)} %copy-done, bf16[8,512,128]{2,1,0:T(8,128)(2,1)S(1)} %copy-done.1, bf16[768,640]{1,0:T(8,128)(2,1)S(1)} %build_keys.1.near, ...), custom_call_target="tpu_custom_call" | custom-call | tf_op jit(solution)/shard_map/attend_1/pallas_call | solution.py:357
  47.9 6.8 %attend_2.1 = bf16[128,1152]{1,0:T(8,128)(2,1)S(1)} custom-call(s32[4]{0:T(128)S(1)} %copy-done.15, bf16[128,1536]{1,0:T(8,128)(2,1)S(1)} %collective-permute-done.3.query, bf16[8,512,128]{2,1,0:T(8,128)(2,1)S(1)} %copy-done, bf16[8,512,128]{2,1,0:T(8,128)(2,1)S(1)} %copy-done.1, bf16[768,640]{1,0:T(8,128)(2,1)S(1)} %build_keys.1.near, ...), custom_call_target="tpu_custom_call" | custom-call | tf_op jit(solution)/shard_map/attend_2/pallas_call | solution.py:357
  54.7 2.0 %collective-permute-done.4.one = bf16[128,1152]{1,0:T(8,128)(2,1)S(1)} collective-permute-done((bf16[128,1152]{1,0:T(8,128)(2,1)S(1)}, bf16[128,1152]{1,0:T(8,128)(2,1)S(1)}, u32[]{:S(2)}, u32[]{:S(2)}) %collective-permute-start.4) | collective-permute-done | bytes 294944 | tf_op jit(solution)/shard_map/ppermute | solution.py:483
  56.8 6.8 %attend_3.1 = bf16[128,1152]{1,0:T(8,128)(2,1)S(1)} custom-call(s32[4]{0:T(128)S(1)} %copy-done.15, bf16[128,1536]{1,0:T(8,128)(2,1)S(1)} %copy-done.11, bf16[8,512,128]{2,1,0:T(8,128)(2,1)S(1)} %copy-done, bf16[8,512,128]{2,1,0:T(8,128)(2,1)S(1)} %copy-done.1, bf16[768,640]{1,0:T(8,128)(2,1)S(1)} %build_keys.1.near, ...), custom_call_target="tpu_custom_call" | custom-call | tf_op jit(solution)/shard_map/attend_3/pallas_call | solution.py:357
  63.6 1.1 %collective-permute-done.5 = bf16[128,1152]{1,0:T(8,128)(2,1)S(1)} collective-permute-done((bf16[128,1152]{1,0:T(8,128)(2,1)S(1)}, bf16[128,1152]{1,0:T(8,128)(2,1)S(1)}, u32[]{:S(2)}, u32[]{:S(2)}) %collective-permute-start.5) | collective-permute-done | bytes 294944 | tf_op jit(solution)/shard_map/ppermute | solution.py:483
  65.1 2.3 %collective-permute-start.7 = (bf16[128,1152]{1,0:T(8,128)(2,1)S(1)}, bf16[128,1152]{1,0:T(8,128)(2,1)S(1)}, u32[]{:S(2)}, u32[]{:S(2)}) collective-permute-start(bf16[128,1152]{1,0:T(8,128)(2,1)S(1)} %attend_3.1), channel_id=1, source_target_pairs={{2,0},{4,2},{6,4},{0,6},{3,1},{5,3},{7,5},{1,7},{10,8},{12,10},{14... | collective-permute-start | bytes 884744 | tf_op jit(solution)/shard_map/ppermute | solution.py:483
  67.4 6.8 %attend_0.1.own = bf16[128,1152]{1,0:T(8,128)(2,1)S(1)} custom-call(s32[4]{0:T(128)S(1)} %copy-done.15, bf16[128,1536]{1,0:T(8,128)(2,1)S(1)} %copy-done.9, bf16[8,512,128]{2,1,0:T(8,128)(2,1)S(1)} %copy-done, bf16[8,512,128]{2,1,0:T(8,128)(2,1)S(1)} %copy-done.1, bf16[768,640]{1,0:T(8,128)(2,1)S(1)} %build_keys.1.near, ...), custom_call_target="tpu_custom_call" | custom-call | tf_op jit(solution)/shard_map/attend_0/pallas_call | solution.py:357
  74.3 1.5 %project_output.1 = (f32[128,2048]{1,0:T(8,128)S(1)}, bf16[128,2048]{1,0:T(8,128)(2,1)S(1)}) custom-call(bf16[128,1152]{1,0:T(8,128)(2,1)S(1)} %attend_0.1.own, bf16[128,1152]{1,0:T(8,128)(2,1)S(1)} %collective-permute-done.4.one, bf16[128,1152]{1,0:T(8,128)(2,1)S(1)} %collective-permute-done.6.two, bf16[128,1152]{1,0:T(8,128)(2,1)S(1)} %collective-permute-done.7.three, ...), custom_call_target="tpu_custom_call" | custom-call | tf_op jit(solution)/shard_map/project_output/pallas_call | solution.py:401
  75.8 3.3 %collective-permute-start.8 = (bf16[128,2048]{1,0:T(8,128)(2,1)S(1)}, bf16[128,2048]{1,0:T(8,128)(2,1)S(1)}, u32[]{:S(2)}, u32[]{:S(2)}) collective-permute-start(bf16[128,2048]{1,0:T(8,128)(2,1)S(1)} %get-tuple-element.48), channel_id=1, source_target_pairs={{0,1},{1,0},{2,3},{3,2},{4,5},{5,4},{6,7},{7,6},{8,9},{9,8},{10,11... | collective-permute-start | bytes 1572872 | tf_op jit(solution)/shard_map/ppermute | solution.py:514
  79.1 1.5 %collective-permute-done.8.other = bf16[128,2048]{1,0:T(8,128)(2,1)S(1)} collective-permute-done((bf16[128,2048]{1,0:T(8,128)(2,1)S(1)}, bf16[128,2048]{1,0:T(8,128)(2,1)S(1)}, u32[]{:S(2)}, u32[]{:S(2)}) %collective-permute-start.8) | collective-permute-done | bytes 524320 | tf_op jit(solution)/shard_map/ppermute | solution.py:514
  80.7 3.1 %expert.1 = (f32[128,1024]{1,0:T(8,128)S(1)}, bf16[128,1024]{1,0:T(8,128)(2,1)S(1)}) custom-call(s32[4]{0:T(128)S(1)} %copy-done.15, bf16[128,2048]{1,0:T(8,128)(2,1)S(1)} %copy-done.7, f32[128,2048]{1,0:T(8,128)S(1)} %get-tuple-element.47.exact, bf16[128,2048]{1,0:T(8,128)(2,1)S(1)} %collective-permute-done.8.other, bf16[2048]{0:T(1024)(128)(2,1)S(1)} %copy-done.17, ...), custom_call_target="tpu_custom_call" | custom-call | tf_op jit(solution)/shard_map/expert/pallas_call | solution.py:432
  84.3 1.2 %collective-permute-done.9 = bf16[128,1024]{1,0:T(8,128)(2,1)S(1)} collective-permute-done((bf16[128,1024]{1,0:T(8,128)(2,1)S(1)}, bf16[128,1024]{1,0:T(8,128)(2,1)S(1)}, u32[]{:S(2)}, u32[]{:S(2)}) %collective-permute-start.9) | collective-permute-done | bytes 262176 | tf_op jit(solution)/shard_map/ppermute | solution.py:525
  (50 shorter events, 7.3 us)
Async XLA Ops:
  5.7 28.2 %all-to-all-start = ((bf16[16,2,16,1152]{3,2,1,0:T(8,128)(2,1)}), bf16[16,2,16,1152]{3,2,1,0:T(8,128)(2,1)S(1)}, u32[]{:S(2)}, u32[]{:S(2)}) async-start(bf16[16,2,16,1152]{3,2,1,0:T(8,128)(2,1)} %bitcast.18), calls=%async_computation | async-start | bytes 2359296 | tf_op jit(solution)/shard_map/all_to_all | solution.py:478
  13.3 9.0 %copy-start.19 = (bf16[512]{0:T(512)(128)(2,1)S(1)}, bf16[512]{0:T(512)(128)(2,1)}, u32[]{:S(2)}) copy-start(bf16[512]{0:T(512)(128)(2,1)} %kv_gain.1) | copy-start | bytes 3076
  13.3 20.5 %copy-start.15 = (s32[4]{0:T(128)S(1)}, s32[4]{0:T(128)}, u32[]{:S(2)}) copy-start(s32[4]{0:T(128)} %pad_add_fusion.place) | copy-start | bytes 52
  13.3 20.5 %copy-start.16 = (s32[16,24,1]{1,2,0:T(1,128)S(1)}, s32[16,24,1]{1,2,0:T(1,128)}, u32[]{:S(2)}) copy-start(s32[16,24,1]{1,2,0:T(1,128)} %param.30) | copy-start | bytes 4612
  13.3 20.5 %copy-start.18 = (s32[16]{0:T(128)S(1)}, s32[16]{0:T(128)}, u32[]{:S(2)}) copy-start(s32[16]{0:T(128)} %count.3) | copy-start | bytes 196
  18.4 20.7 %copy-start = (bf16[8,512,128]{2,1,0:T(8,128)(2,1)S(1)}, bf16[8,512,128]{2,1,0:T(8,128)(2,1)}, u32[]{:S(2)}) copy-start(bf16[8,512,128]{2,1,0:T(8,128)(2,1)} %key_up.7) | copy-start | bytes 3145732
  18.4 20.7 %copy-start.1 = (bf16[8,512,128]{2,1,0:T(8,128)(2,1)S(1)}, bf16[8,512,128]{2,1,0:T(8,128)(2,1)}, u32[]{:S(2)}) copy-start(bf16[8,512,128]{2,1,0:T(8,128)(2,1)} %value_up.7) | copy-start | bytes 3145732
  18.5 11.6 %collective-permute-start = (bf16[128,1536]{1,0:T(8,128)(2,1)}, bf16[128,1536]{1,0:T(8,128)(2,1)S(1)}, u32[]{:S(2)}, u32[]{:S(2)}) collective-permute-start(bf16[128,1536]{1,0:T(8,128)(2,1)} %get-tuple-element.43.query), channel_id=1, source_target_pairs={{2,0},{4,2},{6,4},{0,6},{3,1},{5,3},{7,5},{1,7},{10,8},{12,10},{14... | collective-permute-start | bytes 1179656 | tf_op jit(solution)/shard_map/ppermute | solution.py:483
  22.3 10.8 %collective-permute-start.1 = (bf16[128,1536]{1,0:T(8,128)(2,1)}, bf16[128,1536]{1,0:T(8,128)(2,1)S(1)}, u32[]{:S(2)}, u32[]{:S(2)}) collective-permute-start(bf16[128,1536]{1,0:T(8,128)(2,1)} %get-tuple-element.43.query), channel_id=1, source_target_pairs={{6,0},{0,2},{2,4},{4,6},{7,1},{1,3},{3,5},{5,7},{14,8},{8,10},{10,... | collective-permute-start | bytes 1179656 | tf_op jit(solution)/shard_map/ppermute | solution.py:483
  34.7 4.4 %collective-permute-start.2 = (bf16[768,640]{1,0:T(8,128)(2,1)S(1)}, bf16[768,640]{1,0:T(8,128)(2,1)S(1)}, u32[]{:S(2)}, u32[]{:S(2)}) collective-permute-start(bf16[768,640]{1,0:T(8,128)(2,1)S(1)} %build_keys.1.near), channel_id=1, source_target_pairs={{0,1},{1,0},{2,3},{3,2},{4,5},{5,4},{6,7},{7,6},{8,9},{9,8},{10,11... | collective-permute-start | bytes 2949128 | tf_op jit(solution)/shard_map/ppermute | solution.py:497
  37.0 10.9 %collective-permute-start.3 = (bf16[128,1536]{1,0:T(8,128)(2,1)}, bf16[128,1536]{1,0:T(8,128)(2,1)S(1)}, u32[]{:S(2)}, u32[]{:S(2)}) collective-permute-start(bf16[128,1536]{1,0:T(8,128)(2,1)} %copy-done.12), channel_id=1, source_target_pairs={{2,0},{4,2},{6,4},{0,6},{3,1},{5,3},{7,5},{1,7},{10,8},{12,10},{14... | collective-permute-start | bytes 1179656 | tf_op jit(solution)/shard_map/ppermute | solution.py:483
  47.0 9.7 %copy-start.11 = (bf16[128,1536]{1,0:T(8,128)(2,1)S(1)}, bf16[128,1536]{1,0:T(8,128)(2,1)}, u32[]{:S(2)}) copy-start(bf16[128,1536]{1,0:T(8,128)(2,1)} %copy-done.10) | copy-start | bytes 1179652
  47.9 8.9 %collective-permute-start.4 = (bf16[128,1152]{1,0:T(8,128)(2,1)S(1)}, bf16[128,1152]{1,0:T(8,128)(2,1)S(1)}, u32[]{:S(2)}, u32[]{:S(2)}) collective-permute-start(bf16[128,1152]{1,0:T(8,128)(2,1)S(1)} %get-tuple-element.40), channel_id=1, source_target_pairs={{6,0},{0,2},{2,4},{4,6},{7,1},{1,3},{3,5},{5,7},{14,8},{8,10},{10,... | collective-permute-start | bytes 884744 | tf_op jit(solution)/shard_map/ppermute | solution.py:483
  54.7 12.7 %copy-start.9 = (bf16[128,1536]{1,0:T(8,128)(2,1)S(1)}, bf16[128,1536]{1,0:T(8,128)(2,1)}, u32[]{:S(2)}) copy-start(bf16[128,1536]{1,0:T(8,128)(2,1)} %get-tuple-element.43.query) | copy-start | bytes 1179652
  56.7 8.0 %collective-permute-start.5 = (bf16[128,1152]{1,0:T(8,128)(2,1)S(1)}, bf16[128,1152]{1,0:T(8,128)(2,1)S(1)}, u32[]{:S(2)}, u32[]{:S(2)}) collective-permute-start(bf16[128,1152]{1,0:T(8,128)(2,1)S(1)} %attend_2.1), channel_id=1, source_target_pairs={{6,0},{0,2},{2,4},{4,6},{7,1},{1,3},{3,5},{5,7},{14,8},{8,10},{10,... | collective-permute-start | bytes 884744 | tf_op jit(solution)/shard_map/ppermute | solution.py:483
  56.7 23.9 %copy-start.5 = (bf16[704,2048]{1,0:T(8,128)(2,1)S(1)}, bf16[704,2048]{1,0:T(8,128)(2,1)}, u32[]{:S(2)}) copy-start(bf16[704,2048]{1,0:T(8,128)(2,1)} %w_down.1) | copy-start | bytes 8650756
  56.7 23.9 %copy-start.7 = (bf16[128,2048]{1,0:T(8,128)(2,1)S(1)}, bf16[128,2048]{1,0:T(8,128)(2,1)}, u32[]{:S(2)}) copy-start(bf16[128,2048]{1,0:T(8,128)(2,1)} %tokens.1) | copy-start | bytes 1572868
  63.6 10.7 %copy-start.2 = (bf16[1024,2048]{1,0:T(8,128)(2,1)S(1)}, bf16[1024,2048]{1,0:T(8,128)(2,1)}, u32[]{:S(2)}) copy-start(bf16[1024,2048]{1,0:T(8,128)(2,1)} %weight.1) | copy-start | bytes 12582916
  64.7 9.5 %collective-permute-start.6 = (bf16[128,1152]{1,0:T(8,128)(2,1)S(1)}, bf16[128,1152]{1,0:T(8,128)(2,1)S(1)}, u32[]{:S(2)}, u32[]{:S(2)}) collective-permute-start(bf16[128,1152]{1,0:T(8,128)(2,1)S(1)} %collective-permute-done.5), channel_id=1, source_target_pairs={{6,0},{0,2},{2,4},{4,6},{7,1},{1,3},{3,5},{5,7},{14,8},{8,10},{10,... | collective-permute-start | bytes 884744 | tf_op jit(solution)/shard_map/ppermute | solution.py:483
  65.1 9.2 %collective-permute-start.7 = (bf16[128,1152]{1,0:T(8,128)(2,1)S(1)}, bf16[128,1152]{1,0:T(8,128)(2,1)S(1)}, u32[]{:S(2)}, u32[]{:S(2)}) collective-permute-start(bf16[128,1152]{1,0:T(8,128)(2,1)S(1)} %attend_3.1), channel_id=1, source_target_pairs={{2,0},{4,2},{6,4},{0,6},{3,1},{5,3},{7,5},{1,7},{10,8},{12,10},{14... | collective-permute-start | bytes 884744 | tf_op jit(solution)/shard_map/ppermute | solution.py:483
  67.4 13.3 %copy-start.4 = (bf16[2048,704]{0,1:T(8,128)(2,1)S(1)}, bf16[2048,704]{0,1:T(8,128)(2,1)}, u32[]{:S(2)}) copy-start(bf16[2048,704]{0,1:T(8,128)(2,1)} %param.27) | copy-start | bytes 8650756
  74.2 6.5 %copy-start.3 = (bf16[2048,704]{0,1:T(8,128)(2,1)S(1)}, bf16[2048,704]{0,1:T(8,128)(2,1)}, u32[]{:S(2)}) copy-start(bf16[2048,704]{0,1:T(8,128)(2,1)} %param.26) | copy-start | bytes 8650756
  75.8 4.9 %collective-permute-start.8 = (bf16[128,2048]{1,0:T(8,128)(2,1)S(1)}, bf16[128,2048]{1,0:T(8,128)(2,1)S(1)}, u32[]{:S(2)}, u32[]{:S(2)}) collective-permute-start(bf16[128,2048]{1,0:T(8,128)(2,1)S(1)} %get-tuple-element.48), channel_id=1, source_target_pairs={{0,1},{1,0},{2,3},{3,2},{4,5},{5,4},{6,7},{7,6},{8,9},{9,8},{10,11... | collective-permute-start | bytes 1572872 | tf_op jit(solution)/shard_map/ppermute | solution.py:514
  83.8 1.6 %collective-permute-start.9 = (bf16[128,1024]{1,0:T(8,128)(2,1)S(1)}, bf16[128,1024]{1,0:T(8,128)(2,1)S(1)}, u32[]{:S(2)}, u32[]{:S(2)}) collective-permute-start(bf16[128,1024]{1,0:T(8,128)(2,1)S(1)} %get-tuple-element.50), channel_id=1, source_target_pairs={{0,1},{1,0},{2,3},{3,2},{4,5},{5,4},{6,7},{7,6},{8,9},{9,8},{10,11... | collective-permute-start | bytes 786440 | tf_op jit(solution)/shard_map/ppermute | solution.py:525
  (7 other events, 12.5 us)

commit v4 on v3

--- a/solution.py
+++ b/solution.py
@@ -258,30 +258,62 @@
     )(normed, turns, w_latent_t, kv_gain)
 
 
-def attend_kernel(by, n_section, place, query, key_up, value_up, near, *refs):
-    n_head, rows = key_up.shape[0], query.shape[0]
-    if len(refs) == 5:
-        arrived, span, out, far, probes = refs
+def fill_probes(query, key_up, probes):
+    rows = query.shape[0]
+    pair_width = 2 * (NOPE + ROPE)
+    lane = lax.broadcasted_iota(jnp.int32, (rows, 2 * NOPE), 1)
+    rope_lane = lane[:, : 2 * ROPE]
+    for h in range(0, key_up.shape[0], 2):
+        base = (h // 2) * pair_width
+        nope = query[:, base : base + 2 * NOPE].astype(F32)
+        both = jnp.concatenate(
+            [jnp.where(lane < NOPE, nope, 0.0), jnp.where(lane < NOPE, 0.0, nope)], axis=0
+        )
+        maps = jnp.concatenate([key_up[h], key_up[h + 1]], axis=1)
+        at = pl.ds(h * rows, 2 * rows)
+        probes[at, :KVR] = (dot_nt(both.astype(BF16), maps) * SCALE).astype(BF16)
+        pair = query[:, base + 2 * NOPE : base + pair_width].astype(F32)
+        pair = jnp.concatenate([pair, pltpu.roll(pair, ROPE, axis=1)], axis=0)
+        rope_lanes = jnp.concatenate([rope_lane, rope_lane], axis=0)
+        one = jnp.where(rope_lanes == ROPE, 1.0, 0.0)
+        probes[at, KVR:] = jnp.where(rope_lanes < ROPE, pair, one).astype(BF16)
+
+
+def probes_kernel(key_up, *refs):
+    count = len(refs) // 2
+    for query, probes in zip(refs[:count], refs[count:]):
+        fill_probes(query, key_up, probes)
+
+
+def make_probes(key_up, *queries):
+    rows = queries[0].shape[0]
+    return pl.pallas_call(
+        probes_kernel,
+        out_shape=[jax.ShapeDtypeStruct((key_up.shape[0] * rows, WIDE), BF16)] * len(queries),
+        in_specs=[VMEM] * (1 + len(queries)),
+        out_specs=[VMEM] * len(queries),
+        compiler_params=params(16),
+        name="make_probes",
+    )(key_up, *queries)
+
+
+def attend_kernel(by, n_section, keep_far, place, value_up, near, arrived, span, *refs):
+    far = arrived
+    if by == 2:
+        query, key_up, out, probes = refs
+        fill_probes(query, key_up, probes)
+    elif keep_far:
+        probes, out, far = refs
         far[...] = arrived[...]
     else:
-        far, span, out, probes = refs
+        probes, out = refs
+    n_head, rows = value_up.shape[0], out.shape[0]
     blocks = (near, far, span)
     lane = lax.broadcasted_iota(jnp.int32, (rows, 128), 1)
-    head_pair = 2 * (NOPE + ROPE)
-    at_once = 2
+    at_once = 4
     tile = at_once * rows
     steps = n_head // at_once
     width = n_head * NOPE
-    for h in range(n_head):
-        at = pl.ds(h * rows, rows)
-        base = (h // 2) * head_pair
-        nope = query[:, base + (h % 2) * NOPE : base + (h % 2 + 1) * NOPE]
-        probes[at, :KVR] = (dot_nt(nope, key_up[h]) * SCALE).astype(BF16)
-        pair = query[:, base + 2 * NOPE : base + head_pair].astype(F32)
-        if h % 2 == 1:
-            pair = pltpu.roll(pair, ROPE, axis=1)
-        one = jnp.where(lane == ROPE, 1.0, 0.0)
-        probes[at, KVR:] = jnp.where(lane < ROPE, pair, one).astype(BF16)
 
     if by == 0:
         row_of = lax.broadcasted_iota(jnp.int32, (tile, rows), 0) & (rows - 1)
@@ -311,11 +343,14 @@
         total = jnp.sum(total, axis=1, keepdims=True)
         mixed = (summed * (1.0 / total)).astype(BF16)
         level = top + jnp.log2(total)
+        for k in range(0, at_once, 2):
+            h = i * at_once + k
+            maps = jnp.concatenate([value_up[h], value_up[h + 1]], axis=1)
+            value = dot(mixed[k * rows : (k + 2) * rows], maps).astype(BF16)
+            out[:, h * VDIM : (h + 1) * VDIM] = value[:rows, :VDIM]
+            out[:, (h + 1) * VDIM : (h + 2) * VDIM] = value[rows:, VDIM:]
         for k in range(at_once):
-            h = i * at_once + k
-            value = dot(mixed[k * rows : (k + 1) * rows], value_up[h])
-            out[:, h * VDIM : (h + 1) * VDIM] = value.astype(BF16)
-            stats = jnp.where(lane == h, level[k * rows : (k + 1) * rows], stats)
+            stats = jnp.where(lane == i * at_once + k, level[k * rows : (k + 1) * rows], stats)
         return stats
 
     stats = jnp.zeros((rows, 128), F32)
@@ -349,20 +384,21 @@
     out[:, width:] = joined.astype(BF16)
 
 
-def attend(by, n_section, place, query, key_up, value_up, near, far, span, keep_far=False):
-    rows, n_head = query.shape[0], key_up.shape[0]
+def attend(by, n_section, place, value_up, near, far, span, *queries, keep_far=False):
+    rows, n_head = span.shape[0], value_up.shape[0]
     out_shape = [jax.ShapeDtypeStruct((rows, n_head * VDIM + 128), BF16)]
     if keep_far:
         out_shape.append(jax.ShapeDtypeStruct(far.shape, BF16))
-    return pl.pallas_call(
-        functools.partial(attend_kernel, by, n_section),
+    scratch = [pltpu.VMEM((n_head * rows, WIDE), BF16)] if by == 2 else []
+    return pl.pallas_call(
+        functools.partial(attend_kernel, by, n_section, keep_far),
         out_shape=out_shape,
-        in_specs=[SMEM] + [VMEM] * 6,
+        in_specs=[SMEM] + [VMEM] * (4 + len(queries)),
         out_specs=[VMEM] * len(out_shape),
-        scratch_shapes=[pltpu.VMEM((n_head * rows, WIDE), BF16)],
-        compiler_params=params(28),
+        scratch_shapes=scratch,
+        compiler_params=params(32),
         name="attend_%d" % by,
-    )(place, query, key_up, value_up, near, far, span)
+    )(place, value_up, near, far, span, *queries)
 
 
 def output_kernel(n_head, own, one, two, three, weight, exact, send):
@@ -496,20 +532,22 @@
     near = build_keys(place, owner, fetch_count, arrived)
     far = lax.ppermute(near, "tp", swap)
 
-    def partial_for(by, query, far, **flags):
-        return attend(by, n_section, place, query, w_key_up, w_value_up, near, far, span, **flags)
-
-    one, far = partial_for(1, next_query, far, keep_far=True)
+    own_probes, next_probes, last_probes = make_probes(w_key_up, query, next_query, last_query)
+
+    def partial_for(by, far, *queries, **flags):
+        return attend(by, n_section, place, w_value_up, near, far, span, *queries, **flags)
+
+    one, far = partial_for(1, far, next_probes, keep_far=True)
     one, far_query = lax.optimization_barrier((one, far_query))
     one = shift(one, -1)
-    (two,) = partial_for(2, far_query, far)
-    two, last_query, one = lax.optimization_barrier((two, last_query, one))
+    (two,) = partial_for(2, far, far_query, w_key_up)
+    two, last_probes, one = lax.optimization_barrier((two, last_probes, one))
     two = shift(two, -1)
-    (three,) = partial_for(3, last_query, far)
-    three, query, two = lax.optimization_barrier((three, query, two))
+    (three,) = partial_for(3, far, last_probes)
+    three, own_probes, two = lax.optimization_barrier((three, own_probes, two))
     three = shift(three, -3)
     two = shift(two, -1)
-    (own,) = partial_for(0, query, far)
+    (own,) = partial_for(0, far, own_probes)
     exact, send = project_output(own, one, two, three, w_out)
     incoming = lax.ppermute(send, "tp", swap)
     keep, send = expert(

time: 86.7 us -> 86.2 us (level)
  starting transfers between devices: 21.4 us -> 23.6 us
  local copies, waits for them, and re-layouts: 6.1 us -> 4.36 us
    ppermute x7, starting transfers between devices: 7.82 us -> 10.7 us  [shift(): return lax.ppermute(value, 'section', pairs)]
    unnamed x40 -> x36, local copies, waits for them, and re-layouts: 6.1 us -> 4.36 us
    ppermute x1, waiting for transfers between devices: 0.88 us -> 0.01 us  [on_device(): far = lax.ppermute(near, 'tp', swap)]
    pallas_call x4 -> x5, Pallas kernels: 27.3 us -> 27.2 us  [the longest x4 25.1 us: attend(): pl.pallas_call(functools.partial(attend_kernel, by, n_section, keep_far),...]
  transfers between devices with their start and end apart: 11 -> 11, of which waited for: 8 -> 6; matrix products, arithmetic and copies ran while one was open for 0% -> 0% of each run, Pallas kernels for 40% -> 40%
where the time goes in v4:
time: 86.2 us; the launch traced here: 85.8 us
  Pallas kernels  44.2 us (51%)
  starting transfers between devices  23.6 us (27%)
  waiting for transfers between devices  11.4 us (13%)
  local copies, waits for them, and re-layouts  4.36 us (5%)
  other arithmetic  1.36 us (2%)
  between operations  0.87 us (1%)
    pallas_call x4, Pallas kernels, attend(): pl.pallas_call(functools.partial(attend_kernel, by, n_section, keep_far),...  25.1 us
    ppermute x7, starting transfers between devices, shift(): return lax.ppermute(value, 'section', pairs)  10.7 us
    ppermute x7, waiting for transfers between devices, shift(): return lax.ppermute(value, 'section', pairs)  8.69 us
    all_to_all x1, starting transfers between devices, on_device(): lax.all_to_all(outgoing, 'store', split_axis=0, concat_axis=0, tiled=True)  7.6 us
    pallas_call x1, Pallas kernels, project(): pl.pallas_call(project_kernel, out_shape=[jax.ShapeDtypeStruct((rows, col...  5.12 us
    unnamed x36, local copies, waits for them, and re-layouts  4.36 us
    pallas_call x1, Pallas kernels, pack_pages(): pl.pallas_call(pack_kernel, out_shape=jax.ShapeDtypeStruct((n_store, rows...  4.34 us
    pallas_call x1, Pallas kernels, expert(): pl.pallas_call(expert_kernel, out_shape=[jax.ShapeDtypeStruct((rows, half...  3.15 us
  transfers between devices with their start and end apart: 11, of which 6 were waited for; matrix products, arithmetic and copies ran while one was open for 0% of the time, Pallas kernels for 40%

profile of v4, /device:TPU:1, one launch (start us, length us, event | category | flops | bytes accessed | tf_op | source)
XLA Modules:
  0.0 85.8 jit_solution(2558090523182984807)
XLA Ops:
  1.2 4.3 %pack_pages.1 = bf16[16,32,1152]{2,1,0:T(8,128)(2,1)} custom-call(s32[4]{0:T(128)} %pad_add_fusion.place, s32[16,24]{1,0:T(8,128)} %bitcast.16, s32[16,24]{1,0:T(8,128)} %slot_src.1, bf16[8,576,256]{2,1,0:T(8,128)(2,1)} %bitcast.19), custom_call_target="tpu_custom_call" | custom-call | tf_op jit(solution)/shard_map/pack_pages/pallas_call | solution.py:113
  5.6 7.6 %all-to-all-start = ((bf16[16,2,16,1152]{3,2,1,0:T(8,128)(2,1)}), bf16[16,2,16,1152]{3,2,1,0:T(8,128)(2,1)S(1)}, u32[]{:S(2)}, u32[]{:S(2)}) async-start(bf16[16,2,16,1152]{3,2,1,0:T(8,128)(2,1)} %bitcast.18), calls=%async_computation | async-start | bytes 2359296 | tf_op jit(solution)/shard_map/all_to_all | solution.py:514
  13.2 5.1 %project.1 = (bf16[128,1536]{1,0:T(8,128)(2,1)}, bf16[128,2048]{1,0:T(8,128)(2,1)}, f32[128,128]{1,0:T(8,128)}) custom-call(s32[4]{0:T(128)} %pad_add_fusion.place, s32[16]{0:T(128)} %count.3, bf16[128,2048]{1,0:T(8,128)(2,1)} %tokens.1, bf16[2048]{0:T(1024)(128)(2,1)} %gain.2, f32[6656,128]{1,0:T(8,128)} %constant.17.clone.table, bf16[2048,1536]{1,0:T(8,128)(2,1)} %w_query_src.1), custom_call_target="tpu_custom_call" | custom-call | tf_op jit(solution)/shard_map/project/pallas_call | solution.py:211
  18.4 1.7 %collective-permute-start.1 = (bf16[128,1536]{1,0:T(8,128)(2,1)}, bf16[128,1536]{1,0:T(8,128)(2,1)S(1)}, u32[]{:S(2)}, u32[]{:S(2)}) collective-permute-start(bf16[128,1536]{1,0:T(8,128)(2,1)} %get-tuple-element.32.refs_0_), channel_id=1, source_target_pairs={{6,0},{0,2},{2,4},{4,6},{7,1},{1,3},{3,5},{5,7},{14,8},{8,10},{10,... | collective-permute-start | bytes 1179656 | tf_op jit(solution)/shard_map/ppermute | solution.py:519
  20.1 2.2 %collective-permute-start = (bf16[128,1536]{1,0:T(8,128)(2,1)}, bf16[128,1536]{1,0:T(8,128)(2,1)}, u32[]{:S(2)}, u32[]{:S(2)}) collective-permute-start(bf16[128,1536]{1,0:T(8,128)(2,1)} %get-tuple-element.32.refs_0_), channel_id=1, source_target_pairs={{2,0},{4,2},{6,4},{0,6},{3,1},{5,3},{7,5},{1,7},{10,8},{12,10},{14... | collective-permute-start | bytes 1179656 | tf_op jit(solution)/shard_map/ppermute | solution.py:519
  22.3 1.7 %copy-done.6 = bf16[2048,576]{0,1:T(8,128)(2,1)S(1)} copy-done((bf16[2048,576]{0,1:T(8,128)(2,1)S(1)}, bf16[2048,576]{0,1:T(8,128)(2,1)}, u32[]{:S(2)}) %copy-start.6) | copy-done | bytes 2359320
  23.9 1.0 %copy-done.8 = bf16[128,2048]{1,0:T(8,128)(2,1)S(1)} copy-done((bf16[128,2048]{1,0:T(8,128)(2,1)S(1)}, bf16[128,2048]{1,0:T(8,128)(2,1)}, u32[]{:S(2)}) %copy-start.8) | copy-done | bytes 524312
  25.8 1.9 %project_latent.1 = (bf16[576,128]{1,0:T(8,128)(2,1)}, bf16[128,640]{1,0:T(8,128)(2,1)S(1)}) custom-call(bf16[128,2048]{1,0:T(8,128)(2,1)S(1)} %copy-done.8, f32[128,128]{1,0:T(8,128)S(1)} %copy-done.12, bf16[576,2048]{1,0:T(8,128)(2,1)S(1)} %bitcast.15, bf16[512]{0:T(512)(128)(2,1)S(1)} %copy-done.17), custom_call_target="tpu_custom_call" | custom-call | tf_op jit(solution)/shard_map/project_latent/pallas_call | solution.py:248
  27.8 3.1 %collective-permute-done.1.refs_2_ = bf16[128,1536]{1,0:T(8,128)(2,1)S(1)} collective-permute-done((bf16[128,1536]{1,0:T(8,128)(2,1)}, bf16[128,1536]{1,0:T(8,128)(2,1)S(1)}, u32[]{:S(2)}, u32[]{:S(2)}) %collective-permute-start.1) | collective-permute-done | bytes 393248 | tf_op jit(solution)/shard_map/ppermute | solution.py:519
  32.6 1.8 %collective-permute-start.2 = (bf16[768,640]{1,0:T(8,128)(2,1)S(1)}, bf16[768,640]{1,0:T(8,128)(2,1)S(1)}, u32[]{:S(2)}, u32[]{:S(2)}) collective-permute-start(bf16[768,640]{1,0:T(8,128)(2,1)S(1)} %build_keys.1.near), channel_id=1, source_target_pairs={{0,1},{1,0},{2,3},{3,2},{4,5},{5,4},{6,7},{7,6},{8,9},{9,8},{10,11... | collective-permute-start | bytes 2949128 | tf_op jit(solution)/shard_map/ppermute | solution.py:533
  34.4 3.8 %collective-permute-start.3 = (bf16[128,1536]{1,0:T(8,128)(2,1)}, bf16[128,1536]{1,0:T(8,128)(2,1)S(1)}, u32[]{:S(2)}, u32[]{:S(2)}) collective-permute-start(bf16[128,1536]{1,0:T(8,128)(2,1)} %collective-permute-done.refs_1_), channel_id=1, source_target_pairs={{2,0},{4,2},{6,4},{0,6},{3,1},{5,3},{7,5},{1,7},{10,8},{12,10},{14... | collective-permute-start | bytes 1179656 | tf_op jit(solution)/shard_map/ppermute | solution.py:519
  38.2 2.1 %make_probes.1 = (bf16[1024,640]{1,0:T(8,128)(2,1)S(1)}, bf16[1024,640]{1,0:T(8,128)(2,1)S(1)}, bf16[1024,640]{1,0:T(8,128)(2,1)S(1)}) custom-call(bf16[8,512,128]{2,1,0:T(8,128)(2,1)S(1)} %copy-done.1, bf16[128,1536]{1,0:T(8,128)(2,1)S(1)} %copy-done.9, bf16[128,1536]{1,0:T(8,128)(2,1)} %collective-permute-done.refs_1_, bf16[128,1536]{1,0:T(8,128)(2,1)S(1)} %copy-done.11), custom_call_target="tpu_custom_call" | custom-call | tf_op jit(solution)/shard_map/make_probes/pallas_call | solution.py:290
  40.3 6.3 %attend_1.1 = (bf16[128,1152]{1,0:T(8,128)(2,1)S(1)}, bf16[768,640]{1,0:T(8,128)(2,1)S(1)}) custom-call(s32[4]{0:T(128)S(1)} %copy-done.13, bf16[8,512,128]{2,1,0:T(8,128)(2,1)S(1)} %copy-done, bf16[768,640]{1,0:T(8,128)(2,1)S(1)} %build_keys.1.near, bf16[768,640]{1,0:T(8,128)(2,1)S(1)} %collective-permute-done.2.arrived, ...), custom_call_target="tpu_custom_call" | custom-call | tf_op jit(solution)/shard_map/attend_1/pallas_call | solution.py:393
  47.3 6.3 %attend_2.1 = bf16[128,1152]{1,0:T(8,128)(2,1)S(1)} custom-call(s32[4]{0:T(128)S(1)} %copy-done.13, bf16[8,512,128]{2,1,0:T(8,128)(2,1)S(1)} %copy-done, bf16[768,640]{1,0:T(8,128)(2,1)S(1)} %build_keys.1.near, bf16[768,640]{1,0:T(8,128)(2,1)S(1)} %get-tuple-element.41.arrived, bf16[128,640]{1,0:T(8,128)(2,1)S(1)} %get-tuple-element.37.span, ...), custom_call_target="tpu_custom_call" | custom-call | tf_op jit(solution)/shard_map/attend_2/pallas_call | solution.py:393
  53.6 3.2 %collective-permute-done.4.one = bf16[128,1152]{1,0:T(8,128)(2,1)S(1)} collective-permute-done((bf16[128,1152]{1,0:T(8,128)(2,1)S(1)}, bf16[128,1152]{1,0:T(8,128)(2,1)S(1)}, u32[]{:S(2)}, u32[]{:S(2)}) %collective-permute-start.4) | collective-permute-done | bytes 294944 | tf_op jit(solution)/shard_map/ppermute | solution.py:519
  56.8 6.3 %attend_3.1 = bf16[128,1152]{1,0:T(8,128)(2,1)S(1)} custom-call(s32[4]{0:T(128)S(1)} %copy-done.13, bf16[8,512,128]{2,1,0:T(8,128)(2,1)S(1)} %copy-done, bf16[768,640]{1,0:T(8,128)(2,1)S(1)} %build_keys.1.near, bf16[768,640]{1,0:T(8,128)(2,1)S(1)} %get-tuple-element.41.arrived, bf16[128,640]{1,0:T(8,128)(2,1)S(1)} %get-tuple-element.37.span, ...), custom_call_target="tpu_custom_call" | custom-call | tf_op jit(solution)/shard_map/attend_3/pallas_call | solution.py:393
  63.1 2.0 %collective-permute-done.5 = bf16[128,1152]{1,0:T(8,128)(2,1)S(1)} collective-permute-done((bf16[128,1152]{1,0:T(8,128)(2,1)S(1)}, bf16[128,1152]{1,0:T(8,128)(2,1)S(1)}, u32[]{:S(2)}, u32[]{:S(2)}) %collective-permute-start.5) | collective-permute-done | bytes 294944 | tf_op jit(solution)/shard_map/ppermute | solution.py:519
  65.1 2.7 %collective-permute-start.7 = (bf16[128,1152]{1,0:T(8,128)(2,1)S(1)}, bf16[128,1152]{1,0:T(8,128)(2,1)S(1)}, u32[]{:S(2)}, u32[]{:S(2)}) collective-permute-start(bf16[128,1152]{1,0:T(8,128)(2,1)S(1)} %attend_3.1), channel_id=1, source_target_pairs={{2,0},{4,2},{6,4},{0,6},{3,1},{5,3},{7,5},{1,7},{10,8},{12,10},{14... | collective-permute-start | bytes 884744 | tf_op jit(solution)/shard_map/ppermute | solution.py:519
  67.8 6.3 %attend_0.1.own = bf16[128,1152]{1,0:T(8,128)(2,1)S(1)} custom-call(s32[4]{0:T(128)S(1)} %copy-done.13, bf16[8,512,128]{2,1,0:T(8,128)(2,1)S(1)} %copy-done, bf16[768,640]{1,0:T(8,128)(2,1)S(1)} %build_keys.1.near, bf16[768,640]{1,0:T(8,128)(2,1)S(1)} %get-tuple-element.41.arrived, bf16[128,640]{1,0:T(8,128)(2,1)S(1)} %get-tuple-element.37.span, ...), custom_call_target="tpu_custom_call" | custom-call | tf_op jit(solution)/shard_map/attend_0/pallas_call | solution.py:393
  74.1 1.5 %project_output.1 = (f32[128,2048]{1,0:T(8,128)S(1)}, bf16[128,2048]{1,0:T(8,128)(2,1)S(1)}) custom-call(bf16[128,1152]{1,0:T(8,128)(2,1)S(1)} %attend_0.1.own, bf16[128,1152]{1,0:T(8,128)(2,1)S(1)} %collective-permute-done.4.one, bf16[128,1152]{1,0:T(8,128)(2,1)S(1)} %collective-permute-done.6.two, bf16[128,1152]{1,0:T(8,128)(2,1)S(1)} %collective-permute-done.7.three, ...), custom_call_target="tpu_custom_call" | custom-call | tf_op jit(solution)/shard_map/project_output/pallas_call | solution.py:437
  75.7 3.0 %collective-permute-start.8 = (bf16[128,2048]{1,0:T(8,128)(2,1)S(1)}, bf16[128,2048]{1,0:T(8,128)(2,1)S(1)}, u32[]{:S(2)}, u32[]{:S(2)}) collective-permute-start(bf16[128,2048]{1,0:T(8,128)(2,1)S(1)} %get-tuple-element.54), channel_id=1, source_target_pairs={{0,1},{1,0},{2,3},{3,2},{4,5},{5,4},{6,7},{7,6},{8,9},{9,8},{10,11... | collective-permute-start | bytes 1572872 | tf_op jit(solution)/shard_map/ppermute | solution.py:552
  78.7 1.5 %collective-permute-done.8.other = bf16[128,2048]{1,0:T(8,128)(2,1)S(1)} collective-permute-done((bf16[128,2048]{1,0:T(8,128)(2,1)S(1)}, bf16[128,2048]{1,0:T(8,128)(2,1)S(1)}, u32[]{:S(2)}, u32[]{:S(2)}) %collective-permute-start.8) | collective-permute-done | bytes 524320 | tf_op jit(solution)/shard_map/ppermute | solution.py:552
  80.2 3.1 %expert.1 = (f32[128,1024]{1,0:T(8,128)S(1)}, bf16[128,1024]{1,0:T(8,128)(2,1)S(1)}) custom-call(s32[4]{0:T(128)S(1)} %copy-done.13, bf16[128,2048]{1,0:T(8,128)(2,1)S(1)} %copy-done.7, f32[128,2048]{1,0:T(8,128)S(1)} %get-tuple-element.53.exact, bf16[128,2048]{1,0:T(8,128)(2,1)S(1)} %collective-permute-done.8.other, bf16[2048]{0:T(1024)(128)(2,1)S(1)} %copy-done.15, ...), custom_call_target="tpu_custom_call" | custom-call | tf_op jit(solution)/shard_map/expert/pallas_call | solution.py:468
  83.8 1.2 %collective-permute-done.9 = bf16[128,1024]{1,0:T(8,128)(2,1)S(1)} collective-permute-done((bf16[128,1024]{1,0:T(8,128)(2,1)S(1)}, bf16[128,1024]{1,0:T(8,128)(2,1)S(1)}, u32[]{:S(2)}, u32[]{:S(2)}) %collective-permute-start.9) | collective-permute-done | bytes 262176 | tf_op jit(solution)/shard_map/ppermute | solution.py:563
  (47 shorter events, 5.1 us)
Async XLA Ops:
  5.6 26.1 %all-to-all-start = ((bf16[16,2,16,1152]{3,2,1,0:T(8,128)(2,1)}), bf16[16,2,16,1152]{3,2,1,0:T(8,128)(2,1)S(1)}, u32[]{:S(2)}, u32[]{:S(2)}) async-start(bf16[16,2,16,1152]{3,2,1,0:T(8,128)(2,1)} %bitcast.18), calls=%async_computation | async-start | bytes 2359296 | tf_op jit(solution)/shard_map/all_to_all | solution.py:514
  13.2 9.1 %copy-start.17 = (bf16[512]{0:T(512)(128)(2,1)S(1)}, bf16[512]{0:T(512)(128)(2,1)}, u32[]{:S(2)}) copy-start(bf16[512]{0:T(512)(128)(2,1)} %kv_gain.1) | copy-start | bytes 3076
  13.2 18.5 %copy-start.14 = (s32[16,24,1]{1,2,0:T(1,128)S(1)}, s32[16,24,1]{1,2,0:T(1,128)}, u32[]{:S(2)}) copy-start(s32[16,24,1]{1,2,0:T(1,128)} %param.30) | copy-start | bytes 4612
  18.3 13.4 %copy-start.13 = (s32[4]{0:T(128)S(1)}, s32[4]{0:T(128)}, u32[]{:S(2)}) copy-start(s32[4]{0:T(128)} %pad_add_fusion.place) | copy-start | bytes 52
  18.3 13.4 %copy-start.16 = (s32[16]{0:T(128)S(1)}, s32[16]{0:T(128)}, u32[]{:S(2)}) copy-start(s32[16]{0:T(128)} %count.3) | copy-start | bytes 196
  18.4 12.6 %collective-permute-start.1 = (bf16[128,1536]{1,0:T(8,128)(2,1)}, bf16[128,1536]{1,0:T(8,128)(2,1)S(1)}, u32[]{:S(2)}, u32[]{:S(2)}) collective-permute-start(bf16[128,1536]{1,0:T(8,128)(2,1)} %get-tuple-element.32.refs_0_), channel_id=1, source_target_pairs={{6,0},{0,2},{2,4},{4,6},{7,1},{1,3},{3,5},{5,7},{14,8},{8,10},{10,... | collective-permute-start | bytes 1179656 | tf_op jit(solution)/shard_map/ppermute | solution.py:519
  20.1 11.6 %collective-permute-start = (bf16[128,1536]{1,0:T(8,128)(2,1)}, bf16[128,1536]{1,0:T(8,128)(2,1)}, u32[]{:S(2)}, u32[]{:S(2)}) collective-permute-start(bf16[128,1536]{1,0:T(8,128)(2,1)} %get-tuple-element.32.refs_0_), channel_id=1, source_target_pairs={{2,0},{4,2},{6,4},{0,6},{3,1},{5,3},{7,5},{1,7},{10,8},{12,10},{14... | collective-permute-start | bytes 1179656 | tf_op jit(solution)/shard_map/ppermute | solution.py:519
  25.8 12.4 %copy-start.1 = (bf16[8,512,128]{2,1,0:T(8,128)(2,1)S(1)}, bf16[8,512,128]{2,1,0:T(8,128)(2,1)}, u32[]{:S(2)}) copy-start(bf16[8,512,128]{2,1,0:T(8,128)(2,1)} %refs_1_.1) | copy-start | bytes 3145732
  27.8 12.5 %copy-start = (bf16[8,512,128]{2,1,0:T(8,128)(2,1)S(1)}, bf16[8,512,128]{2,1,0:T(8,128)(2,1)}, u32[]{:S(2)}) copy-start(bf16[8,512,128]{2,1,0:T(8,128)(2,1)} %value_up.7) | copy-start | bytes 3145732
  31.7 6.5 %copy-start.9 = (bf16[128,1536]{1,0:T(8,128)(2,1)S(1)}, bf16[128,1536]{1,0:T(8,128)(2,1)}, u32[]{:S(2)}) copy-start(bf16[128,1536]{1,0:T(8,128)(2,1)} %get-tuple-element.32.refs_0_) | copy-start | bytes 1179652
  31.7 6.5 %copy-start.11 = (bf16[128,1536]{1,0:T(8,128)(2,1)S(1)}, bf16[128,1536]{1,0:T(8,128)(2,1)}, u32[]{:S(2)}) copy-start(bf16[128,1536]{1,0:T(8,128)(2,1)} %copy-done.10) | copy-start | bytes 1179652
  32.6 7.7 %collective-permute-start.2 = (bf16[768,640]{1,0:T(8,128)(2,1)S(1)}, bf16[768,640]{1,0:T(8,128)(2,1)S(1)}, u32[]{:S(2)}, u32[]{:S(2)}) collective-permute-start(bf16[768,640]{1,0:T(8,128)(2,1)S(1)} %build_keys.1.near), channel_id=1, source_target_pairs={{0,1},{1,0},{2,3},{3,2},{4,5},{5,4},{6,7},{7,6},{8,9},{9,8},{10,11... | collective-permute-start | bytes 2949128 | tf_op jit(solution)/shard_map/ppermute | solution.py:533
  34.4 12.6 %collective-permute-start.3 = (bf16[128,1536]{1,0:T(8,128)(2,1)}, bf16[128,1536]{1,0:T(8,128)(2,1)S(1)}, u32[]{:S(2)}, u32[]{:S(2)}) collective-permute-start(bf16[128,1536]{1,0:T(8,128)(2,1)} %collective-permute-done.refs_1_), channel_id=1, source_target_pairs={{2,0},{4,2},{6,4},{0,6},{3,1},{5,3},{7,5},{1,7},{10,8},{12,10},{14... | collective-permute-start | bytes 1179656 | tf_op jit(solution)/shard_map/ppermute | solution.py:519
  47.0 9.8 %collective-permute-start.4 = (bf16[128,1152]{1,0:T(8,128)(2,1)S(1)}, bf16[128,1152]{1,0:T(8,128)(2,1)S(1)}, u32[]{:S(2)}, u32[]{:S(2)}) collective-permute-start(bf16[128,1152]{1,0:T(8,128)(2,1)S(1)} %get-tuple-element.45), channel_id=1, source_target_pairs={{6,0},{0,2},{2,4},{4,6},{7,1},{1,3},{3,5},{5,7},{14,8},{8,10},{10,... | collective-permute-start | bytes 884744 | tf_op jit(solution)/shard_map/ppermute | solution.py:519
  56.8 8.3 %collective-permute-start.5 = (bf16[128,1152]{1,0:T(8,128)(2,1)S(1)}, bf16[128,1152]{1,0:T(8,128)(2,1)S(1)}, u32[]{:S(2)}, u32[]{:S(2)}) collective-permute-start(bf16[128,1152]{1,0:T(8,128)(2,1)S(1)} %attend_2.1), channel_id=1, source_target_pairs={{6,0},{0,2},{2,4},{4,6},{7,1},{1,3},{3,5},{5,7},{14,8},{8,10},{10,... | collective-permute-start | bytes 884744 | tf_op jit(solution)/shard_map/ppermute | solution.py:519
  56.8 23.4 %copy-start.5 = (bf16[704,2048]{1,0:T(8,128)(2,1)S(1)}, bf16[704,2048]{1,0:T(8,128)(2,1)}, u32[]{:S(2)}) copy-start(bf16[704,2048]{1,0:T(8,128)(2,1)} %w_down.1) | copy-start | bytes 8650756
  56.8 23.4 %copy-start.7 = (bf16[128,2048]{1,0:T(8,128)(2,1)S(1)}, bf16[128,2048]{1,0:T(8,128)(2,1)}, u32[]{:S(2)}) copy-start(bf16[128,2048]{1,0:T(8,128)(2,1)} %tokens.1) | copy-start | bytes 1572868
  65.1 9.0 %copy-start.2 = (bf16[1024,2048]{1,0:T(8,128)(2,1)S(1)}, bf16[1024,2048]{1,0:T(8,128)(2,1)}, u32[]{:S(2)}) copy-start(bf16[1024,2048]{1,0:T(8,128)(2,1)} %weight.1) | copy-start | bytes 12582916
  65.1 9.0 %collective-permute-start.6 = (bf16[128,1152]{1,0:T(8,128)(2,1)S(1)}, bf16[128,1152]{1,0:T(8,128)(2,1)S(1)}, u32[]{:S(2)}, u32[]{:S(2)}) collective-permute-start(bf16[128,1152]{1,0:T(8,128)(2,1)S(1)} %collective-permute-done.5), channel_id=1, source_target_pairs={{6,0},{0,2},{2,4},{4,6},{7,1},{1,3},{3,5},{5,7},{14,8},{8,10},{10,... | collective-permute-start | bytes 884744 | tf_op jit(solution)/shard_map/ppermute | solution.py:519
  65.1 9.0 %collective-permute-start.7 = (bf16[128,1152]{1,0:T(8,128)(2,1)S(1)}, bf16[128,1152]{1,0:T(8,128)(2,1)S(1)}, u32[]{:S(2)}, u32[]{:S(2)}) collective-permute-start(bf16[128,1152]{1,0:T(8,128)(2,1)S(1)} %attend_3.1), channel_id=1, source_target_pairs={{2,0},{4,2},{6,4},{0,6},{3,1},{5,3},{7,5},{1,7},{10,8},{12,10},{14... | collective-permute-start | bytes 884744 | tf_op jit(solution)/shard_map/ppermute | solution.py:519
  67.8 12.4 %copy-start.4 = (bf16[2048,704]{0,1:T(8,128)(2,1)S(1)}, bf16[2048,704]{0,1:T(8,128)(2,1)}, u32[]{:S(2)}) copy-start(bf16[2048,704]{0,1:T(8,128)(2,1)} %param.27) | copy-start | bytes 8650756
  74.0 6.2 %copy-start.3 = (bf16[2048,704]{0,1:T(8,128)(2,1)S(1)}, bf16[2048,704]{0,1:T(8,128)(2,1)}, u32[]{:S(2)}) copy-start(bf16[2048,704]{0,1:T(8,128)(2,1)} %param.26) | copy-start | bytes 8650756
  75.7 4.5 %collective-permute-start.8 = (bf16[128,2048]{1,0:T(8,128)(2,1)S(1)}, bf16[128,2048]{1,0:T(8,128)(2,1)S(1)}, u32[]{:S(2)}, u32[]{:S(2)}) collective-permute-start(bf16[128,2048]{1,0:T(8,128)(2,1)S(1)} %get-tuple-element.54), channel_id=1, source_target_pairs={{0,1},{1,0},{2,3},{3,2},{4,5},{5,4},{6,7},{7,6},{8,9},{9,8},{10,11... | collective-permute-start | bytes 1572872 | tf_op jit(solution)/shard_map/ppermute | solution.py:552
  83.4 1.6 %collective-permute-start.9 = (bf16[128,1024]{1,0:T(8,128)(2,1)S(1)}, bf16[128,1024]{1,0:T(8,128)(2,1)S(1)}, u32[]{:S(2)}, u32[]{:S(2)}) collective-permute-start(bf16[128,1024]{1,0:T(8,128)(2,1)S(1)} %get-tuple-element.56), channel_id=1, source_target_pairs={{0,1},{1,0},{2,3},{3,2},{4,5},{5,4},{6,7},{7,6},{8,9},{9,8},{10,11... | collective-permute-start | bytes 786440 | tf_op jit(solution)/shard_map/ppermute | solution.py:563
  (5 other events, 10.4 us)

commit v5 on v4

--- a/solution.py
+++ b/solution.py
@@ -56,79 +56,92 @@
     return values * cosine + partner * sine
 
 
-def pack_kernel(
-    place, owner_src, slot_src, pool_src, out, owner, slot, pool, sems
-):
+def pack_kernel(owner_src, slot_src, pool_src, out, owner, slot, pool, message, sems):
+    group = lax.axis_index("store")
+    shard = lax.axis_index("section") * lax.axis_size("tp") + lax.axis_index("tp")
     n_pages, width, window = pool.shape
-    n_store, rows, _ = out.shape
+    n_store, rows, _ = message.shape
     per = window // rows
     pairs = [(owner_src, owner), (slot_src, slot)]
-    part = pl.ds(pl.multiple_of((place[1] // per) * window, window), window)
-    strip = n_pages // 4
-    for k in range(4):
-        at = pl.ds(k * strip, strip)
+    part = pl.ds(pl.multiple_of((shard // per) * window, window), window)
+    for k in range(n_pages // 2):
+        at = pl.ds(2 * k, 2)
         pairs.append((pool_src.at[at, :, part], pool.at[at]))
     copies = [
         pltpu.make_async_copy(src, dst, sems.at[i]) for i, (src, dst) in enumerate(pairs)
     ]
     for copy in copies:
         copy.start()
-    for copy in copies:
-        copy.wait()
-    first = (place[1] % per) * rows
+    copies[0].wait()
+    copies[1].wait()
+    n_list = owner.shape[1]
+    held = owner[...] == group
+    entry = lax.broadcasted_iota(jnp.int32, held.shape, 1)
+    low = jnp.min(jnp.where(held, entry, n_list), axis=1, keepdims=True)
+    high = jnp.max(jnp.where(held, entry, -1), axis=1, keepdims=True)
+    at_once = n_store // 2
+    row = lax.broadcasted_iota(jnp.int32, (rows, 1), 0)
+    column = lax.broadcasted_iota(jnp.int32, (at_once * rows, n_pages * rows), 1)
+    chosen = {}
+    for which, hit in enumerate((low, high)):
+        page = jnp.sum(jnp.where(entry == hit, slot[...], 0), axis=1, keepdims=True) * rows
+        for to in range(0, n_store, at_once):
+            wanted = [
+                jnp.broadcast_to(page[g : g + 1], (rows, 1)) + row for g in range(to, to + at_once)
+            ]
+            wanted = jnp.concatenate(wanted, axis=0)
+            chosen[to, which] = jnp.where(column == wanted, 1.0, 0.0).astype(BF16)
+    first = (shard % per) * rows
     lane = lax.broadcasted_iota(jnp.int32, (width, window), 1)
     joined = []
     for at in range(0, n_pages, per):
         part = None
         for k in range(per):
+            if k % 2 == 0:
+                copies[2 + (at + k) // 2].wait()
             moved = pltpu.roll(pool[at + k].astype(F32), (k * rows - first + window) % window, axis=1)
             part = moved if part is None else jnp.where(lane >= k * rows, moved, part)
         joined.append(part.astype(BF16))
     stage = jnp.concatenate(joined, axis=1)
-    total = n_store * rows
-    n_list = owner.shape[1]
-    held = owner[...] == place[0]
-    entry = lax.broadcasted_iota(jnp.int32, held.shape, 1)
-    low = jnp.min(jnp.where(held, entry, n_list), axis=1, keepdims=True)
-    high = jnp.max(jnp.where(held, entry, -1), axis=1, keepdims=True)
-    row = lax.broadcasted_iota(jnp.int32, (rows, 1), 0)
-    column = lax.broadcasted_iota(jnp.int32, (total, n_pages * rows), 1)
-    taken = []
-    for which in (low, high):
-        page = jnp.sum(jnp.where(entry == which, slot[...], 0), axis=1, keepdims=True) * rows
-        wanted = [jnp.broadcast_to(page[g : g + 1], (rows, 1)) + row for g in range(n_store)]
-        wanted = jnp.concatenate(wanted, axis=0)
-        choose = jnp.where(column == wanted, 1.0, 0.0).astype(BF16)
-        taken.append(dot_nt(choose, stage))
-    ropes = jnp.concatenate([part[:, KVR:] for part in taken], axis=1)
-    for which, part in enumerate(taken):
-        out[:, :, which * KVR : (which + 1) * KVR] = (
-            part[:, :KVR].astype(BF16).reshape(n_store, rows, KVR)
-        )
-    out[:, :, 2 * KVR :] = ropes.astype(BF16).reshape(n_store, rows, 2 * ROPE)
-
-
-def pack_pages(place, owner, slot, pool_t, rows):
-    n_store = owner.shape[0]
+    sends = []
+    for to in range(0, n_store, at_once):
+        at = pl.ds(to, at_once)
+        taken = [dot_nt(chosen[to, which], stage) for which in range(2)]
+        ropes = jnp.concatenate([part[:, KVR:] for part in taken], axis=1)
+        for which, part in enumerate(taken):
+            message[at, :, which * KVR : (which + 1) * KVR] = (
+                part[:, :KVR].astype(BF16).reshape(at_once, rows, KVR)
+            )
+        message[at, :, 2 * KVR :] = ropes.astype(BF16).reshape(at_once, rows, 2 * ROPE)
+        send = pltpu.make_async_copy(message.at[at], out.at[at], sems.at[len(copies) + len(sends)])
+        send.start()
+        sends.append(send)
+    for send in sends:
+        send.wait()
+
+
+def pack_pages(owner, slot, pool_t, rows):
+    n_store, n_pages = owner.shape[0], pool_t.shape[0]
     return pl.pallas_call(
         pack_kernel,
         out_shape=jax.ShapeDtypeStruct((n_store, rows, MSG), BF16),
-        in_specs=[SMEM] + [HBM] * 3,
-        out_specs=VMEM,
+        in_specs=[HBM] * 3,
+        out_specs=HBM,
         scratch_shapes=[
             pltpu.VMEM(owner.shape, jnp.int32),
             pltpu.VMEM(slot.shape, jnp.int32),
             pltpu.VMEM((*pool_t.shape[:2], 128), BF16),
-            pltpu.SemaphoreType.DMA((6,)),
+            pltpu.VMEM((n_store, rows, MSG), BF16),
+            pltpu.SemaphoreType.DMA((4 + n_pages // 2,)),
         ],
         compiler_params=params(60),
         name="pack_pages",
-    )(place, owner, slot, pool_t)
-
-
-def keys_kernel(place, owner, count, pages, out, seen):
+    )(owner, slot, pool_t)
+
+
+def keys_kernel(owner, count, pages, out, seen):
     rows = pages.shape[1]
-    group = place[0]
+    group = lax.axis_index("store")
     lane = lax.broadcasted_iota(jnp.int32, (rows, 128), 1)
     for k in range(pages.shape[0]):
         seen[k] = 0
@@ -146,17 +159,17 @@
         out[at, KVR:] = jnp.where(lane < ROPE, rot, last).astype(BF16)
 
 
-def build_keys(place, owner, count, pages):
+def build_keys(owner, count, pages):
     n_keys = owner.shape[1] * pages.shape[1]
     return pl.pallas_call(
         keys_kernel,
         out_shape=jax.ShapeDtypeStruct((n_keys, WIDE), BF16),
-        in_specs=[SMEM, SMEM, SMEM, VMEM],
+        in_specs=[SMEM, SMEM, VMEM],
         out_specs=VMEM,
         scratch_shapes=[pltpu.SMEM((pages.shape[0],), jnp.int32)],
         compiler_params=params(24),
         name="build_keys",
-    )(place, owner, count, pages)
+    )(owner, count, pages)
 
 
 def rotation_table(n_rows):
@@ -169,10 +182,11 @@
 
 
 def project_kernel(
-    place, count, tokens_src, gain, table, w_query_src, query, normed, turns, tokens, w_query, total, sems
+    count, tokens_src, gain, table, w_query_src, query, normed, turns, tokens, w_query, total, sems
 ):
     rows = tokens.shape[0]
-    start = pl.multiple_of(count[place[0]] * PAGE + place[2] * rows, rows)
+    group, section = lax.axis_index("store"), lax.axis_index("section")
+    start = pl.multiple_of(count[group] * PAGE + section * rows, rows)
     pairs = [(tokens_src, tokens), (table.at[pl.ds(start, rows), :], turns)]
     pieces = 8
     depth = w_query.shape[0] // pieces
@@ -205,7 +219,7 @@
         query[:, at + 2 * NOPE : at + 2 * head] = (turn(pair, cosine, sine) * SCALE).astype(BF16)
 
 
-def project(place, count, tokens, gain, table, w_query):
+def project(count, tokens, gain, table, w_query):
     rows, width = tokens.shape
     cols = w_query.shape[1]
     return pl.pallas_call(
@@ -215,7 +229,7 @@
             jax.ShapeDtypeStruct(tokens.shape, BF16),
             jax.ShapeDtypeStruct((rows, 2 * ROPE), F32),
         ],
-        in_specs=[SMEM] * 2 + [HBM, VMEM] + [HBM] * 2,
+        in_specs=[SMEM, HBM, VMEM] + [HBM] * 2,
         out_specs=[VMEM] * 3,
         scratch_shapes=[
             pltpu.VMEM(tokens.shape, BF16),
@@ -225,7 +239,7 @@
         ],
         compiler_params=params(60),
         name="project",
-    )(place, count, tokens, gain, table, w_query)
+    )(count, tokens, gain, table, w_query)
 
 
 def latent_kernel(normed, turns, w_latent_t, kv_gain, new_latent, span):
@@ -279,28 +293,34 @@
         probes[at, KVR:] = jnp.where(rope_lanes < ROPE, pair, one).astype(BF16)
 
 
-def probes_kernel(key_up, *refs):
-    count = len(refs) // 2
-    for query, probes in zip(refs[:count], refs[count:]):
+def probes_kernel(key_up, own, ahead, behind, own_probes, ahead_probes, behind_probes, low, high):
+    cut = low.shape[0]
+    low[...] = ahead[:cut, :]
+    high[...] = behind[cut:, :]
+    for query, probes in ((own, own_probes), (ahead, ahead_probes), (behind, behind_probes)):
         fill_probes(query, key_up, probes)
 
 
-def make_probes(key_up, *queries):
-    rows = queries[0].shape[0]
+def make_probes(key_up, own, ahead, behind):
+    rows, width = own.shape
+    probes = jax.ShapeDtypeStruct((key_up.shape[0] * rows, WIDE), BF16)
+    half = jax.ShapeDtypeStruct((rows // 2, width), BF16)
     return pl.pallas_call(
         probes_kernel,
-        out_shape=[jax.ShapeDtypeStruct((key_up.shape[0] * rows, WIDE), BF16)] * len(queries),
-        in_specs=[VMEM] * (1 + len(queries)),
-        out_specs=[VMEM] * len(queries),
+        out_shape=[probes] * 3 + [half] * 2,
+        in_specs=[VMEM] * 4,
+        out_specs=[VMEM] * 5,
         compiler_params=params(16),
         name="make_probes",
-    )(key_up, *queries)
-
-
-def attend_kernel(by, n_section, keep_far, place, value_up, near, arrived, span, *refs):
+    )(key_up, own, ahead, behind)
+
+
+def attend_kernel(by, keep_far, value_up, near, arrived, span, *refs):
     far = arrived
     if by == 2:
-        query, key_up, out, probes = refs
+        low, high, key_up, out, query, probes = refs
+        query[: low.shape[0], :] = low[...]
+        query[low.shape[0] :, :] = high[...]
         fill_probes(query, key_up, probes)
     elif keep_far:
         probes, out, far = refs
@@ -310,7 +330,7 @@
     n_head, rows = value_up.shape[0], out.shape[0]
     blocks = (near, far, span)
     lane = lax.broadcasted_iota(jnp.int32, (rows, 128), 1)
-    at_once = 4
+    at_once = 2
     tile = at_once * rows
     steps = n_head // at_once
     width = n_head * NOPE
@@ -320,7 +340,8 @@
         key_of = lax.broadcasted_iota(jnp.int32, (tile, rows), 1)
         hide = jnp.where(key_of <= row_of, 0.0, MASKED_SCORE)
     else:
-        hide = jnp.where(place[2] + by < n_section, 0.0, MASKED_SCORE)
+        later = lax.axis_index("section") + by < lax.axis_size("section")
+        hide = jnp.where(later, 0.0, MASKED_SCORE)
 
     pieces, closing = [], []
     for block in blocks:
@@ -333,25 +354,11 @@
         return [value[:, at : at + 128] for at in range(0, value.shape[1], 128)]
 
     def score(i, p, peak):
-        block, at, step = pieces[p]
-        value = dot_nt(probes[i * tile : (i + 1) * tile, :], block[at : at + step, :])
+        block, at, size = pieces[p]
+        value = dot_nt(probes[i * tile : (i + 1) * tile, :], block[at : at + size, :])
         if block is span:
             value = value + hide
         return value, functools.reduce(jnp.maximum, lanes(value), peak)
-
-    def finish(i, total, summed, stats, top):
-        total = jnp.sum(total, axis=1, keepdims=True)
-        mixed = (summed * (1.0 / total)).astype(BF16)
-        level = top + jnp.log2(total)
-        for k in range(0, at_once, 2):
-            h = i * at_once + k
-            maps = jnp.concatenate([value_up[h], value_up[h + 1]], axis=1)
-            value = dot(mixed[k * rows : (k + 2) * rows], maps).astype(BF16)
-            out[:, h * VDIM : (h + 1) * VDIM] = value[:rows, :VDIM]
-            out[:, (h + 1) * VDIM : (h + 2) * VDIM] = value[rows:, VDIM:]
-        for k in range(at_once):
-            stats = jnp.where(lane == i * at_once + k, level[k * rows : (k + 1) * rows], stats)
-        return stats
 
     stats = jnp.zeros((rows, 128), F32)
     lowest = jnp.full((tile, 128), MASKED_SCORE, F32)
@@ -375,8 +382,17 @@
             if closing[p]:
                 summed = summed + dot(jnp.concatenate(weights, axis=1), pieces[p][0][:, :KVR])
                 weights = []
-        stats = finish(i, total, summed, stats, top)
         ready = coming
+        total = jnp.sum(total, axis=1, keepdims=True)
+        mixed = (summed * (1.0 / total)).astype(BF16)
+        level = top + jnp.log2(total)
+        h = i * at_once
+        maps = jnp.concatenate([value_up[h], value_up[h + 1]], axis=1)
+        value = dot(mixed, maps).astype(BF16)
+        out[:, h * VDIM : (h + 1) * VDIM] = value[:rows, :VDIM]
+        out[:, (h + 1) * VDIM : (h + 2) * VDIM] = value[rows:, VDIM:]
+        for k in range(at_once):
+            stats = jnp.where(lane == h + k, level[k * rows : (k + 1) * rows], stats)
     high = stats.astype(BF16).astype(F32)
     rest = stats - high
     mid = rest.astype(BF16).astype(F32)
@@ -384,21 +400,24 @@
     out[:, width:] = joined.astype(BF16)
 
 
-def attend(by, n_section, place, value_up, near, far, span, *queries, keep_far=False):
+def attend(by, value_up, near, far, span, *queries, keep_far=False):
     rows, n_head = span.shape[0], value_up.shape[0]
     out_shape = [jax.ShapeDtypeStruct((rows, n_head * VDIM + 128), BF16)]
     if keep_far:
         out_shape.append(jax.ShapeDtypeStruct(far.shape, BF16))
-    scratch = [pltpu.VMEM((n_head * rows, WIDE), BF16)] if by == 2 else []
-    return pl.pallas_call(
-        functools.partial(attend_kernel, by, n_section, keep_far),
+    scratch = []
+    if by == 2:
+        scratch.append(pltpu.VMEM((rows, queries[0].shape[1]), BF16))
+        scratch.append(pltpu.VMEM((n_head * rows, WIDE), BF16))
+    return pl.pallas_call(
+        functools.partial(attend_kernel, by, keep_far),
         out_shape=out_shape,
-        in_specs=[SMEM] + [VMEM] * (4 + len(queries)),
+        in_specs=[VMEM] * (4 + len(queries)),
         out_specs=[VMEM] * len(out_shape),
         scratch_shapes=scratch,
         compiler_params=params(32),
         name="attend_%d" % by,
-    )(place, value_up, near, far, span, *queries)
+    )(value_up, near, far, span, *queries)
 
 
 def output_kernel(n_head, own, one, two, three, weight, exact, send):
@@ -447,7 +466,7 @@
     )(own, one, two, three, w_out)
 
 
-def expert_kernel(place, tokens, exact, other, gain, w_gate_t, w_up_t, w_down, keep, send):
+def expert_kernel(tokens, exact, other, gain, w_gate_t, w_up_t, w_down, keep, send):
     half = keep.shape[1]
     middle = tokens[...].astype(F32) + (exact[...] + other[...].astype(F32))
     middle = middle.astype(BF16).astype(F32)
@@ -457,12 +476,12 @@
     hidden = (gate / (1.0 + jnp.exp(-gate)) * up).astype(BF16)
     low = dot(hidden, w_down[:, :half])
     high = dot(hidden, w_down[:, half:])
-    first = place[3] == 0
+    first = lax.axis_index("tp") == 0
     keep[...] = jnp.where(first, middle[:, :half] + low, middle[:, half:] + high)
     send[...] = jnp.where(first, high, low).astype(BF16)
 
 
-def expert(place, tokens, exact, other, gain, w_gate_t, w_up_t, w_down):
+def expert(tokens, exact, other, gain, w_gate_t, w_up_t, w_down):
     rows, width = tokens.shape
     half = width // 2
     return pl.pallas_call(
@@ -471,11 +490,11 @@
             jax.ShapeDtypeStruct((rows, half), F32),
             jax.ShapeDtypeStruct((rows, half), BF16),
         ],
-        in_specs=[SMEM] + [VMEM] * 7,
+        in_specs=[VMEM] * 7,
         out_specs=[VMEM] * 2,
         compiler_params=params(24),
         name="expert",
-    )(place, tokens, exact, other, gain, w_gate_t, w_up_t, w_down)
+    )(tokens, exact, other, gain, w_gate_t, w_up_t, w_down)
 
 
 def on_device(
@@ -499,16 +518,12 @@
     n_store = lax.axis_size("store")
     n_section = lax.axis_size("section")
     n_tp = lax.axis_size("tp")
-    group = lax.axis_index("store")
-    section = lax.axis_index("section")
-    core = lax.axis_index("tp")
     rows = tokens.shape[0]
     share = PAGE // (n_section * n_tp)
 
     swap = [(0, 1), (1, 0)]
-    place = jnp.stack([group, section * n_tp + core, section, core]).astype(jnp.int32)
     owner = hit_owner[:, :, 0]
-    outgoing = pack_pages(place, owner, hit_slot, jnp.swapaxes(page_pool, 1, 2), share)
+    outgoing = pack_pages(owner, hit_slot, jnp.swapaxes(page_pool, 1, 2), share)
     outgoing, early_tokens = lax.optimization_barrier((outgoing, tokens))
     outgoing = outgoing.reshape(n_store, 2, share // 2, MSG)
     arrived = lax.all_to_all(outgoing, "store", split_axis=0, concat_axis=0, tiled=True)
@@ -520,27 +535,29 @@
 
     table = rotation_table((hit_owner.shape[1]) * PAGE + n_section * rows)
     query, normed, turns = project(
-        place, fetch_count, early_tokens, attn_gain, jnp.asarray(table), w_query
+        fetch_count, early_tokens, attn_gain, jnp.asarray(table), w_query
     )
     next_query, last_query = shift(query, 1), shift(query, -1)
     new_latent, span = project_latent(normed, turns, w_latent.T, kv_gain)
     arrived, next_query, last_query, span = lax.optimization_barrier(
         (arrived, next_query, last_query, span)
     )
-    far_query = shift(next_query, 1)
-
-    near = build_keys(place, owner, fetch_count, arrived)
+
+    near = build_keys(owner, fetch_count, arrived)
     far = lax.ppermute(near, "tp", swap)
 
-    own_probes, next_probes, last_probes = make_probes(w_key_up, query, next_query, last_query)
+    own_probes, next_probes, last_probes, low, high = make_probes(
+        w_key_up, query, next_query, last_query
+    )
+    far_low, far_high = shift(low, 1), shift(high, -1)
 
     def partial_for(by, far, *queries, **flags):
-        return attend(by, n_section, place, w_value_up, near, far, span, *queries, **flags)
+        return attend(by, w_value_up, near, far, span, *queries, **flags)
 
     one, far = partial_for(1, far, next_probes, keep_far=True)
-    one, far_query = lax.optimization_barrier((one, far_query))
+    one, far_low, far_high = lax.optimization_barrier((one, far_low, far_high))
     one = shift(one, -1)
-    (two,) = partial_for(2, far, far_query, w_key_up)
+    (two,) = partial_for(2, far, far_low, far_high, w_key_up)
     two, last_probes, one = lax.optimization_barrier((two, last_probes, one))
     two = shift(two, -1)
     (three,) = partial_for(3, far, last_probes)
@@ -551,7 +568,6 @@
     exact, send = project_output(own, one, two, three, w_out)
     incoming = lax.ppermute(send, "tp", swap)
     keep, send = expert(
-        place,
         tokens,
         exact,
         incoming,

time: 86.2 us -> 82.8 us (0.961)
  Pallas kernels: 44.2 us -> 40.1 us
  local copies, waits for them, and re-layouts: 4.36 us -> 6.08 us
    pallas_call x5, Pallas kernels: 27.2 us -> 24.8 us  [the longest x4 23.7 us: attend(): pl.pallas_call(functools.partial(attend_kernel, by, keep_far), out_shape=...]
    unnamed x36 -> x38, local copies, waits for them, and re-layouts: 4.36 us -> 6.08 us
    pallas_call x1, Pallas kernels: 4.34 us -> 3.33 us  [pack_pages(): pl.pallas_call(pack_kernel, out_shape=jax.ShapeDtypeStruct((n_store, rows...]
    ppermute x7 -> x8, starting transfers between devices: 10.7 us -> 9.93 us  [shift(): return lax.ppermute(value, 'section', pairs)]
    ppermute x7 -> x8, waiting for transfers between devices: 8.69 us -> 8.49 us  [shift(): return lax.ppermute(value, 'section', pairs)]
  transfers between devices with their start and end apart: 11 -> 12, of which waited for: 6 -> 6; matrix products, arithmetic and copies ran while one was open for 0% -> 0% of each run, Pallas kernels for 40% -> 39%
where the time goes in v5:
time: 82.8 us; the launch traced here: 82.4 us
  Pallas kernels  40.1 us (48%)
  starting transfers between devices  23.4 us (28%)
  waiting for transfers between devices  11.2 us (14%)
  local copies, waits for them, and re-layouts  6.08 us (7%)
  between operations  0.84 us (1%)
    pallas_call x4, Pallas kernels, attend(): pl.pallas_call(functools.partial(attend_kernel, by, keep_far), out_shape=...  23.7 us
    ppermute x8, starting transfers between devices, shift(): return lax.ppermute(value, 'section', pairs)  9.93 us
    ppermute x8, waiting for transfers between devices, shift(): return lax.ppermute(value, 'section', pairs)  8.49 us
    all_to_all x1, starting transfers between devices, on_device(): lax.all_to_all(outgoing, 'store', split_axis=0, concat_axis=0, tiled=True)  7.6 us
    unnamed x38, local copies, waits for them, and re-layouts  6.08 us
    pallas_call x1, Pallas kernels, project(): pl.pallas_call(project_kernel, out_shape=[jax.ShapeDtypeStruct((rows, col...  5.09 us
    ppermute x1, starting transfers between devices, on_device(): incoming = lax.ppermute(send, 'tp', swap)  3.75 us
    pallas_call x1, Pallas kernels, pack_pages(): pl.pallas_call(pack_kernel, out_shape=jax.ShapeDtypeStruct((n_store, rows...  3.33 us
  transfers between devices with their start and end apart: 12, of which 6 were waited for; matrix products, arithmetic and copies ran while one was open for 0% of the time, Pallas kernels for 39%

profile of v5, /device:TPU:1, one launch (start us, length us, event | category | flops | bytes accessed | tf_op | source)
XLA Modules:
  0.0 82.4 jit_solution(1071889539507052200)
XLA Ops:
  0.6 3.3 %pack_pages.1 = bf16[16,32,1152]{2,1,0:T(8,128)(2,1)} custom-call(s32[16,24]{1,0:T(8,128)} %bitcast.12, s32[16,24]{1,0:T(8,128)} %slot_src.1, bf16[8,576,256]{2,1,0:T(8,128)(2,1)} %bitcast.15), custom_call_target="tpu_custom_call" | custom-call | tf_op jit(solution)/shard_map/pack_pages/pallas_call | solution.py:125
  4.0 7.6 %all-to-all-start = ((bf16[16,2,16,1152]{3,2,1,0:T(8,128)(2,1)}), bf16[16,2,16,1152]{3,2,1,0:T(8,128)(2,1)S(1)}, u32[]{:S(2)}, u32[]{:S(2)}) async-start(bf16[16,2,16,1152]{3,2,1,0:T(8,128)(2,1)} %bitcast.14), calls=%async_computation | async-start | bytes 2359296 | tf_op jit(solution)/shard_map/all_to_all | solution.py:529
  11.6 5.1 %project.1 = (bf16[128,1536]{1,0:T(8,128)(2,1)}, bf16[128,2048]{1,0:T(8,128)(2,1)}, f32[128,128]{1,0:T(8,128)}) custom-call(s32[16]{0:T(128)} %count.3, bf16[128,2048]{1,0:T(8,128)(2,1)} %tokens.1, bf16[2048]{0:T(1024)(128)(2,1)} %gain.2, f32[6656,128]{1,0:T(8,128)} %constant.2.clone.table, bf16[2048,1536]{1,0:T(8,128)(2,1)} %w_query_src.1), custom_call_target="tpu_custom_call" | custom-call | tf_op jit(solution)/shard_map/project/pallas_call | solution.py:225
  16.7 1.7 %collective-permute-start.1 = (bf16[128,1536]{1,0:T(8,128)(2,1)}, bf16[128,1536]{1,0:T(8,128)(2,1)S(1)}, u32[]{:S(2)}, u32[]{:S(2)}) collective-permute-start(bf16[128,1536]{1,0:T(8,128)(2,1)} %get-tuple-element.35.own), channel_id=1, source_target_pairs={{6,0},{0,2},{2,4},{4,6},{7,1},{1,3},{3,5},{5,7},{14,8},{8,10},{10,... | collective-permute-start | bytes 1179656 | tf_op jit(solution)/shard_map/ppermute | solution.py:534
  18.4 2.2 %collective-permute-start = (bf16[128,1536]{1,0:T(8,128)(2,1)}, bf16[128,1536]{1,0:T(8,128)(2,1)S(1)}, u32[]{:S(2)}, u32[]{:S(2)}) collective-permute-start(bf16[128,1536]{1,0:T(8,128)(2,1)} %get-tuple-element.35.own), channel_id=1, source_target_pairs={{2,0},{4,2},{6,4},{0,6},{3,1},{5,3},{7,5},{1,7},{10,8},{12,10},{14... | collective-permute-start | bytes 1179656 | tf_op jit(solution)/shard_map/ppermute | solution.py:534
  20.6 1.7 %copy-done.6 = bf16[2048,576]{0,1:T(8,128)(2,1)S(1)} copy-done((bf16[2048,576]{0,1:T(8,128)(2,1)S(1)}, bf16[2048,576]{0,1:T(8,128)(2,1)}, u32[]{:S(2)}) %copy-start.6) | copy-done | bytes 2359320
  22.3 1.0 %copy-done.8 = bf16[128,2048]{1,0:T(8,128)(2,1)S(1)} copy-done((bf16[128,2048]{1,0:T(8,128)(2,1)S(1)}, bf16[128,2048]{1,0:T(8,128)(2,1)}, u32[]{:S(2)}) %copy-start.8) | copy-done | bytes 524312
  24.2 1.9 %project_latent.1 = (bf16[576,128]{1,0:T(8,128)(2,1)}, bf16[128,640]{1,0:T(8,128)(2,1)S(1)}) custom-call(bf16[128,2048]{1,0:T(8,128)(2,1)S(1)} %copy-done.8, f32[128,128]{1,0:T(8,128)S(1)} %copy-done.14, bf16[576,2048]{1,0:T(8,128)(2,1)S(1)} %bitcast.11, bf16[512]{0:T(512)(128)(2,1)S(1)} %copy-done.18), custom_call_target="tpu_custom_call" | custom-call | tf_op jit(solution)/shard_map/project_latent/pallas_call | solution.py:262
  26.1 3.2 %collective-permute-done.1.behind = bf16[128,1536]{1,0:T(8,128)(2,1)S(1)} collective-permute-done((bf16[128,1536]{1,0:T(8,128)(2,1)}, bf16[128,1536]{1,0:T(8,128)(2,1)S(1)}, u32[]{:S(2)}, u32[]{:S(2)}) %collective-permute-start.1) | collective-permute-done | bytes 393248 | tf_op jit(solution)/shard_map/ppermute | solution.py:534
  31.7 1.6 %collective-permute-start.2 = (bf16[768,640]{1,0:T(8,128)(2,1)S(1)}, bf16[768,640]{1,0:T(8,128)(2,1)S(1)}, u32[]{:S(2)}, u32[]{:S(2)}) collective-permute-start(bf16[768,640]{1,0:T(8,128)(2,1)S(1)} %build_keys.1.near), channel_id=1, source_target_pairs={{0,1},{1,0},{2,3},{3,2},{4,5},{5,4},{6,7},{7,6},{8,9},{9,8},{10,11... | collective-permute-start | bytes 2949128 | tf_op jit(solution)/shard_map/ppermute | solution.py:547
  35.3 3.3 %collective-permute-start.3 = (bf16[64,1536]{1,0:T(8,128)(2,1)S(1)}, bf16[64,1536]{1,0:T(8,128)(2,1)S(1)}, u32[]{:S(2)}, u32[]{:S(2)}) collective-permute-start(bf16[64,1536]{1,0:T(8,128)(2,1)S(1)} %get-tuple-element.46), channel_id=1, source_target_pairs={{2,0},{4,2},{6,4},{0,6},{3,1},{5,3},{7,5},{1,7},{10,8},{12,10},{14... | collective-permute-start | bytes 589832 | tf_op jit(solution)/shard_map/ppermute | solution.py:534
  38.7 5.9 %attend_1.1 = (bf16[128,1152]{1,0:T(8,128)(2,1)S(1)}, bf16[768,640]{1,0:T(8,128)(2,1)S(1)}) custom-call(bf16[8,512,128]{2,1,0:T(8,128)(2,1)S(1)} %copy-done, bf16[768,640]{1,0:T(8,128)(2,1)S(1)} %build_keys.1.near, bf16[768,640]{1,0:T(8,128)(2,1)S(1)} %collective-permute-done.2.arrived, bf16[128,640]{1,0:T(8,128)(2,1)S(1)} %get-tuple-element.40.span, ...), custom_call_target="tpu_custom_call" | custom-call | tf_op jit(solution)/shard_map/attend_1/pallas_call | solution.py:412
  44.6 1.4 %collective-permute-done.4.refs_1_ = bf16[64,1536]{1,0:T(8,128)(2,1)S(1)} collective-permute-done((bf16[64,1536]{1,0:T(8,128)(2,1)S(1)}, bf16[64,1536]{1,0:T(8,128)(2,1)S(1)}, u32[]{:S(2)}, u32[]{:S(2)}) %collective-permute-start.4) | collective-permute-done | bytes 196640 | tf_op jit(solution)/shard_map/ppermute | solution.py:534
  45.9 6.1 %attend_2.1 = bf16[128,1152]{1,0:T(8,128)(2,1)S(1)} custom-call(bf16[8,512,128]{2,1,0:T(8,128)(2,1)S(1)} %copy-done, bf16[768,640]{1,0:T(8,128)(2,1)S(1)} %build_keys.1.near, bf16[768,640]{1,0:T(8,128)(2,1)S(1)} %get-tuple-element.44.arrived, bf16[128,640]{1,0:T(8,128)(2,1)S(1)} %get-tuple-element.40.span, ...), custom_call_target="tpu_custom_call" | custom-call | tf_op jit(solution)/shard_map/attend_2/pallas_call | solution.py:412
  52.1 2.3 %collective-permute-done.5.one = bf16[128,1152]{1,0:T(8,128)(2,1)S(1)} collective-permute-done((bf16[128,1152]{1,0:T(8,128)(2,1)S(1)}, bf16[128,1152]{1,0:T(8,128)(2,1)S(1)}, u32[]{:S(2)}, u32[]{:S(2)}) %collective-permute-start.5) | collective-permute-done | bytes 294944 | tf_op jit(solution)/shard_map/ppermute | solution.py:534
  54.4 5.9 %attend_3.1 = bf16[128,1152]{1,0:T(8,128)(2,1)S(1)} custom-call(bf16[8,512,128]{2,1,0:T(8,128)(2,1)S(1)} %copy-done, bf16[768,640]{1,0:T(8,128)(2,1)S(1)} %build_keys.1.near, bf16[768,640]{1,0:T(8,128)(2,1)S(1)} %get-tuple-element.44.arrived, bf16[128,640]{1,0:T(8,128)(2,1)S(1)} %get-tuple-element.40.span, bf16[1024,640]{1,0:T(8,128)(2,1)S(1)} %get-tuple-element.52.refs_0_), custom_call_target="tpu_custom_call" | custom-call | tf_op jit(solution)/shard_map/attend_3/pallas_call | solution.py:412
  60.3 1.6 %collective-permute-done.6 = bf16[128,1152]{1,0:T(8,128)(2,1)S(1)} collective-permute-done((bf16[128,1152]{1,0:T(8,128)(2,1)S(1)}, bf16[128,1152]{1,0:T(8,128)(2,1)S(1)}, u32[]{:S(2)}, u32[]{:S(2)}) %collective-permute-start.6) | collective-permute-done | bytes 294944 | tf_op jit(solution)/shard_map/ppermute | solution.py:534
  61.9 2.7 %collective-permute-start.8 = (bf16[128,1152]{1,0:T(8,128)(2,1)S(1)}, bf16[128,1152]{1,0:T(8,128)(2,1)S(1)}, u32[]{:S(2)}, u32[]{:S(2)}) collective-permute-start(bf16[128,1152]{1,0:T(8,128)(2,1)S(1)} %attend_3.1), channel_id=1, source_target_pairs={{2,0},{4,2},{6,4},{0,6},{3,1},{5,3},{7,5},{1,7},{10,8},{12,10},{14... | collective-permute-start | bytes 884744 | tf_op jit(solution)/shard_map/ppermute | solution.py:534
  64.6 5.9 %attend_0.1.own = bf16[128,1152]{1,0:T(8,128)(2,1)S(1)} custom-call(bf16[8,512,128]{2,1,0:T(8,128)(2,1)S(1)} %copy-done, bf16[768,640]{1,0:T(8,128)(2,1)S(1)} %build_keys.1.near, bf16[768,640]{1,0:T(8,128)(2,1)S(1)} %get-tuple-element.44.arrived, bf16[128,640]{1,0:T(8,128)(2,1)S(1)} %get-tuple-element.40.span, bf16[1024,640]{1,0:T(8,128)(2,1)S(1)} %get-tuple-element.55.refs_0_), custom_call_target="tpu_custom_call" | custom-call | tf_op jit(solution)/shard_map/attend_0/pallas_call | solution.py:412
  70.5 1.5 %project_output.1 = (f32[128,2048]{1,0:T(8,128)S(1)}, bf16[128,2048]{1,0:T(8,128)(2,1)S(1)}) custom-call(bf16[128,1152]{1,0:T(8,128)(2,1)S(1)} %attend_0.1.own, bf16[128,1152]{1,0:T(8,128)(2,1)S(1)} %collective-permute-done.5.one, bf16[128,1152]{1,0:T(8,128)(2,1)S(1)} %collective-permute-done.7.two, bf16[128,1152]{1,0:T(8,128)(2,1)S(1)} %collective-permute-done.8.three, ...), custom_call_target="tpu_custom_call" | custom-call | tf_op jit(solution)/shard_map/project_output/pallas_call | solution.py:456
  72.1 3.7 %collective-permute-start.9 = (bf16[128,2048]{1,0:T(8,128)(2,1)S(1)}, bf16[128,2048]{1,0:T(8,128)(2,1)S(1)}, u32[]{:S(2)}, u32[]{:S(2)}) collective-permute-start(bf16[128,2048]{1,0:T(8,128)(2,1)S(1)} %get-tuple-element.60), channel_id=1, source_target_pairs={{0,1},{1,0},{2,3},{3,2},{4,5},{5,4},{6,7},{7,6},{8,9},{9,8},{10,11... | collective-permute-start | bytes 1572872 | tf_op jit(solution)/shard_map/ppermute | solution.py:569
  75.8 1.5 %collective-permute-done.9.other = bf16[128,2048]{1,0:T(8,128)(2,1)S(1)} collective-permute-done((bf16[128,2048]{1,0:T(8,128)(2,1)S(1)}, bf16[128,2048]{1,0:T(8,128)(2,1)S(1)}, u32[]{:S(2)}, u32[]{:S(2)}) %collective-permute-start.9) | collective-permute-done | bytes 524320 | tf_op jit(solution)/shard_map/ppermute | solution.py:569
  77.4 2.6 %expert.1 = (f32[128,1024]{1,0:T(8,128)S(1)}, bf16[128,1024]{1,0:T(8,128)(2,1)S(1)}) custom-call(bf16[128,2048]{1,0:T(8,128)(2,1)S(1)} %copy-done.7, f32[128,2048]{1,0:T(8,128)S(1)} %get-tuple-element.59.exact, bf16[128,2048]{1,0:T(8,128)(2,1)S(1)} %collective-permute-done.9.other, bf16[2048]{0:T(1024)(128)(2,1)S(1)} %copy-done.16, ...), custom_call_target="tpu_custom_call" | custom-call | tf_op jit(solution)/shard_map/expert/pallas_call | solution.py:487
  80.4 1.2 %collective-permute-done.10 = bf16[128,1024]{1,0:T(8,128)(2,1)S(1)} collective-permute-done((bf16[128,1024]{1,0:T(8,128)(2,1)S(1)}, bf16[128,1024]{1,0:T(8,128)(2,1)S(1)}, u32[]{:S(2)}, u32[]{:S(2)}) %collective-permute-start.10) | collective-permute-done | bytes 262176 | tf_op jit(solution)/shard_map/ppermute | solution.py:579
  (50 shorter events, 6.5 us)
Async XLA Ops:
  4.0 26.8 %all-to-all-start = ((bf16[16,2,16,1152]{3,2,1,0:T(8,128)(2,1)}), bf16[16,2,16,1152]{3,2,1,0:T(8,128)(2,1)S(1)}, u32[]{:S(2)}, u32[]{:S(2)}) async-start(bf16[16,2,16,1152]{3,2,1,0:T(8,128)(2,1)} %bitcast.14), calls=%async_computation | async-start | bytes 2359296 | tf_op jit(solution)/shard_map/all_to_all | solution.py:529
  11.6 9.0 %copy-start.18 = (bf16[512]{0:T(512)(128)(2,1)S(1)}, bf16[512]{0:T(512)(128)(2,1)}, u32[]{:S(2)}) copy-start(bf16[512]{0:T(512)(128)(2,1)} %kv_gain.1) | copy-start | bytes 3076
  11.6 19.2 %copy-start.15 = (s32[16,24,1]{1,2,0:T(1,128)S(1)}, s32[16,24,1]{1,2,0:T(1,128)}, u32[]{:S(2)}) copy-start(s32[16,24,1]{1,2,0:T(1,128)} %param.30) | copy-start | bytes 4612
  16.7 14.1 %copy-start.17 = (s32[16]{0:T(128)S(1)}, s32[16]{0:T(128)}, u32[]{:S(2)}) copy-start(s32[16]{0:T(128)} %count.3) | copy-start | bytes 196
  16.7 12.6 %collective-permute-start.1 = (bf16[128,1536]{1,0:T(8,128)(2,1)}, bf16[128,1536]{1,0:T(8,128)(2,1)S(1)}, u32[]{:S(2)}, u32[]{:S(2)}) collective-permute-start(bf16[128,1536]{1,0:T(8,128)(2,1)} %get-tuple-element.35.own), channel_id=1, source_target_pairs={{6,0},{0,2},{2,4},{4,6},{7,1},{1,3},{3,5},{5,7},{14,8},{8,10},{10,... | collective-permute-start | bytes 1179656 | tf_op jit(solution)/shard_map/ppermute | solution.py:534
  18.4 11.6 %collective-permute-start = (bf16[128,1536]{1,0:T(8,128)(2,1)}, bf16[128,1536]{1,0:T(8,128)(2,1)S(1)}, u32[]{:S(2)}, u32[]{:S(2)}) collective-permute-start(bf16[128,1536]{1,0:T(8,128)(2,1)} %get-tuple-element.35.own), channel_id=1, source_target_pairs={{2,0},{4,2},{6,4},{0,6},{3,1},{5,3},{7,5},{1,7},{10,8},{12,10},{14... | collective-permute-start | bytes 1179656 | tf_op jit(solution)/shard_map/ppermute | solution.py:534
  24.2 9.1 %copy-start.1 = (bf16[8,512,128]{2,1,0:T(8,128)(2,1)S(1)}, bf16[8,512,128]{2,1,0:T(8,128)(2,1)}, u32[]{:S(2)}) copy-start(bf16[8,512,128]{2,1,0:T(8,128)(2,1)} %refs_2_.1) | copy-start | bytes 3145732
  26.1 12.6 %copy-start = (bf16[8,512,128]{2,1,0:T(8,128)(2,1)S(1)}, bf16[8,512,128]{2,1,0:T(8,128)(2,1)}, u32[]{:S(2)}) copy-start(bf16[8,512,128]{2,1,0:T(8,128)(2,1)} %value_up.7) | copy-start | bytes 3145732
  30.8 2.5 %copy-start.11 = (bf16[128,1536]{1,0:T(8,128)(2,1)S(1)}, bf16[128,1536]{1,0:T(8,128)(2,1)}, u32[]{:S(2)}) copy-start(bf16[128,1536]{1,0:T(8,128)(2,1)} %copy-done.10) | copy-start | bytes 1179652
  31.7 7.0 %collective-permute-start.2 = (bf16[768,640]{1,0:T(8,128)(2,1)S(1)}, bf16[768,640]{1,0:T(8,128)(2,1)S(1)}, u32[]{:S(2)}, u32[]{:S(2)}) collective-permute-start(bf16[768,640]{1,0:T(8,128)(2,1)S(1)} %build_keys.1.near), channel_id=1, source_target_pairs={{0,1},{1,0},{2,3},{3,2},{4,5},{5,4},{6,7},{7,6},{8,9},{9,8},{10,11... | collective-permute-start | bytes 2949128 | tf_op jit(solution)/shard_map/ppermute | solution.py:547
  35.3 9.2 %collective-permute-start.3 = (bf16[64,1536]{1,0:T(8,128)(2,1)S(1)}, bf16[64,1536]{1,0:T(8,128)(2,1)S(1)}, u32[]{:S(2)}, u32[]{:S(2)}) collective-permute-start(bf16[64,1536]{1,0:T(8,128)(2,1)S(1)} %get-tuple-element.46), channel_id=1, source_target_pairs={{2,0},{4,2},{6,4},{0,6},{3,1},{5,3},{7,5},{1,7},{10,8},{12,10},{14... | collective-permute-start | bytes 589832 | tf_op jit(solution)/shard_map/ppermute | solution.py:534
  38.7 7.3 %collective-permute-start.4 = (bf16[64,1536]{1,0:T(8,128)(2,1)S(1)}, bf16[64,1536]{1,0:T(8,128)(2,1)S(1)}, u32[]{:S(2)}, u32[]{:S(2)}) collective-permute-start(bf16[64,1536]{1,0:T(8,128)(2,1)S(1)} %get-tuple-element.47), channel_id=1, source_target_pairs={{6,0},{0,2},{2,4},{4,6},{7,1},{1,3},{3,5},{5,7},{14,8},{8,10},{10,... | collective-permute-start | bytes 589832 | tf_op jit(solution)/shard_map/ppermute | solution.py:534
  45.9 8.4 %collective-permute-start.5 = (bf16[128,1152]{1,0:T(8,128)(2,1)S(1)}, bf16[128,1152]{1,0:T(8,128)(2,1)S(1)}, u32[]{:S(2)}, u32[]{:S(2)}) collective-permute-start(bf16[128,1152]{1,0:T(8,128)(2,1)S(1)} %get-tuple-element.51), channel_id=1, source_target_pairs={{6,0},{0,2},{2,4},{4,6},{7,1},{1,3},{3,5},{5,7},{14,8},{8,10},{10,... | collective-permute-start | bytes 884744 | tf_op jit(solution)/shard_map/ppermute | solution.py:534
  54.4 7.5 %collective-permute-start.6 = (bf16[128,1152]{1,0:T(8,128)(2,1)S(1)}, bf16[128,1152]{1,0:T(8,128)(2,1)S(1)}, u32[]{:S(2)}, u32[]{:S(2)}) collective-permute-start(bf16[128,1152]{1,0:T(8,128)(2,1)S(1)} %attend_2.1), channel_id=1, source_target_pairs={{6,0},{0,2},{2,4},{4,6},{7,1},{1,3},{3,5},{5,7},{14,8},{8,10},{10,... | collective-permute-start | bytes 884744 | tf_op jit(solution)/shard_map/ppermute | solution.py:534
  54.4 23.0 %copy-start.5 = (bf16[704,2048]{1,0:T(8,128)(2,1)S(1)}, bf16[704,2048]{1,0:T(8,128)(2,1)}, u32[]{:S(2)}) copy-start(bf16[704,2048]{1,0:T(8,128)(2,1)} %w_down.1) | copy-start | bytes 8650756
  54.4 23.0 %copy-start.7 = (bf16[128,2048]{1,0:T(8,128)(2,1)S(1)}, bf16[128,2048]{1,0:T(8,128)(2,1)}, u32[]{:S(2)}) copy-start(bf16[128,2048]{1,0:T(8,128)(2,1)} %tokens.1) | copy-start | bytes 1572868
  61.9 8.6 %copy-start.2 = (bf16[1024,2048]{1,0:T(8,128)(2,1)S(1)}, bf16[1024,2048]{1,0:T(8,128)(2,1)}, u32[]{:S(2)}) copy-start(bf16[1024,2048]{1,0:T(8,128)(2,1)} %weight.1) | copy-start | bytes 12582916
  61.9 8.6 %collective-permute-start.7 = (bf16[128,1152]{1,0:T(8,128)(2,1)S(1)}, bf16[128,1152]{1,0:T(8,128)(2,1)S(1)}, u32[]{:S(2)}, u32[]{:S(2)}) collective-permute-start(bf16[128,1152]{1,0:T(8,128)(2,1)S(1)} %collective-permute-done.6), channel_id=1, source_target_pairs={{6,0},{0,2},{2,4},{4,6},{7,1},{1,3},{3,5},{5,7},{14,8},{8,10},{10,... | collective-permute-start | bytes 884744 | tf_op jit(solution)/shard_map/ppermute | solution.py:534
  61.9 8.6 %collective-permute-start.8 = (bf16[128,1152]{1,0:T(8,128)(2,1)S(1)}, bf16[128,1152]{1,0:T(8,128)(2,1)S(1)}, u32[]{:S(2)}, u32[]{:S(2)}) collective-permute-start(bf16[128,1152]{1,0:T(8,128)(2,1)S(1)} %attend_3.1), channel_id=1, source_target_pairs={{2,0},{4,2},{6,4},{0,6},{3,1},{5,3},{7,5},{1,7},{10,8},{12,10},{14... | collective-permute-start | bytes 884744 | tf_op jit(solution)/shard_map/ppermute | solution.py:534
  64.6 12.8 %copy-start.4 = (bf16[2048,704]{0,1:T(8,128)(2,1)S(1)}, bf16[2048,704]{0,1:T(8,128)(2,1)}, u32[]{:S(2)}) copy-start(bf16[2048,704]{0,1:T(8,128)(2,1)} %param.27) | copy-start | bytes 8650756
  70.5 6.9 %copy-start.3 = (bf16[2048,704]{0,1:T(8,128)(2,1)S(1)}, bf16[2048,704]{0,1:T(8,128)(2,1)}, u32[]{:S(2)}) copy-start(bf16[2048,704]{0,1:T(8,128)(2,1)} %param.26) | copy-start | bytes 8650756
  70.5 6.9 %copy-start.16 = (bf16[2048]{0:T(1024)(128)(2,1)S(1)}, bf16[2048]{0:T(1024)(128)(2,1)}, u32[]{:S(2)}) copy-start(bf16[2048]{0:T(1024)(128)(2,1)} %gain.3) | copy-start | bytes 12292
  72.1 5.3 %collective-permute-start.9 = (bf16[128,2048]{1,0:T(8,128)(2,1)S(1)}, bf16[128,2048]{1,0:T(8,128)(2,1)S(1)}, u32[]{:S(2)}, u32[]{:S(2)}) collective-permute-start(bf16[128,2048]{1,0:T(8,128)(2,1)S(1)} %get-tuple-element.60), channel_id=1, source_target_pairs={{0,1},{1,0},{2,3},{3,2},{4,5},{5,4},{6,7},{7,6},{8,9},{9,8},{10,11... | collective-permute-start | bytes 1572872 | tf_op jit(solution)/shard_map/ppermute | solution.py:569
  80.0 1.6 %collective-permute-start.10 = (bf16[128,1024]{1,0:T(8,128)(2,1)S(1)}, bf16[128,1024]{1,0:T(8,128)(2,1)S(1)}, u32[]{:S(2)}, u32[]{:S(2)}) collective-permute-start(bf16[128,1024]{1,0:T(8,128)(2,1)S(1)} %get-tuple-element.62), channel_id=1, source_target_pairs={{0,1},{1,0},{2,3},{3,2},{4,5},{5,4},{6,7},{7,6},{8,9},{9,8},{10,11... | collective-permute-start | bytes 786440 | tf_op jit(solution)/shard_map/ppermute | solution.py:579
  (7 other events, 8.6 us)

commit v6 on v5

--- a/solution.py
+++ b/solution.py
@@ -134,7 +134,8 @@
             pltpu.VMEM((n_store, rows, MSG), BF16),
             pltpu.SemaphoreType.DMA((4 + n_pages // 2,)),
         ],
-        compiler_params=params(60),
+        compiler_params=params(56),
+        cost_estimate=pl.CostEstimate(flops=2 * 10**10, bytes_accessed=6 * 10**7, transcendentals=0),
         name="pack_pages",
     )(owner, slot, pool_t)
 
@@ -182,17 +183,12 @@
 
 
 def project_kernel(
-    count, tokens_src, gain, table, w_query_src, query, normed, turns, tokens, w_query, total, sems
+    count, tokens_src, gain, table, w_query, query, normed, turns, tokens, total, sems
 ):
     rows = tokens.shape[0]
     group, section = lax.axis_index("store"), lax.axis_index("section")
     start = pl.multiple_of(count[group] * PAGE + section * rows, rows)
     pairs = [(tokens_src, tokens), (table.at[pl.ds(start, rows), :], turns)]
-    pieces = 8
-    depth = w_query.shape[0] // pieces
-    for k in range(pieces):
-        at = pl.ds(k * depth, depth)
-        pairs.append((w_query_src.at[at, :], w_query.at[at, :]))
     copies = [
         pltpu.make_async_copy(src, dst, sems.at[i]) for i, (src, dst) in enumerate(pairs)
     ]
@@ -204,12 +200,7 @@
     cosine, sine = turns[:, :ROPE], turns[:, ROPE:]
     cosine = jnp.concatenate([cosine, cosine], axis=1)
     sine = jnp.concatenate([sine, sine], axis=1)
-    for k in range(0, pieces, 2):
-        copies[2 + k].wait()
-        copies[3 + k].wait()
-        at = slice(k * depth, (k + 2) * depth)
-        part = dot(normed[:, at], w_query[at, :])
-        total[...] = part if k == 0 else total[...] + part
+    total[...] = dot(normed[...], w_query[...])
     head = NOPE + ROPE
     for at in range(0, query.shape[1], 2 * head):
         part = total[:, at : at + 2 * head].astype(BF16).astype(F32)
@@ -229,15 +220,14 @@
             jax.ShapeDtypeStruct(tokens.shape, BF16),
             jax.ShapeDtypeStruct((rows, 2 * ROPE), F32),
         ],
-        in_specs=[SMEM, HBM, VMEM] + [HBM] * 2,
+        in_specs=[SMEM, HBM, VMEM, HBM, VMEM],
         out_specs=[VMEM] * 3,
         scratch_shapes=[
             pltpu.VMEM(tokens.shape, BF16),
-            pltpu.VMEM(w_query.shape, BF16),
             pltpu.VMEM((rows, cols), F32),
-            pltpu.SemaphoreType.DMA((10,)),
+            pltpu.SemaphoreType.DMA((2,)),
         ],
-        compiler_params=params(60),
+        compiler_params=params(30),
         name="project",
     )(count, tokens, gain, table, w_query)
 
@@ -293,7 +283,18 @@
         probes[at, KVR:] = jnp.where(rope_lanes < ROPE, pair, one).astype(BF16)
 
 
-def probes_kernel(key_up, own, ahead, behind, own_probes, ahead_probes, behind_probes, low, high):
+def probes_kernel(
+    key_up, own_src, ahead_src, behind_src, own_probes, ahead_probes, behind_probes, low, high,
+    own, ahead, behind, sems
+):
+    pairs = ((ahead_src, ahead), (behind_src, behind), (own_src, own))
+    copies = [
+        pltpu.make_async_copy(src, dst, sems.at[i]) for i, (src, dst) in enumerate(pairs)
+    ]
+    for copy in copies:
+        copy.start()
+    for copy in copies:
+        copy.wait()
     cut = low.shape[0]
     low[...] = ahead[:cut, :]
     high[...] = behind[cut:, :]
@@ -308,9 +309,10 @@
     return pl.pallas_call(
         probes_kernel,
         out_shape=[probes] * 3 + [half] * 2,
-        in_specs=[VMEM] * 4,
+        in_specs=[VMEM] + [HBM] * 3,
         out_specs=[VMEM] * 5,
-        compiler_params=params(16),
+        scratch_shapes=[pltpu.VMEM((rows, width), BF16)] * 3 + [pltpu.SemaphoreType.DMA((3,))],
+        compiler_params=params(30),
         name="make_probes",
     )(key_up, own, ahead, behind)
 

time: 82.8 us -> 83.7 us (1.011)
  waiting for transfers between devices: 11.2 us -> 14.5 us
  Pallas kernels: 40.1 us -> 37.7 us
  local copies, waits for them, and re-layouts: 6.08 us -> 7.32 us
  starting transfers between devices: 23.4 us -> 22.2 us
    ppermute x8, waiting for transfers between devices: 8.49 us -> 11.8 us  [shift(): return lax.ppermute(value, 'section', pairs)]
    pallas_call x1, Pallas kernels: 5.09 us -> 2.05 us  [project(): pl.pallas_call(project_kernel, out_shape=[jax.ShapeDtypeStruct((rows, col...]
    ppermute x8, starting transfers between devices: 9.93 us -> 8.65 us  [shift(): return lax.ppermute(value, 'section', pairs)]
    unnamed x38 -> x44, local copies, waits for them, and re-layouts: 6.08 us -> 7.32 us
  transfers between devices with their start and end apart: 12 -> 12, of which waited for: 6 -> 6; matrix products, arithmetic and copies ran while one was open for 0% -> 0% of each run, Pallas kernels for 39% -> 35%
where the time goes in v6:
time: 83.7 us; the launch traced here: 83.4 us
  Pallas kernels  37.7 us (45%)
  starting transfers between devices  22.2 us (27%)
  waiting for transfers between devices  14.5 us (17%)
  local copies, waits for them, and re-layouts  7.32 us (9%)
  between operations  0.88 us (1%)
    pallas_call x4, Pallas kernels, attend(): pl.pallas_call(functools.partial(attend_kernel, by, keep_far), out_shape=...  23.7 us
    ppermute x8, waiting for transfers between devices, shift(): return lax.ppermute(value, 'section', pairs)  11.8 us
    ppermute x8, starting transfers between devices, shift(): return lax.ppermute(value, 'section', pairs)  8.65 us
    all_to_all x1, starting transfers between devices, on_device(): lax.all_to_all(outgoing, 'store', split_axis=0, concat_axis=0, tiled=True)  7.73 us
    unnamed x44, local copies, waits for them, and re-layouts  7.32 us
    ppermute x1, starting transfers between devices, on_device(): incoming = lax.ppermute(send, 'tp', swap)  3.76 us
    pallas_call x1, Pallas kernels, pack_pages(): pl.pallas_call(pack_kernel, out_shape=jax.ShapeDtypeStruct((n_store, rows...  3.32 us
    pallas_call x1, Pallas kernels, expert(): pl.pallas_call(expert_kernel, out_shape=[jax.ShapeDtypeStruct((rows, half...  2.59 us
  transfers between devices with their start and end apart: 12, of which 6 were waited for; matrix products, arithmetic and copies ran while one was open for 0% of the time, Pallas kernels for 35%

profile of v6, /device:TPU:1, one launch (start us, length us, event | category | flops | bytes accessed | tf_op | source)
XLA Modules:
  0.0 83.4 jit_solution(14052434858003933761)
XLA Ops:
  0.6 3.3 %pack_pages.1 = bf16[16,32,1152]{2,1,0:T(8,128)(2,1)} custom-call(s32[16,24]{1,0:T(8,128)} %bitcast.12, s32[16,24]{1,0:T(8,128)} %slot_src.1, bf16[8,576,256]{2,1,0:T(8,128)(2,1)} %bitcast.15), custom_call_target="tpu_custom_call" | custom-call | flops 20000000000 | bytes 60000000 | tf_op jit(solution)/shard_map/pack_pages/pallas_call | solution.py:125
  4.0 7.7 %all-to-all-start = ((bf16[16,2,16,1152]{3,2,1,0:T(8,128)(2,1)}), bf16[16,2,16,1152]{3,2,1,0:T(8,128)(2,1)S(1)}, u32[]{:S(2)}, u32[]{:S(2)}) async-start(bf16[16,2,16,1152]{3,2,1,0:T(8,128)(2,1)} %bitcast.14), calls=%async_computation | async-start | bytes 2359296 | tf_op jit(solution)/shard_map/all_to_all | solution.py:531
  11.8 2.8 %copy-done.1 = bf16[2048,1536]{1,0:T(8,128)(2,1)S(1)} copy-done((bf16[2048,1536]{1,0:T(8,128)(2,1)S(1)}, bf16[2048,1536]{1,0:T(8,128)(2,1)}, u32[]{:S(2)}) %copy-start.1) | copy-done | bytes 6291480
  14.6 2.0 %copy-done.4 = f32[6656,128]{1,0:T(8,128)S(1)} copy-done((f32[6656,128]{1,0:T(8,128)S(1)}, f32[6656,128]{1,0:T(8,128)}, u32[]{:S(2)}) %copy-start.4) | copy-done | bytes 3407896
  16.5 2.0 %project.1 = (bf16[128,1536]{1,0:T(8,128)(2,1)S(1)}, bf16[128,2048]{1,0:T(8,128)(2,1)S(1)}, f32[128,128]{1,0:T(8,128)S(1)}) custom-call(s32[16]{0:T(128)S(1)} %copy-done.20, bf16[128,2048]{1,0:T(8,128)(2,1)S(1)} %copy-done.9, bf16[2048]{0:T(1024)(128)(2,1)S(1)} %copy-done.19, f32[6656,128]{1,0:T(8,128)S(1)} %copy-done.4, bf16[2048,1536]{1,0:T(8,128)(2,1)S(1)} %copy-done.1), custom_call_target="tpu_custom_call" | custom-call | tf_op jit(solution)/shard_map/project/pallas_call | solution.py:216
  18.6 1.7 %collective-permute-start.1 = (bf16[128,1536]{1,0:T(8,128)(2,1)S(1)}, bf16[128,1536]{1,0:T(8,128)(2,1)S(1)}, u32[]{:S(2)}, u32[]{:S(2)}) collective-permute-start(bf16[128,1536]{1,0:T(8,128)(2,1)S(1)} %get-tuple-element.35.own_src), channel_id=1, source_target_pairs={{6,0},{0,2},{2,4},{4,6},{7,1},{1,3},{3,5},{5,7},{14,8},{8,10},{10,... | collective-permute-start | bytes 1179656 | tf_op jit(solution)/shard_map/ppermute | solution.py:536
  20.3 2.2 %collective-permute-start = (bf16[128,1536]{1,0:T(8,128)(2,1)S(1)}, bf16[128,1536]{1,0:T(8,128)(2,1)S(1)}, u32[]{:S(2)}, u32[]{:S(2)}) collective-permute-start(bf16[128,1536]{1,0:T(8,128)(2,1)S(1)} %get-tuple-element.35.own_src), channel_id=1, source_target_pairs={{2,0},{4,2},{6,4},{0,6},{3,1},{5,3},{7,5},{1,7},{10,8},{12,10},{14... | collective-permute-start | bytes 1179656 | tf_op jit(solution)/shard_map/ppermute | solution.py:536
  22.5 1.9 %project_latent.1 = (bf16[576,128]{1,0:T(8,128)(2,1)}, bf16[128,640]{1,0:T(8,128)(2,1)S(1)}) custom-call(bf16[128,2048]{1,0:T(8,128)(2,1)S(1)} %get-tuple-element.36.normed, f32[128,128]{1,0:T(8,128)S(1)} %get-tuple-element.37.turns, bf16[576,2048]{1,0:T(8,128)(2,1)S(1)} %bitcast.11, bf16[512]{0:T(512)(128)(2,1)S(1)} %copy-done.21), custom_call_target="tpu_custom_call" | custom-call | tf_op jit(solution)/shard_map/project_latent/pallas_call | solution.py:252
  24.4 6.5 %collective-permute-done.1.behind_src = bf16[128,1536]{1,0:T(8,128)(2,1)S(1)} collective-permute-done((bf16[128,1536]{1,0:T(8,128)(2,1)S(1)}, bf16[128,1536]{1,0:T(8,128)(2,1)S(1)}, u32[]{:S(2)}, u32[]{:S(2)}) %collective-permute-start.1) | collective-permute-done | bytes 393248 | tf_op jit(solution)/shard_map/ppermute | solution.py:536
  33.3 1.6 %collective-permute-start.2 = (bf16[768,640]{1,0:T(8,128)(2,1)S(1)}, bf16[768,640]{1,0:T(8,128)(2,1)S(1)}, u32[]{:S(2)}, u32[]{:S(2)}) collective-permute-start(bf16[768,640]{1,0:T(8,128)(2,1)S(1)} %build_keys.1.near), channel_id=1, source_target_pairs={{0,1},{1,0},{2,3},{3,2},{4,5},{5,4},{6,7},{7,6},{8,9},{9,8},{10,11... | collective-permute-start | bytes 2949128 | tf_op jit(solution)/shard_map/ppermute | solution.py:549
  36.0 1.6 %make_probes.1 = (bf16[1024,640]{1,0:T(8,128)(2,1)S(1)}, bf16[1024,640]{1,0:T(8,128)(2,1)S(1)}, bf16[1024,640]{1,0:T(8,128)(2,1)S(1)}, bf16[64,1536]{1,0:T(8,128)(2,1)S(1)}, bf16[64,1536]{1,0:T(8,128)(2,1)S(1)}) custom-call(bf16[8,512,128]{2,1,0:T(8,128)(2,1)S(1)} %copy-done.2, bf16[128,1536]{1,0:T(8,128)(2,1)S(1)} %copy-done.12, ...), custom_call_target="tpu_custom_call" | custom-call | tf_op jit(solution)/shard_map/make_probes/pallas_call | solution.py:309
  37.6 2.1 %collective-permute-start.3 = (bf16[64,1536]{1,0:T(8,128)(2,1)S(1)}, bf16[64,1536]{1,0:T(8,128)(2,1)S(1)}, u32[]{:S(2)}, u32[]{:S(2)}) collective-permute-start(bf16[64,1536]{1,0:T(8,128)(2,1)S(1)} %get-tuple-element.46), channel_id=1, source_target_pairs={{2,0},{4,2},{6,4},{0,6},{3,1},{5,3},{7,5},{1,7},{10,8},{12,10},{14... | collective-permute-start | bytes 589832 | tf_op jit(solution)/shard_map/ppermute | solution.py:536
  39.7 5.9 %attend_1.1 = (bf16[128,1152]{1,0:T(8,128)(2,1)S(1)}, bf16[768,640]{1,0:T(8,128)(2,1)S(1)}) custom-call(bf16[8,512,128]{2,1,0:T(8,128)(2,1)S(1)} %copy-done, bf16[768,640]{1,0:T(8,128)(2,1)S(1)} %build_keys.1.near, bf16[768,640]{1,0:T(8,128)(2,1)S(1)} %collective-permute-done.2.arrived, bf16[128,640]{1,0:T(8,128)(2,1)S(1)} %get-tuple-element.40.span, ...), custom_call_target="tpu_custom_call" | custom-call | tf_op jit(solution)/shard_map/attend_1/pallas_call | solution.py:414
  45.6 1.4 %collective-permute-done.4.refs_1_ = bf16[64,1536]{1,0:T(8,128)(2,1)S(1)} collective-permute-done((bf16[64,1536]{1,0:T(8,128)(2,1)S(1)}, bf16[64,1536]{1,0:T(8,128)(2,1)S(1)}, u32[]{:S(2)}, u32[]{:S(2)}) %collective-permute-start.4) | collective-permute-done | bytes 196640 | tf_op jit(solution)/shard_map/ppermute | solution.py:536
  47.0 6.1 %attend_2.1 = bf16[128,1152]{1,0:T(8,128)(2,1)S(1)} custom-call(bf16[8,512,128]{2,1,0:T(8,128)(2,1)S(1)} %copy-done, bf16[768,640]{1,0:T(8,128)(2,1)S(1)} %build_keys.1.near, bf16[768,640]{1,0:T(8,128)(2,1)S(1)} %get-tuple-element.44.arrived, bf16[128,640]{1,0:T(8,128)(2,1)S(1)} %get-tuple-element.40.span, ...), custom_call_target="tpu_custom_call" | custom-call | tf_op jit(solution)/shard_map/attend_2/pallas_call | solution.py:414
  53.1 2.3 %collective-permute-done.5.one = bf16[128,1152]{1,0:T(8,128)(2,1)S(1)} collective-permute-done((bf16[128,1152]{1,0:T(8,128)(2,1)S(1)}, bf16[128,1152]{1,0:T(8,128)(2,1)S(1)}, u32[]{:S(2)}, u32[]{:S(2)}) %collective-permute-start.5) | collective-permute-done | bytes 294944 | tf_op jit(solution)/shard_map/ppermute | solution.py:536
  55.4 5.9 %attend_3.1 = bf16[128,1152]{1,0:T(8,128)(2,1)S(1)} custom-call(bf16[8,512,128]{2,1,0:T(8,128)(2,1)S(1)} %copy-done, bf16[768,640]{1,0:T(8,128)(2,1)S(1)} %build_keys.1.near, bf16[768,640]{1,0:T(8,128)(2,1)S(1)} %get-tuple-element.44.arrived, bf16[128,640]{1,0:T(8,128)(2,1)S(1)} %get-tuple-element.40.span, bf16[1024,640]{1,0:T(8,128)(2,1)S(1)} %get-tuple-element.52.refs_0_), custom_call_target="tpu_custom_call" | custom-call | tf_op jit(solution)/shard_map/attend_3/pallas_call | solution.py:414
  61.3 1.6 %collective-permute-done.6 = bf16[128,1152]{1,0:T(8,128)(2,1)S(1)} collective-permute-done((bf16[128,1152]{1,0:T(8,128)(2,1)S(1)}, bf16[128,1152]{1,0:T(8,128)(2,1)S(1)}, u32[]{:S(2)}, u32[]{:S(2)}) %collective-permute-start.6) | collective-permute-done | bytes 294944 | tf_op jit(solution)/shard_map/ppermute | solution.py:536
  62.9 2.7 %collective-permute-start.8 = (bf16[128,1152]{1,0:T(8,128)(2,1)S(1)}, bf16[128,1152]{1,0:T(8,128)(2,1)S(1)}, u32[]{:S(2)}, u32[]{:S(2)}) collective-permute-start(bf16[128,1152]{1,0:T(8,128)(2,1)S(1)} %attend_3.1), channel_id=1, source_target_pairs={{2,0},{4,2},{6,4},{0,6},{3,1},{5,3},{7,5},{1,7},{10,8},{12,10},{14... | collective-permute-start | bytes 884744 | tf_op jit(solution)/shard_map/ppermute | solution.py:536
  65.6 5.9 %attend_0.1.own = bf16[128,1152]{1,0:T(8,128)(2,1)S(1)} custom-call(bf16[8,512,128]{2,1,0:T(8,128)(2,1)S(1)} %copy-done, bf16[768,640]{1,0:T(8,128)(2,1)S(1)} %build_keys.1.near, bf16[768,640]{1,0:T(8,128)(2,1)S(1)} %get-tuple-element.44.arrived, bf16[128,640]{1,0:T(8,128)(2,1)S(1)} %get-tuple-element.40.span, bf16[1024,640]{1,0:T(8,128)(2,1)S(1)} %get-tuple-element.55.refs_0_), custom_call_target="tpu_custom_call" | custom-call | tf_op jit(solution)/shard_map/attend_0/pallas_call | solution.py:414
  71.5 1.5 %project_output.1 = (f32[128,2048]{1,0:T(8,128)S(1)}, bf16[128,2048]{1,0:T(8,128)(2,1)S(1)}) custom-call(bf16[128,1152]{1,0:T(8,128)(2,1)S(1)} %attend_0.1.own, bf16[128,1152]{1,0:T(8,128)(2,1)S(1)} %collective-permute-done.5.one, bf16[128,1152]{1,0:T(8,128)(2,1)S(1)} %collective-permute-done.7.two, bf16[128,1152]{1,0:T(8,128)(2,1)S(1)} %collective-permute-done.8.three, ...), custom_call_target="tpu_custom_call" | custom-call | tf_op jit(solution)/shard_map/project_output/pallas_call | solution.py:458
  73.1 3.8 %collective-permute-start.9 = (bf16[128,2048]{1,0:T(8,128)(2,1)S(1)}, bf16[128,2048]{1,0:T(8,128)(2,1)S(1)}, u32[]{:S(2)}, u32[]{:S(2)}) collective-permute-start(bf16[128,2048]{1,0:T(8,128)(2,1)S(1)} %get-tuple-element.60), channel_id=1, source_target_pairs={{0,1},{1,0},{2,3},{3,2},{4,5},{5,4},{6,7},{7,6},{8,9},{9,8},{10,11... | collective-permute-start | bytes 1572872 | tf_op jit(solution)/shard_map/ppermute | solution.py:571
  76.8 1.5 %collective-permute-done.9.other = bf16[128,2048]{1,0:T(8,128)(2,1)S(1)} collective-permute-done((bf16[128,2048]{1,0:T(8,128)(2,1)S(1)}, bf16[128,2048]{1,0:T(8,128)(2,1)S(1)}, u32[]{:S(2)}, u32[]{:S(2)}) %collective-permute-start.9) | collective-permute-done | bytes 524320 | tf_op jit(solution)/shard_map/ppermute | solution.py:571
  78.4 2.6 %expert.1 = (f32[128,1024]{1,0:T(8,128)S(1)}, bf16[128,1024]{1,0:T(8,128)(2,1)S(1)}) custom-call(bf16[128,2048]{1,0:T(8,128)(2,1)S(1)} %copy-done.10, f32[128,2048]{1,0:T(8,128)S(1)} %get-tuple-element.59.exact, bf16[128,2048]{1,0:T(8,128)(2,1)S(1)} %collective-permute-done.9.other, bf16[2048]{0:T(1024)(128)(2,1)S(1)} %copy-done.18, ...), custom_call_target="tpu_custom_call" | custom-call | tf_op jit(solution)/shard_map/expert/pallas_call | solution.py:489
  (56 shorter events, 5.9 us)
Async XLA Ops:
  4.0 7.8 %copy-start.9 = (bf16[128,2048]{1,0:T(8,128)(2,1)S(1)}, bf16[128,2048]{1,0:T(8,128)(2,1)}, u32[]{:S(2)}) copy-start(bf16[128,2048]{1,0:T(8,128)(2,1)} %tokens.1) | copy-start | bytes 1572868
  4.0 7.8 %copy-start.19 = (bf16[2048]{0:T(1024)(128)(2,1)S(1)}, bf16[2048]{0:T(1024)(128)(2,1)}, u32[]{:S(2)}) copy-start(bf16[2048]{0:T(1024)(128)(2,1)} %gain.2) | copy-start | bytes 12292
  4.0 7.8 %copy-start.20 = (s32[16]{0:T(128)S(1)}, s32[16]{0:T(128)}, u32[]{:S(2)}) copy-start(s32[16]{0:T(128)} %count.3) | copy-start | bytes 196
  4.0 28.5 %all-to-all-start = ((bf16[16,2,16,1152]{3,2,1,0:T(8,128)(2,1)}), bf16[16,2,16,1152]{3,2,1,0:T(8,128)(2,1)S(1)}, u32[]{:S(2)}, u32[]{:S(2)}) async-start(bf16[16,2,16,1152]{3,2,1,0:T(8,128)(2,1)} %bitcast.14), calls=%async_computation | async-start | bytes 2359296 | tf_op jit(solution)/shard_map/all_to_all | solution.py:531
  18.6 12.4 %copy-start.11 = (bf16[128,1536]{1,0:T(8,128)(2,1)}, bf16[128,1536]{1,0:T(8,128)(2,1)S(1)}, u32[]{:S(2)}) copy-start(bf16[128,1536]{1,0:T(8,128)(2,1)S(1)} %get-tuple-element.35.own_src) | copy-start | bytes 1179652
  18.6 13.9 %copy-start.17 = (s32[16,24,1]{1,2,0:T(1,128)S(1)}, s32[16,24,1]{1,2,0:T(1,128)}, u32[]{:S(2)}) copy-start(s32[16,24,1]{1,2,0:T(1,128)} %param.30) | copy-start | bytes 4612
  18.6 12.3 %collective-permute-start.1 = (bf16[128,1536]{1,0:T(8,128)(2,1)S(1)}, bf16[128,1536]{1,0:T(8,128)(2,1)S(1)}, u32[]{:S(2)}, u32[]{:S(2)}) collective-permute-start(bf16[128,1536]{1,0:T(8,128)(2,1)S(1)} %get-tuple-element.35.own_src), channel_id=1, source_target_pairs={{6,0},{0,2},{2,4},{4,6},{7,1},{1,3},{3,5},{5,7},{14,8},{8,10},{10,... | collective-permute-start | bytes 1179656 | tf_op jit(solution)/shard_map/ppermute | solution.py:536
  20.3 11.4 %collective-permute-start = (bf16[128,1536]{1,0:T(8,128)(2,1)S(1)}, bf16[128,1536]{1,0:T(8,128)(2,1)S(1)}, u32[]{:S(2)}, u32[]{:S(2)}) collective-permute-start(bf16[128,1536]{1,0:T(8,128)(2,1)S(1)} %get-tuple-element.35.own_src), channel_id=1, source_target_pairs={{2,0},{4,2},{6,4},{0,6},{3,1},{5,3},{7,5},{1,7},{10,8},{12,10},{14... | collective-permute-start | bytes 1179656 | tf_op jit(solution)/shard_map/ppermute | solution.py:536
  22.5 12.5 %copy-start.2 = (bf16[8,512,128]{2,1,0:T(8,128)(2,1)S(1)}, bf16[8,512,128]{2,1,0:T(8,128)(2,1)}, u32[]{:S(2)}) copy-start(bf16[8,512,128]{2,1,0:T(8,128)(2,1)} %refs_2_.1) | copy-start | bytes 3145732
  24.4 15.3 %copy-start = (bf16[8,512,128]{2,1,0:T(8,128)(2,1)S(1)}, bf16[8,512,128]{2,1,0:T(8,128)(2,1)}, u32[]{:S(2)}) copy-start(bf16[8,512,128]{2,1,0:T(8,128)(2,1)} %value_up.7) | copy-start | bytes 3145732
  33.3 6.4 %collective-permute-start.2 = (bf16[768,640]{1,0:T(8,128)(2,1)S(1)}, bf16[768,640]{1,0:T(8,128)(2,1)S(1)}, u32[]{:S(2)}, u32[]{:S(2)}) collective-permute-start(bf16[768,640]{1,0:T(8,128)(2,1)S(1)} %build_keys.1.near), channel_id=1, source_target_pairs={{0,1},{1,0},{2,3},{3,2},{4,5},{5,4},{6,7},{7,6},{8,9},{9,8},{10,11... | collective-permute-start | bytes 2949128 | tf_op jit(solution)/shard_map/ppermute | solution.py:549
  37.6 8.0 %collective-permute-start.3 = (bf16[64,1536]{1,0:T(8,128)(2,1)S(1)}, bf16[64,1536]{1,0:T(8,128)(2,1)S(1)}, u32[]{:S(2)}, u32[]{:S(2)}) collective-permute-start(bf16[64,1536]{1,0:T(8,128)(2,1)S(1)} %get-tuple-element.46), channel_id=1, source_target_pairs={{2,0},{4,2},{6,4},{0,6},{3,1},{5,3},{7,5},{1,7},{10,8},{12,10},{14... | collective-permute-start | bytes 589832 | tf_op jit(solution)/shard_map/ppermute | solution.py:536
  39.7 7.3 %collective-permute-start.4 = (bf16[64,1536]{1,0:T(8,128)(2,1)S(1)}, bf16[64,1536]{1,0:T(8,128)(2,1)S(1)}, u32[]{:S(2)}, u32[]{:S(2)}) collective-permute-start(bf16[64,1536]{1,0:T(8,128)(2,1)S(1)} %get-tuple-element.47), channel_id=1, source_target_pairs={{6,0},{0,2},{2,4},{4,6},{7,1},{1,3},{3,5},{5,7},{14,8},{8,10},{10,... | collective-permute-start | bytes 589832 | tf_op jit(solution)/shard_map/ppermute | solution.py:536
  47.0 8.4 %collective-permute-start.5 = (bf16[128,1152]{1,0:T(8,128)(2,1)S(1)}, bf16[128,1152]{1,0:T(8,128)(2,1)S(1)}, u32[]{:S(2)}, u32[]{:S(2)}) collective-permute-start(bf16[128,1152]{1,0:T(8,128)(2,1)S(1)} %get-tuple-element.51), channel_id=1, source_target_pairs={{6,0},{0,2},{2,4},{4,6},{7,1},{1,3},{3,5},{5,7},{14,8},{8,10},{10,... | collective-permute-start | bytes 884744 | tf_op jit(solution)/shard_map/ppermute | solution.py:536
  55.4 7.5 %collective-permute-start.6 = (bf16[128,1152]{1,0:T(8,128)(2,1)S(1)}, bf16[128,1152]{1,0:T(8,128)(2,1)S(1)}, u32[]{:S(2)}, u32[]{:S(2)}) collective-permute-start(bf16[128,1152]{1,0:T(8,128)(2,1)S(1)} %attend_2.1), channel_id=1, source_target_pairs={{6,0},{0,2},{2,4},{4,6},{7,1},{1,3},{3,5},{5,7},{14,8},{8,10},{10,... | collective-permute-start | bytes 884744 | tf_op jit(solution)/shard_map/ppermute | solution.py:536
  55.4 23.0 %copy-start.7 = (bf16[704,2048]{1,0:T(8,128)(2,1)S(1)}, bf16[704,2048]{1,0:T(8,128)(2,1)}, u32[]{:S(2)}) copy-start(bf16[704,2048]{1,0:T(8,128)(2,1)} %w_down.1) | copy-start | bytes 8650756
  55.4 23.0 %copy-start.10 = (bf16[128,2048]{1,0:T(8,128)(2,1)S(1)}, bf16[128,2048]{1,0:T(8,128)(2,1)}, u32[]{:S(2)}) copy-start(bf16[128,2048]{1,0:T(8,128)(2,1)} %tokens.1) | copy-start | bytes 1572868
  62.9 8.6 %copy-start.3 = (bf16[1024,2048]{1,0:T(8,128)(2,1)S(1)}, bf16[1024,2048]{1,0:T(8,128)(2,1)}, u32[]{:S(2)}) copy-start(bf16[1024,2048]{1,0:T(8,128)(2,1)} %weight.1) | copy-start | bytes 12582916
  62.9 8.6 %collective-permute-start.7 = (bf16[128,1152]{1,0:T(8,128)(2,1)S(1)}, bf16[128,1152]{1,0:T(8,128)(2,1)S(1)}, u32[]{:S(2)}, u32[]{:S(2)}) collective-permute-start(bf16[128,1152]{1,0:T(8,128)(2,1)S(1)} %collective-permute-done.6), channel_id=1, source_target_pairs={{6,0},{0,2},{2,4},{4,6},{7,1},{1,3},{3,5},{5,7},{14,8},{8,10},{10,... | collective-permute-start | bytes 884744 | tf_op jit(solution)/shard_map/ppermute | solution.py:536
  62.9 8.6 %collective-permute-start.8 = (bf16[128,1152]{1,0:T(8,128)(2,1)S(1)}, bf16[128,1152]{1,0:T(8,128)(2,1)S(1)}, u32[]{:S(2)}, u32[]{:S(2)}) collective-permute-start(bf16[128,1152]{1,0:T(8,128)(2,1)S(1)} %attend_3.1), channel_id=1, source_target_pairs={{2,0},{4,2},{6,4},{0,6},{3,1},{5,3},{7,5},{1,7},{10,8},{12,10},{14... | collective-permute-start | bytes 884744 | tf_op jit(solution)/shard_map/ppermute | solution.py:536
  65.6 12.8 %copy-start.6 = (bf16[2048,704]{0,1:T(8,128)(2,1)S(1)}, bf16[2048,704]{0,1:T(8,128)(2,1)}, u32[]{:S(2)}) copy-start(bf16[2048,704]{0,1:T(8,128)(2,1)} %param.27) | copy-start | bytes 8650756
  71.5 6.9 %copy-start.5 = (bf16[2048,704]{0,1:T(8,128)(2,1)S(1)}, bf16[2048,704]{0,1:T(8,128)(2,1)}, u32[]{:S(2)}) copy-start(bf16[2048,704]{0,1:T(8,128)(2,1)} %param.26) | copy-start | bytes 8650756
  73.1 5.3 %collective-permute-start.9 = (bf16[128,2048]{1,0:T(8,128)(2,1)S(1)}, bf16[128,2048]{1,0:T(8,128)(2,1)S(1)}, u32[]{:S(2)}, u32[]{:S(2)}) collective-permute-start(bf16[128,2048]{1,0:T(8,128)(2,1)S(1)} %get-tuple-element.60), channel_id=1, source_target_pairs={{0,1},{1,0},{2,3},{3,2},{4,5},{5,4},{6,7},{7,6},{8,9},{9,8},{10,11... | collective-permute-start | bytes 1572872 | tf_op jit(solution)/shard_map/ppermute | solution.py:571
  81.0 1.6 %collective-permute-start.10 = (bf16[128,1024]{1,0:T(8,128)(2,1)S(1)}, bf16[128,1024]{1,0:T(8,128)(2,1)S(1)}, u32[]{:S(2)}, u32[]{:S(2)}) collective-permute-start(bf16[128,1024]{1,0:T(8,128)(2,1)S(1)} %get-tuple-element.62), channel_id=1, source_target_pairs={{0,1},{1,0},{2,3},{3,2},{4,5},{5,4},{6,7},{7,6},{8,9},{9,8},{10,11... | collective-permute-start | bytes 786440 | tf_op jit(solution)/shard_map/ppermute | solution.py:581
  (10 other events, 31.2 us)

commit v7 on v5

--- a/solution.py
+++ b/solution.py
@@ -28,6 +28,7 @@
 VMEM = pl.BlockSpec(memory_space=pltpu.VMEM)
 SMEM = pl.BlockSpec(memory_space=pltpu.SMEM)
 HBM = pl.BlockSpec(memory_space=pltpu.HBM)
+ANY = pl.BlockSpec(memory_space=pl.ANY)
 
 
 def params(mb):
@@ -242,7 +243,9 @@
     )(count, tokens, gain, table, w_query)
 
 
-def latent_kernel(normed, turns, w_latent_t, kv_gain, new_latent, span):
+def latent_kernel(
+    normed, turns, w_latent_t, kv_gain, query, key_up, new_latent, span, probes
+):
     cosine, sine = turns[:, :ROPE], turns[:, ROPE:]
     cosine = jnp.concatenate([cosine, cosine], axis=1)
     sine = jnp.concatenate([sine, sine], axis=1)
@@ -255,21 +258,23 @@
     lane = lax.broadcasted_iota(jnp.int32, turned.shape, 1)
     span[:, :KVR] = latent
     span[:, KVR:] = jnp.where(lane < ROPE, turned, 0.0).astype(BF16)
-
-
-def project_latent(normed, turns, w_latent_t, kv_gain):
+    fill_probes(query, key_up, probes)
+
+
+def project_latent(normed, turns, w_latent_t, kv_gain, query, key_up):
     rows = normed.shape[0]
     return pl.pallas_call(
         latent_kernel,
         out_shape=[
             jax.ShapeDtypeStruct((LAT, rows), BF16),
             jax.ShapeDtypeStruct((rows, WIDE), BF16),
+            jax.ShapeDtypeStruct((key_up.shape[0] * rows, WIDE), BF16),
         ],
-        in_specs=[VMEM] * 4,
-        out_specs=[VMEM] * 2,
-        compiler_params=params(16),
+        in_specs=[VMEM] * 6,
+        out_specs=[VMEM] * 3,
+        compiler_params=params(20),
         name="project_latent",
-    )(normed, turns, w_latent_t, kv_gain)
+    )(normed, turns, w_latent_t, kv_gain, query, key_up)
 
 
 def fill_probes(query, key_up, probes):
@@ -293,26 +298,30 @@
         probes[at, KVR:] = jnp.where(rope_lanes < ROPE, pair, one).astype(BF16)
 
 
-def probes_kernel(key_up, own, ahead, behind, own_probes, ahead_probes, behind_probes, low, high):
-    cut = low.shape[0]
-    low[...] = ahead[:cut, :]
-    high[...] = behind[cut:, :]
-    for query, probes in ((own, own_probes), (ahead, ahead_probes), (behind, behind_probes)):
+def probes_kernel(key_up, ahead_src, behind_src, ahead_probes, behind_probes, ahead, behind, sems):
+    pairs = ((ahead_src, ahead), (behind_src, behind))
+    copies = [
+        pltpu.make_async_copy(src, dst, sems.at[i]) for i, (src, dst) in enumerate(pairs)
+    ]
+    for copy in copies:
+        copy.start()
+    for copy, query, probes in zip(copies, (ahead, behind), (ahead_probes, behind_probes)):
+        copy.wait()
         fill_probes(query, key_up, probes)
 
 
-def make_probes(key_up, own, ahead, behind):
-    rows, width = own.shape
+def make_probes(key_up, ahead, behind):
+    rows, width = ahead.shape
     probes = jax.ShapeDtypeStruct((key_up.shape[0] * rows, WIDE), BF16)
-    half = jax.ShapeDtypeStruct((rows // 2, width), BF16)
     return pl.pallas_call(
         probes_kernel,
-        out_shape=[probes] * 3 + [half] * 2,
-        in_specs=[VMEM] * 4,
-        out_specs=[VMEM] * 5,
-        compiler_params=params(16),
+        out_shape=[probes] * 2,
+        in_specs=[VMEM] + [ANY] * 2,
+        out_specs=[VMEM] * 2,
+        scratch_shapes=[pltpu.VMEM((rows, width), BF16)] * 2 + [pltpu.SemaphoreType.DMA((2,))],
+        compiler_params=params(20),
         name="make_probes",
-    )(key_up, own, ahead, behind)
+    )(key_up, ahead, behind)
 
 
 def attend_kernel(by, keep_far, value_up, near, arrived, span, *refs):
@@ -538,18 +547,20 @@
         fetch_count, early_tokens, attn_gain, jnp.asarray(table), w_query
     )
     next_query, last_query = shift(query, 1), shift(query, -1)
-    new_latent, span = project_latent(normed, turns, w_latent.T, kv_gain)
+    new_latent, span, own_probes = project_latent(
+        normed, turns, w_latent.T, kv_gain, query, w_key_up
+    )
     arrived, next_query, last_query, span = lax.optimization_barrier(
         (arrived, next_query, last_query, span)
     )
 
+    cut = rows // 2
+    far_low, far_high = shift(next_query[:cut], 1), shift(last_query[cut:], -1)
+
     near = build_keys(owner, fetch_count, arrived)
     far = lax.ppermute(near, "tp", swap)
 
-    own_probes, next_probes, last_probes, low, high = make_probes(
-        w_key_up, query, next_query, last_query
-    )
-    far_low, far_high = shift(low, 1), shift(high, -1)
+    next_probes, last_probes = make_probes(w_key_up, next_query, last_query)
 
     def partial_for(by, far, *queries, **flags):
         return attend(by, w_value_up, near, far, span, *queries, **flags)

time: 82.8 us -> 82.1 us (level)
  waiting for transfers between devices: 11.2 us -> 9.78 us
    ppermute x8, waiting for transfers between devices: 8.49 us -> 7.08 us  [shift(): return lax.ppermute(value, 'section', pairs)]
    ppermute x1, starting transfers between devices: 3.75 us -> 2.69 us  [on_device(): incoming = lax.ppermute(send, 'tp', swap)]
    ppermute x1, starting transfers between devices: 1.63 us -> 2.59 us  [on_device(): far = lax.ppermute(near, 'tp', swap)]
    unnamed x38 -> x34, local copies, waits for them, and re-layouts: 6.08 us -> 5.68 us
  transfers between devices with their start and end apart: 12 -> 12, of which waited for: 6 -> 5; matrix products, arithmetic and copies ran while one was open for 0% -> 0% of each run, Pallas kernels for 39% -> 39%
where the time goes in v7:
time: 82.1 us; the launch traced here: 81.7 us
  Pallas kernels  40.5 us (49%)
  starting transfers between devices  24.1 us (29%)
  waiting for transfers between devices  9.78 us (12%)
  local copies, waits for them, and re-layouts  5.71 us (7%)
  between operations  0.89 us (1%)
    pallas_call x4, Pallas kernels, attend(): pl.pallas_call(functools.partial(attend_kernel, by, keep_far), out_shape=...  23.7 us
    ppermute x8, starting transfers between devices, shift(): return lax.ppermute(value, 'section', pairs)  10.8 us
    all_to_all x1, starting transfers between devices, on_device(): lax.all_to_all(outgoing, 'store', split_axis=0, concat_axis=0, tiled=True)  7.6 us
    ppermute x8, waiting for transfers between devices, shift(): return lax.ppermute(value, 'section', pairs)  7.08 us
    unnamed x34, local copies, waits for them, and re-layouts  5.68 us
    pallas_call x1, Pallas kernels, project(): pl.pallas_call(project_kernel, out_shape=[jax.ShapeDtypeStruct((rows, col...  5.11 us
    pallas_call x1, Pallas kernels, pack_pages(): pl.pallas_call(pack_kernel, out_shape=jax.ShapeDtypeStruct((n_store, rows...  3.3 us
    ppermute x1, starting transfers between devices, on_device(): incoming = lax.ppermute(send, 'tp', swap)  2.69 us
  transfers between devices with their start and end apart: 12, of which 5 were waited for; matrix products, arithmetic and copies ran while one was open for 0% of the time, Pallas kernels for 39%

profile of v7, /device:TPU:1, one launch (start us, length us, event | category | flops | bytes accessed | tf_op | source)
XLA Modules:
  0.0 81.7 jit_solution(7970394684391348979)
XLA Ops:
  0.6 3.3 %pack_pages.1 = bf16[16,32,1152]{2,1,0:T(8,128)(2,1)} custom-call(s32[16,24]{1,0:T(8,128)} %bitcast.12, s32[16,24]{1,0:T(8,128)} %slot_src.1, bf16[8,576,256]{2,1,0:T(8,128)(2,1)} %bitcast.15), custom_call_target="tpu_custom_call" | custom-call | tf_op jit(solution)/shard_map/pack_pages/pallas_call | solution.py:126
  3.9 7.6 %all-to-all-start = ((bf16[16,2,16,1152]{3,2,1,0:T(8,128)(2,1)}), bf16[16,2,16,1152]{3,2,1,0:T(8,128)(2,1)S(1)}, u32[]{:S(2)}, u32[]{:S(2)}) async-start(bf16[16,2,16,1152]{3,2,1,0:T(8,128)(2,1)} %bitcast.14), calls=%async_computation | async-start | bytes 2359296 | tf_op jit(solution)/shard_map/all_to_all | solution.py:538
  11.6 5.1 %project.1 = (bf16[128,1536]{1,0:T(8,128)(2,1)}, bf16[128,2048]{1,0:T(8,128)(2,1)}, f32[128,128]{1,0:T(8,128)}) custom-call(s32[16]{0:T(128)} %count.3, bf16[128,2048]{1,0:T(8,128)(2,1)} %tokens.1, bf16[2048]{0:T(1024)(128)(2,1)} %gain.2, f32[6656,128]{1,0:T(8,128)} %constant.2.clone.table, bf16[2048,1536]{1,0:T(8,128)(2,1)} %w_query_src.1), custom_call_target="tpu_custom_call" | custom-call | tf_op jit(solution)/shard_map/project/pallas_call | solution.py:226
  16.7 1.7 %collective-permute-start.1 = (bf16[128,1536]{1,0:T(8,128)(2,1)}, bf16[128,1536]{1,0:T(8,128)(2,1)S(1)}, u32[]{:S(2)}, u32[]{:S(2)}) collective-permute-start(bf16[128,1536]{1,0:T(8,128)(2,1)} %get-tuple-element.33.query), channel_id=1, source_target_pairs={{6,0},{0,2},{2,4},{4,6},{7,1},{1,3},{3,5},{5,7},{14,8},{8,10},{10,... | collective-permute-start | bytes 1179656 | tf_op jit(solution)/shard_map/ppermute | solution.py:543
  18.4 2.2 %collective-permute-start = (bf16[128,1536]{1,0:T(8,128)(2,1)}, bf16[128,1536]{1,0:T(8,128)(2,1)S(1)}, u32[]{:S(2)}, u32[]{:S(2)}) collective-permute-start(bf16[128,1536]{1,0:T(8,128)(2,1)} %get-tuple-element.33.query), channel_id=1, source_target_pairs={{2,0},{4,2},{6,4},{0,6},{3,1},{5,3},{7,5},{1,7},{10,8},{12,10},{14... | collective-permute-start | bytes 1179656 | tf_op jit(solution)/shard_map/ppermute | solution.py:543
  20.6 1.7 %copy-done.6 = bf16[2048,576]{0,1:T(8,128)(2,1)S(1)} copy-done((bf16[2048,576]{0,1:T(8,128)(2,1)S(1)}, bf16[2048,576]{0,1:T(8,128)(2,1)}, u32[]{:S(2)}) %copy-start.6) | copy-done | bytes 2359320
  25.2 2.0 %project_latent.1 = (bf16[576,128]{1,0:T(8,128)(2,1)}, bf16[128,640]{1,0:T(8,128)(2,1)S(1)}, bf16[1024,640]{1,0:T(8,128)(2,1)S(1)}) custom-call(bf16[128,2048]{1,0:T(8,128)(2,1)S(1)} %copy-done.10, f32[128,128]{1,0:T(8,128)S(1)} %copy-done.12, bf16[576,2048]{1,0:T(8,128)(2,1)S(1)} %bitcast.11, bf16[512]{0:T(512)(128)(2,1)S(1)} %copy-done.16, ...), custom_call_target="tpu_custom_call" | custom-call | tf_op jit(solution)/shard_map/project_latent/pallas_call | solution.py:266
  27.2 1.1 %copy-done.8 = bf16[1024,640]{1,0:T(8,128)(2,1)} copy-done((bf16[1024,640]{1,0:T(8,128)(2,1)}, bf16[1024,640]{1,0:T(8,128)(2,1)S(1)}, u32[]{:S(2)}) %copy-start.8) | copy-done | bytes 1310744
  30.2 2.6 %collective-permute-start.2 = (bf16[768,640]{1,0:T(8,128)(2,1)S(1)}, bf16[768,640]{1,0:T(8,128)(2,1)S(1)}, u32[]{:S(2)}, u32[]{:S(2)}) collective-permute-start(bf16[768,640]{1,0:T(8,128)(2,1)S(1)} %build_keys.1.near), channel_id=1, source_target_pairs={{0,1},{1,0},{2,3},{3,2},{4,5},{5,4},{6,7},{7,6},{8,9},{9,8},{10,11... | collective-permute-start | bytes 2949128 | tf_op jit(solution)/shard_map/ppermute | solution.py:561
  32.8 1.7 %collective-permute-start.4 = (bf16[64,1536]{1,0:T(8,128)(2,1)S(1)}, bf16[64,1536]{1,0:T(8,128)(2,1)S(1)}, u32[]{:S(2)}, u32[]{:S(2)}) collective-permute-start(bf16[64,1536]{1,0:T(8,128)(2,1)S(1)} %slice.7), channel_id=1, source_target_pairs={{6,0},{0,2},{2,4},{4,6},{7,1},{1,3},{3,5},{5,7},{14,8},{8,10},{10,... | collective-permute-start | bytes 589832 | tf_op jit(solution)/shard_map/ppermute | solution.py:543
  34.5 2.2 %collective-permute-start.3 = (bf16[64,1536]{1,0:T(8,128)(2,1)S(1)}, bf16[64,1536]{1,0:T(8,128)(2,1)S(1)}, u32[]{:S(2)}, u32[]{:S(2)}) collective-permute-start(bf16[64,1536]{1,0:T(8,128)(2,1)S(1)} %slice.6), channel_id=1, source_target_pairs={{2,0},{4,2},{6,4},{0,6},{3,1},{5,3},{7,5},{1,7},{10,8},{12,10},{14... | collective-permute-start | bytes 589832 | tf_op jit(solution)/shard_map/ppermute | solution.py:543
  36.7 1.3 %make_probes.1 = (bf16[1024,640]{1,0:T(8,128)(2,1)S(1)}, bf16[1024,640]{1,0:T(8,128)(2,1)S(1)}) custom-call(bf16[8,512,128]{2,1,0:T(8,128)(2,1)S(1)} %copy-done.1, bf16[128,1536]{1,0:T(8,128)(2,1)S(1)} %collective-permute-done.ahead_src, bf16[128,1536]{1,0:T(8,128)(2,1)S(1)} %collective-permute-done.1.behind_src), custom_call_target="tpu_custom_call" | custom-call | tf_op jit(solution)/shard_map/make_probes/pallas_call | solution.py:316
  38.1 5.9 %attend_1.1 = (bf16[128,1152]{1,0:T(8,128)(2,1)S(1)}, bf16[768,640]{1,0:T(8,128)(2,1)S(1)}) custom-call(bf16[8,512,128]{2,1,0:T(8,128)(2,1)S(1)} %copy-done, bf16[768,640]{1,0:T(8,128)(2,1)S(1)} %build_keys.1.near, bf16[768,640]{1,0:T(8,128)(2,1)S(1)} %collective-permute-done.2.arrived, bf16[128,640]{1,0:T(8,128)(2,1)S(1)} %get-tuple-element.38.span, ...), custom_call_target="tpu_custom_call" | custom-call | tf_op jit(solution)/shard_map/attend_1/pallas_call | solution.py:421
  44.2 6.1 %attend_2.1 = bf16[128,1152]{1,0:T(8,128)(2,1)S(1)} custom-call(bf16[8,512,128]{2,1,0:T(8,128)(2,1)S(1)} %copy-done, bf16[768,640]{1,0:T(8,128)(2,1)S(1)} %build_keys.1.near, bf16[768,640]{1,0:T(8,128)(2,1)S(1)} %get-tuple-element.42.arrived, bf16[128,640]{1,0:T(8,128)(2,1)S(1)} %get-tuple-element.38.span, ...), custom_call_target="tpu_custom_call" | custom-call | tf_op jit(solution)/shard_map/attend_2/pallas_call | solution.py:421
  50.4 3.3 %collective-permute-done.5.one = bf16[128,1152]{1,0:T(8,128)(2,1)S(1)} collective-permute-done((bf16[128,1152]{1,0:T(8,128)(2,1)S(1)}, bf16[128,1152]{1,0:T(8,128)(2,1)S(1)}, u32[]{:S(2)}, u32[]{:S(2)}) %collective-permute-start.5) | collective-permute-done | bytes 294944 | tf_op jit(solution)/shard_map/ppermute | solution.py:543
  53.7 5.9 %attend_3.1 = bf16[128,1152]{1,0:T(8,128)(2,1)S(1)} custom-call(bf16[8,512,128]{2,1,0:T(8,128)(2,1)S(1)} %copy-done, bf16[768,640]{1,0:T(8,128)(2,1)S(1)} %build_keys.1.near, bf16[768,640]{1,0:T(8,128)(2,1)S(1)} %get-tuple-element.42.arrived, bf16[128,640]{1,0:T(8,128)(2,1)S(1)} %get-tuple-element.38.span, bf16[1024,640]{1,0:T(8,128)(2,1)S(1)} %get-tuple-element.48.refs_0_), custom_call_target="tpu_custom_call" | custom-call | tf_op jit(solution)/shard_map/attend_3/pallas_call | solution.py:421
  59.6 2.7 %collective-permute-done.6 = bf16[128,1152]{1,0:T(8,128)(2,1)S(1)} collective-permute-done((bf16[128,1152]{1,0:T(8,128)(2,1)S(1)}, bf16[128,1152]{1,0:T(8,128)(2,1)S(1)}, u32[]{:S(2)}, u32[]{:S(2)}) %collective-permute-start.6) | collective-permute-done | bytes 294944 | tf_op jit(solution)/shard_map/ppermute | solution.py:543
  62.3 2.7 %collective-permute-start.8 = (bf16[128,1152]{1,0:T(8,128)(2,1)S(1)}, bf16[128,1152]{1,0:T(8,128)(2,1)S(1)}, u32[]{:S(2)}, u32[]{:S(2)}) collective-permute-start(bf16[128,1152]{1,0:T(8,128)(2,1)S(1)} %attend_3.1), channel_id=1, source_target_pairs={{2,0},{4,2},{6,4},{0,6},{3,1},{5,3},{7,5},{1,7},{10,8},{12,10},{14... | collective-permute-start | bytes 884744 | tf_op jit(solution)/shard_map/ppermute | solution.py:543
  65.0 5.9 %attend_0.1.own = bf16[128,1152]{1,0:T(8,128)(2,1)S(1)} custom-call(bf16[8,512,128]{2,1,0:T(8,128)(2,1)S(1)} %copy-done, bf16[768,640]{1,0:T(8,128)(2,1)S(1)} %build_keys.1.near, bf16[768,640]{1,0:T(8,128)(2,1)S(1)} %get-tuple-element.42.arrived, bf16[128,640]{1,0:T(8,128)(2,1)S(1)} %get-tuple-element.38.span, bf16[1024,640]{1,0:T(8,128)(2,1)S(1)} %copy-done.9), custom_call_target="tpu_custom_call" | custom-call | tf_op jit(solution)/shard_map/attend_0/pallas_call | solution.py:421
  70.9 1.5 %project_output.1 = (f32[128,2048]{1,0:T(8,128)S(1)}, bf16[128,2048]{1,0:T(8,128)(2,1)S(1)}) custom-call(bf16[128,1152]{1,0:T(8,128)(2,1)S(1)} %attend_0.1.own, bf16[128,1152]{1,0:T(8,128)(2,1)S(1)} %collective-permute-done.5.one, bf16[128,1152]{1,0:T(8,128)(2,1)S(1)} %collective-permute-done.7.two, bf16[128,1152]{1,0:T(8,128)(2,1)S(1)} %collective-permute-done.8.three, ...), custom_call_target="tpu_custom_call" | custom-call | tf_op jit(solution)/shard_map/project_output/pallas_call | solution.py:465
  72.5 2.7 %collective-permute-start.9 = (bf16[128,2048]{1,0:T(8,128)(2,1)S(1)}, bf16[128,2048]{1,0:T(8,128)(2,1)S(1)}, u32[]{:S(2)}, u32[]{:S(2)}) collective-permute-start(bf16[128,2048]{1,0:T(8,128)(2,1)S(1)} %get-tuple-element.56), channel_id=1, source_target_pairs={{0,1},{1,0},{2,3},{3,2},{4,5},{5,4},{6,7},{7,6},{8,9},{9,8},{10,11... | collective-permute-start | bytes 1572872 | tf_op jit(solution)/shard_map/ppermute | solution.py:580
  75.1 1.5 %collective-permute-done.9.other = bf16[128,2048]{1,0:T(8,128)(2,1)S(1)} collective-permute-done((bf16[128,2048]{1,0:T(8,128)(2,1)S(1)}, bf16[128,2048]{1,0:T(8,128)(2,1)S(1)}, u32[]{:S(2)}, u32[]{:S(2)}) %collective-permute-start.9) | collective-permute-done | bytes 524320 | tf_op jit(solution)/shard_map/ppermute | solution.py:580
  76.7 2.6 %expert.1 = (f32[128,1024]{1,0:T(8,128)S(1)}, bf16[128,1024]{1,0:T(8,128)(2,1)S(1)}) custom-call(bf16[128,2048]{1,0:T(8,128)(2,1)S(1)} %copy-done.7, f32[128,2048]{1,0:T(8,128)S(1)} %get-tuple-element.55.exact, bf16[128,2048]{1,0:T(8,128)(2,1)S(1)} %collective-permute-done.9.other, bf16[2048]{0:T(1024)(128)(2,1)S(1)} %copy-done.14, ...), custom_call_target="tpu_custom_call" | custom-call | tf_op jit(solution)/shard_map/expert/pallas_call | solution.py:496
  79.8 1.2 %collective-permute-done.10 = bf16[128,1024]{1,0:T(8,128)(2,1)S(1)} collective-permute-done((bf16[128,1024]{1,0:T(8,128)(2,1)S(1)}, bf16[128,1024]{1,0:T(8,128)(2,1)S(1)}, u32[]{:S(2)}, u32[]{:S(2)}) %collective-permute-start.10) | collective-permute-done | bytes 262176 | tf_op jit(solution)/shard_map/ppermute | solution.py:590
  (48 shorter events, 6.4 us)
Async XLA Ops:
  3.9 25.3 %all-to-all-start = ((bf16[16,2,16,1152]{3,2,1,0:T(8,128)(2,1)}), bf16[16,2,16,1152]{3,2,1,0:T(8,128)(2,1)S(1)}, u32[]{:S(2)}, u32[]{:S(2)}) async-start(bf16[16,2,16,1152]{3,2,1,0:T(8,128)(2,1)} %bitcast.14), calls=%async_computation | async-start | bytes 2359296 | tf_op jit(solution)/shard_map/all_to_all | solution.py:538
  11.5 9.1 %copy-start.1 = (bf16[8,512,128]{2,1,0:T(8,128)(2,1)S(1)}, bf16[8,512,128]{2,1,0:T(8,128)(2,1)}, u32[]{:S(2)}) copy-start(bf16[8,512,128]{2,1,0:T(8,128)(2,1)} %refs_2_.1) | copy-start | bytes 3145732
  11.5 9.1 %copy-start.16 = (bf16[512]{0:T(512)(128)(2,1)S(1)}, bf16[512]{0:T(512)(128)(2,1)}, u32[]{:S(2)}) copy-start(bf16[512]{0:T(512)(128)(2,1)} %kv_gain.1) | copy-start | bytes 3076
  11.6 17.7 %copy-start.13 = (s32[16,24,1]{1,2,0:T(1,128)S(1)}, s32[16,24,1]{1,2,0:T(1,128)}, u32[]{:S(2)}) copy-start(s32[16,24,1]{1,2,0:T(1,128)} %param.30) | copy-start | bytes 4612
  16.7 12.6 %copy-start.15 = (s32[16]{0:T(128)S(1)}, s32[16]{0:T(128)}, u32[]{:S(2)}) copy-start(s32[16]{0:T(128)} %count.3) | copy-start | bytes 196
  16.7 12.6 %collective-permute-start.1 = (bf16[128,1536]{1,0:T(8,128)(2,1)}, bf16[128,1536]{1,0:T(8,128)(2,1)S(1)}, u32[]{:S(2)}, u32[]{:S(2)}) collective-permute-start(bf16[128,1536]{1,0:T(8,128)(2,1)} %get-tuple-element.33.query), channel_id=1, source_target_pairs={{6,0},{0,2},{2,4},{4,6},{7,1},{1,3},{3,5},{5,7},{14,8},{8,10},{10,... | collective-permute-start | bytes 1179656 | tf_op jit(solution)/shard_map/ppermute | solution.py:543
  18.4 10.9 %collective-permute-start = (bf16[128,1536]{1,0:T(8,128)(2,1)}, bf16[128,1536]{1,0:T(8,128)(2,1)S(1)}, u32[]{:S(2)}, u32[]{:S(2)}) collective-permute-start(bf16[128,1536]{1,0:T(8,128)(2,1)} %get-tuple-element.33.query), channel_id=1, source_target_pairs={{2,0},{4,2},{6,4},{0,6},{3,1},{5,3},{7,5},{1,7},{10,8},{12,10},{14... | collective-permute-start | bytes 1179656 | tf_op jit(solution)/shard_map/ppermute | solution.py:543
  29.3 8.8 %copy-start = (bf16[8,512,128]{2,1,0:T(8,128)(2,1)S(1)}, bf16[8,512,128]{2,1,0:T(8,128)(2,1)}, u32[]{:S(2)}) copy-start(bf16[8,512,128]{2,1,0:T(8,128)(2,1)} %value_up.7) | copy-start | bytes 3145732
  30.2 7.9 %collective-permute-start.2 = (bf16[768,640]{1,0:T(8,128)(2,1)S(1)}, bf16[768,640]{1,0:T(8,128)(2,1)S(1)}, u32[]{:S(2)}, u32[]{:S(2)}) collective-permute-start(bf16[768,640]{1,0:T(8,128)(2,1)S(1)} %build_keys.1.near), channel_id=1, source_target_pairs={{0,1},{1,0},{2,3},{3,2},{4,5},{5,4},{6,7},{7,6},{8,9},{9,8},{10,11... | collective-permute-start | bytes 2949128 | tf_op jit(solution)/shard_map/ppermute | solution.py:561
  32.8 11.1 %collective-permute-start.4 = (bf16[64,1536]{1,0:T(8,128)(2,1)S(1)}, bf16[64,1536]{1,0:T(8,128)(2,1)S(1)}, u32[]{:S(2)}, u32[]{:S(2)}) collective-permute-start(bf16[64,1536]{1,0:T(8,128)(2,1)S(1)} %slice.7), channel_id=1, source_target_pairs={{6,0},{0,2},{2,4},{4,6},{7,1},{1,3},{3,5},{5,7},{14,8},{8,10},{10,... | collective-permute-start | bytes 589832 | tf_op jit(solution)/shard_map/ppermute | solution.py:543
  34.5 9.4 %collective-permute-start.3 = (bf16[64,1536]{1,0:T(8,128)(2,1)S(1)}, bf16[64,1536]{1,0:T(8,128)(2,1)S(1)}, u32[]{:S(2)}, u32[]{:S(2)}) collective-permute-start(bf16[64,1536]{1,0:T(8,128)(2,1)S(1)} %slice.6), channel_id=1, source_target_pairs={{2,0},{4,2},{6,4},{0,6},{3,1},{5,3},{7,5},{1,7},{10,8},{12,10},{14... | collective-permute-start | bytes 589832 | tf_op jit(solution)/shard_map/ppermute | solution.py:543
  44.0 9.8 %collective-permute-start.5 = (bf16[128,1152]{1,0:T(8,128)(2,1)S(1)}, bf16[128,1152]{1,0:T(8,128)(2,1)S(1)}, u32[]{:S(2)}, u32[]{:S(2)}) collective-permute-start(bf16[128,1152]{1,0:T(8,128)(2,1)S(1)} %get-tuple-element.47), channel_id=1, source_target_pairs={{6,0},{0,2},{2,4},{4,6},{7,1},{1,3},{3,5},{5,7},{14,8},{8,10},{10,... | collective-permute-start | bytes 884744 | tf_op jit(solution)/shard_map/ppermute | solution.py:543
  53.7 11.3 %copy-start.9 = (bf16[1024,640]{1,0:T(8,128)(2,1)S(1)}, bf16[1024,640]{1,0:T(8,128)(2,1)}, u32[]{:S(2)}) copy-start(bf16[1024,640]{1,0:T(8,128)(2,1)} %copy-done.8) | copy-start | bytes 3932164
  53.7 8.6 %collective-permute-start.6 = (bf16[128,1152]{1,0:T(8,128)(2,1)S(1)}, bf16[128,1152]{1,0:T(8,128)(2,1)S(1)}, u32[]{:S(2)}, u32[]{:S(2)}) collective-permute-start(bf16[128,1152]{1,0:T(8,128)(2,1)S(1)} %attend_2.1), channel_id=1, source_target_pairs={{6,0},{0,2},{2,4},{4,6},{7,1},{1,3},{3,5},{5,7},{14,8},{8,10},{10,... | collective-permute-start | bytes 884744 | tf_op jit(solution)/shard_map/ppermute | solution.py:543
  53.7 23.0 %copy-start.5 = (bf16[704,2048]{1,0:T(8,128)(2,1)S(1)}, bf16[704,2048]{1,0:T(8,128)(2,1)}, u32[]{:S(2)}) copy-start(bf16[704,2048]{1,0:T(8,128)(2,1)} %w_down.1) | copy-start | bytes 8650756
  53.7 23.0 %copy-start.7 = (bf16[128,2048]{1,0:T(8,128)(2,1)S(1)}, bf16[128,2048]{1,0:T(8,128)(2,1)}, u32[]{:S(2)}) copy-start(bf16[128,2048]{1,0:T(8,128)(2,1)} %tokens.1) | copy-start | bytes 1572868
  62.3 8.6 %copy-start.2 = (bf16[1024,2048]{1,0:T(8,128)(2,1)S(1)}, bf16[1024,2048]{1,0:T(8,128)(2,1)}, u32[]{:S(2)}) copy-start(bf16[1024,2048]{1,0:T(8,128)(2,1)} %weight.1) | copy-start | bytes 12582916
  62.3 8.6 %collective-permute-start.7 = (bf16[128,1152]{1,0:T(8,128)(2,1)S(1)}, bf16[128,1152]{1,0:T(8,128)(2,1)S(1)}, u32[]{:S(2)}, u32[]{:S(2)}) collective-permute-start(bf16[128,1152]{1,0:T(8,128)(2,1)S(1)} %collective-permute-done.6), channel_id=1, source_target_pairs={{6,0},{0,2},{2,4},{4,6},{7,1},{1,3},{3,5},{5,7},{14,8},{8,10},{10,... | collective-permute-start | bytes 884744 | tf_op jit(solution)/shard_map/ppermute | solution.py:543
  62.3 8.6 %collective-permute-start.8 = (bf16[128,1152]{1,0:T(8,128)(2,1)S(1)}, bf16[128,1152]{1,0:T(8,128)(2,1)S(1)}, u32[]{:S(2)}, u32[]{:S(2)}) collective-permute-start(bf16[128,1152]{1,0:T(8,128)(2,1)S(1)} %attend_3.1), channel_id=1, source_target_pairs={{2,0},{4,2},{6,4},{0,6},{3,1},{5,3},{7,5},{1,7},{10,8},{12,10},{14... | collective-permute-start | bytes 884744 | tf_op jit(solution)/shard_map/ppermute | solution.py:543
  65.0 11.7 %copy-start.4 = (bf16[2048,704]{0,1:T(8,128)(2,1)S(1)}, bf16[2048,704]{0,1:T(8,128)(2,1)}, u32[]{:S(2)}) copy-start(bf16[2048,704]{0,1:T(8,128)(2,1)} %param.27) | copy-start | bytes 8650756
  70.8 5.8 %copy-start.3 = (bf16[2048,704]{0,1:T(8,128)(2,1)S(1)}, bf16[2048,704]{0,1:T(8,128)(2,1)}, u32[]{:S(2)}) copy-start(bf16[2048,704]{0,1:T(8,128)(2,1)} %param.26) | copy-start | bytes 8650756
  70.9 5.8 %copy-start.14 = (bf16[2048]{0:T(1024)(128)(2,1)S(1)}, bf16[2048]{0:T(1024)(128)(2,1)}, u32[]{:S(2)}) copy-start(bf16[2048]{0:T(1024)(128)(2,1)} %gain.3) | copy-start | bytes 12292
  72.5 4.2 %collective-permute-start.9 = (bf16[128,2048]{1,0:T(8,128)(2,1)S(1)}, bf16[128,2048]{1,0:T(8,128)(2,1)S(1)}, u32[]{:S(2)}, u32[]{:S(2)}) collective-permute-start(bf16[128,2048]{1,0:T(8,128)(2,1)S(1)} %get-tuple-element.56), channel_id=1, source_target_pairs={{0,1},{1,0},{2,3},{3,2},{4,5},{5,4},{6,7},{7,6},{8,9},{9,8},{10,11... | collective-permute-start | bytes 1572872 | tf_op jit(solution)/shard_map/ppermute | solution.py:580
  79.3 1.6 %collective-permute-start.10 = (bf16[128,1024]{1,0:T(8,128)(2,1)S(1)}, bf16[128,1024]{1,0:T(8,128)(2,1)S(1)}, u32[]{:S(2)}, u32[]{:S(2)}) collective-permute-start(bf16[128,1024]{1,0:T(8,128)(2,1)S(1)} %get-tuple-element.58), channel_id=1, source_target_pairs={{0,1},{1,0},{2,3},{3,2},{4,5},{5,4},{6,7},{7,6},{8,9},{9,8},{10,11... | collective-permute-start | bytes 786440 | tf_op jit(solution)/shard_map/ppermute | solution.py:590
  (5 other events, 5.6 us)

commit v8 on v7

--- a/solution.py
+++ b/solution.py
@@ -298,44 +298,28 @@
         probes[at, KVR:] = jnp.where(rope_lanes < ROPE, pair, one).astype(BF16)
 
 
-def probes_kernel(key_up, ahead_src, behind_src, ahead_probes, behind_probes, ahead, behind, sems):
-    pairs = ((ahead_src, ahead), (behind_src, behind))
-    copies = [
-        pltpu.make_async_copy(src, dst, sems.at[i]) for i, (src, dst) in enumerate(pairs)
-    ]
-    for copy in copies:
-        copy.start()
-    for copy, query, probes in zip(copies, (ahead, behind), (ahead_probes, behind_probes)):
-        copy.wait()
-        fill_probes(query, key_up, probes)
-
-
-def make_probes(key_up, ahead, behind):
-    rows, width = ahead.shape
-    probes = jax.ShapeDtypeStruct((key_up.shape[0] * rows, WIDE), BF16)
-    return pl.pallas_call(
-        probes_kernel,
-        out_shape=[probes] * 2,
-        in_specs=[VMEM] + [ANY] * 2,
-        out_specs=[VMEM] * 2,
-        scratch_shapes=[pltpu.VMEM((rows, width), BF16)] * 2 + [pltpu.SemaphoreType.DMA((2,))],
-        compiler_params=params(20),
-        name="make_probes",
-    )(key_up, ahead, behind)
-
-
 def attend_kernel(by, keep_far, value_up, near, arrived, span, *refs):
     far = arrived
-    if by == 2:
-        low, high, key_up, out, query, probes = refs
-        query[: low.shape[0], :] = low[...]
-        query[low.shape[0] :, :] = high[...]
+    if by == 0:
+        probes, out = refs
+    else:
+        count = 2 if by == 2 else 1
+        parts, (key_up, out), refs = refs[:count], refs[count : count + 2], refs[count + 2 :]
+        if keep_far:
+            far, refs = refs[0], refs[1:]
+        query, probes, sems = refs
+        height = query.shape[0] // count
+        copies = [
+            pltpu.make_async_copy(part, query.at[pl.ds(k * height, height), :], sems.at[k])
+            for k, part in enumerate(parts)
+        ]
+        for copy in copies:
+            copy.start()
+        if keep_far:
+            far[...] = arrived[...]
+        for copy in copies:
+            copy.wait()
         fill_probes(query, key_up, probes)
-    elif keep_far:
-        probes, out, far = refs
-        far[...] = arrived[...]
-    else:
-        probes, out = refs
     n_head, rows = value_up.shape[0], out.shape[0]
     blocks = (near, far, span)
     lane = lax.broadcasted_iota(jnp.int32, (rows, 128), 1)
@@ -414,14 +398,18 @@
     out_shape = [jax.ShapeDtypeStruct((rows, n_head * VDIM + 128), BF16)]
     if keep_far:
         out_shape.append(jax.ShapeDtypeStruct(far.shape, BF16))
-    scratch = []
-    if by == 2:
-        scratch.append(pltpu.VMEM((rows, queries[0].shape[1]), BF16))
-        scratch.append(pltpu.VMEM((n_head * rows, WIDE), BF16))
+    specs, scratch = [VMEM], []
+    if by != 0:
+        specs = [ANY] * (len(queries) - 1) + [VMEM]
+        scratch = [
+            pltpu.VMEM((rows, queries[0].shape[1]), BF16),
+            pltpu.VMEM((n_head * rows, WIDE), BF16),
+            pltpu.SemaphoreType.DMA((2,)),
+        ]
     return pl.pallas_call(
         functools.partial(attend_kernel, by, keep_far),
         out_shape=out_shape,
-        in_specs=[VMEM] * (4 + len(queries)),
+        in_specs=[VMEM] * 4 + specs,
         out_specs=[VMEM] * len(out_shape),
         scratch_shapes=scratch,
         compiler_params=params(32),
@@ -560,18 +548,17 @@
     near = build_keys(owner, fetch_count, arrived)
     far = lax.ppermute(near, "tp", swap)
 
-    next_probes, last_probes = make_probes(w_key_up, next_query, last_query)
 
     def partial_for(by, far, *queries, **flags):
         return attend(by, w_value_up, near, far, span, *queries, **flags)
 
-    one, far = partial_for(1, far, next_probes, keep_far=True)
+    one, far = partial_for(1, far, next_query, w_key_up, keep_far=True)
     one, far_low, far_high = lax.optimization_barrier((one, far_low, far_high))
     one = shift(one, -1)
     (two,) = partial_for(2, far, far_low, far_high, w_key_up)
-    two, last_probes, one = lax.optimization_barrier((two, last_probes, one))
+    two, last_query, one = lax.optimization_barrier((two, last_query, one))
     two = shift(two, -1)
-    (three,) = partial_for(3, far, last_probes)
+    (three,) = partial_for(3, far, last_query, w_key_up)
     three, own_probes, two = lax.optimization_barrier((three, own_probes, two))
     three = shift(three, -3)
     two = shift(two, -1)

time: 82.1 us -> 83 us (1.011)
  local copies, waits for them, and re-layouts: 5.71 us -> 8.3 us
  starting transfers between devices: 24.1 us -> 22.5 us
  waiting for transfers between devices: 9.78 us -> 8.39 us
  Pallas kernels: 40.5 us -> 41.7 us
    pallas_call x4, Pallas kernels: 23.7 us -> 26.3 us  [attend(): pl.pallas_call(functools.partial(attend_kernel, by, keep_far), out_shape=...]
    ppermute x8, starting transfers between devices: 10.8 us -> 8.63 us  [shift(): return lax.ppermute(value, 'section', pairs)]
    ppermute x8, waiting for transfers between devices: 7.08 us -> 5.69 us  [shift(): return lax.ppermute(value, 'section', pairs)]
    pallas_call x1 -> x0, Pallas kernels: 1.33 us -> none  [make_probes(): pl.pallas_call(probes_kernel, out_shape=[probes] * 2, in_specs=[VMEM] + [...]
    slice x1, local copies, waits for them, and re-layouts: 0.01 us -> 0.94 us  [on_device(): next_query[:cut]]
    slice x1, local copies, waits for them, and re-layouts: 0.01 us -> 0.94 us  [on_device(): last_query[cut:]]
    ppermute x1, starting transfers between devices: 2.69 us -> 3.56 us  [on_device(): incoming = lax.ppermute(send, 'tp', swap)]
    unnamed x34 -> x38, local copies, waits for them, and re-layouts: 5.68 us -> 6.42 us
  transfers between devices with their start and end apart: 12 -> 12, of which waited for: 5 -> 7; matrix products, arithmetic and copies ran while one was open for 0% -> 2% of each run, Pallas kernels for 39% -> 40%
where the time goes in v8:
time: 83 us; the launch traced here: 82.6 us
  Pallas kernels  41.7 us (50%)
  starting transfers between devices  22.5 us (27%)
  waiting for transfers between devices  8.39 us (10%)
  local copies, waits for them, and re-layouts  8.3 us (10%)
  between operations  0.89 us (1%)
    pallas_call x4, Pallas kernels, attend(): pl.pallas_call(functools.partial(attend_kernel, by, keep_far), out_shape=...  26.3 us
    ppermute x8, starting transfers between devices, shift(): return lax.ppermute(value, 'section', pairs)  8.63 us
    all_to_all x1, starting transfers between devices, on_device(): lax.all_to_all(outgoing, 'store', split_axis=0, concat_axis=0, tiled=True)  7.6 us
    unnamed x38, local copies, waits for them, and re-layouts  6.42 us
    ppermute x8, waiting for transfers between devices, shift(): return lax.ppermute(value, 'section', pairs)  5.69 us
    pallas_call x1, Pallas kernels, project(): pl.pallas_call(project_kernel, out_shape=[jax.ShapeDtypeStruct((rows, col...  5.13 us
    ppermute x1, starting transfers between devices, on_device(): incoming = lax.ppermute(send, 'tp', swap)  3.56 us
    pallas_call x1, Pallas kernels, pack_pages(): pl.pallas_call(pack_kernel, out_shape=jax.ShapeDtypeStruct((n_store, rows...  3.3 us
  transfers between devices with their start and end apart: 12, of which 7 were waited for; matrix products, arithmetic and copies ran while one was open for 2% of the time, Pallas kernels for 40%

profile of v8, /device:TPU:1, one launch (start us, length us, event | category | flops | bytes accessed | tf_op | source)
XLA Modules:
  0.0 82.6 jit_solution(9616932277609403102)
XLA Ops:
  0.6 3.3 %pack_pages.1 = bf16[16,32,1152]{2,1,0:T(8,128)(2,1)} custom-call(s32[16,24]{1,0:T(8,128)} %bitcast.12, s32[16,24]{1,0:T(8,128)} %slot_src.1, bf16[8,576,256]{2,1,0:T(8,128)(2,1)} %bitcast.15), custom_call_target="tpu_custom_call" | custom-call | tf_op jit(solution)/shard_map/pack_pages/pallas_call | solution.py:126
  3.9 7.6 %all-to-all-start = ((bf16[16,2,16,1152]{3,2,1,0:T(8,128)(2,1)}), bf16[16,2,16,1152]{3,2,1,0:T(8,128)(2,1)S(1)}, u32[]{:S(2)}, u32[]{:S(2)}) async-start(bf16[16,2,16,1152]{3,2,1,0:T(8,128)(2,1)} %bitcast.14), calls=%async_computation | async-start | bytes 2359296 | tf_op jit(solution)/shard_map/all_to_all | solution.py:526
  11.6 5.1 %project.1 = (bf16[128,1536]{1,0:T(8,128)(2,1)}, bf16[128,2048]{1,0:T(8,128)(2,1)}, f32[128,128]{1,0:T(8,128)}) custom-call(s32[16]{0:T(128)} %count.3, bf16[128,2048]{1,0:T(8,128)(2,1)} %tokens.1, bf16[2048]{0:T(1024)(128)(2,1)} %gain.2, f32[6656,128]{1,0:T(8,128)} %constant.2.clone.table, bf16[2048,1536]{1,0:T(8,128)(2,1)} %w_query_src.1), custom_call_target="tpu_custom_call" | custom-call | tf_op jit(solution)/shard_map/project/pallas_call | solution.py:226
  16.7 3.8 %collective-permute-start = (bf16[128,1536]{1,0:T(8,128)(2,1)}, bf16[128,1536]{1,0:T(8,128)(2,1)S(1)}, u32[]{:S(2)}, u32[]{:S(2)}) collective-permute-start(bf16[128,1536]{1,0:T(8,128)(2,1)} %get-tuple-element.31.query), channel_id=1, source_target_pairs={{2,0},{4,2},{6,4},{0,6},{3,1},{5,3},{7,5},{1,7},{10,8},{12,10},{14... | collective-permute-start | bytes 1179656 | tf_op jit(solution)/shard_map/ppermute | solution.py:531
  20.6 1.7 %copy-done.6 = bf16[2048,576]{0,1:T(8,128)(2,1)S(1)} copy-done((bf16[2048,576]{0,1:T(8,128)(2,1)S(1)}, bf16[2048,576]{0,1:T(8,128)(2,1)}, u32[]{:S(2)}) %copy-start.6) | copy-done | bytes 2359320
  22.2 1.0 %copy-done.12 = bf16[128,2048]{1,0:T(8,128)(2,1)S(1)} copy-done((bf16[128,2048]{1,0:T(8,128)(2,1)S(1)}, bf16[128,2048]{1,0:T(8,128)(2,1)}, u32[]{:S(2)}) %copy-start.12) | copy-done | bytes 524312
  23.3 1.0 %copy-done.13 = bf16[128,1536]{1,0:T(8,128)(2,1)S(1)} copy-done((bf16[128,1536]{1,0:T(8,128)(2,1)S(1)}, bf16[128,1536]{1,0:T(8,128)(2,1)}, u32[]{:S(2)}) %copy-start.13) | copy-done | bytes 393240
  25.1 2.0 %project_latent.1 = (bf16[576,128]{1,0:T(8,128)(2,1)}, bf16[128,640]{1,0:T(8,128)(2,1)S(1)}, bf16[1024,640]{1,0:T(8,128)(2,1)S(1)}) custom-call(bf16[128,2048]{1,0:T(8,128)(2,1)S(1)} %copy-done.12, f32[128,128]{1,0:T(8,128)S(1)} %copy-done.14, bf16[576,2048]{1,0:T(8,128)(2,1)S(1)} %bitcast.11, bf16[512]{0:T(512)(128)(2,1)S(1)} %copy-done.18, ...), custom_call_target="tpu_custom_call" | custom-call | tf_op jit(solution)/shard_map/project_latent/pallas_call | solution.py:266
  27.1 1.1 %copy-done.8 = bf16[1024,640]{1,0:T(8,128)(2,1)} copy-done((bf16[1024,640]{1,0:T(8,128)(2,1)}, bf16[1024,640]{1,0:T(8,128)(2,1)S(1)}, u32[]{:S(2)}) %copy-start.8) | copy-done | bytes 1310744
  29.1 2.4 %collective-permute-done.1.refs_0_ = bf16[128,1536]{1,0:T(8,128)(2,1)} collective-permute-done((bf16[128,1536]{1,0:T(8,128)(2,1)}, bf16[128,1536]{1,0:T(8,128)(2,1)}, u32[]{:S(2)}, u32[]{:S(2)}) %collective-permute-start.1) | collective-permute-done | bytes 393248 | tf_op jit(solution)/shard_map/ppermute | solution.py:531
  32.3 2.2 %collective-permute-start.2 = (bf16[768,640]{1,0:T(8,128)(2,1)S(1)}, bf16[768,640]{1,0:T(8,128)(2,1)S(1)}, u32[]{:S(2)}, u32[]{:S(2)}) collective-permute-start(bf16[768,640]{1,0:T(8,128)(2,1)S(1)} %build_keys.1.near), channel_id=1, source_target_pairs={{0,1},{1,0},{2,3},{3,2},{4,5},{5,4},{6,7},{7,6},{8,9},{9,8},{10,11... | collective-permute-start | bytes 2949128 | tf_op jit(solution)/shard_map/ppermute | solution.py:549
  34.6 0.9 %slice.6 = bf16[64,1536]{1,0:T(8,128)(2,1)S(1)} slice(bf16[128,1536]{1,0:T(8,128)(2,1)} %copy-done.10), slice={[0:64], [0:1536]} | slice | bytes 393216 | tf_op jit(solution)/shard_map/slice | solution.py:546
  35.5 2.0 %collective-permute-start.3 = (bf16[64,1536]{1,0:T(8,128)(2,1)S(1)}, bf16[64,1536]{1,0:T(8,128)(2,1)S(1)}, u32[]{:S(2)}, u32[]{:S(2)}) collective-permute-start(bf16[64,1536]{1,0:T(8,128)(2,1)S(1)} %slice.6), channel_id=1, source_target_pairs={{2,0},{4,2},{6,4},{0,6},{3,1},{5,3},{7,5},{1,7},{10,8},{12,10},{14... | collective-permute-start | bytes 589832 | tf_op jit(solution)/shard_map/ppermute | solution.py:531
  38.6 6.4 %attend_1.1 = (bf16[128,1152]{1,0:T(8,128)(2,1)S(1)}, bf16[768,640]{1,0:T(8,128)(2,1)S(1)}) custom-call(bf16[8,512,128]{2,1,0:T(8,128)(2,1)S(1)} %copy-done.1, bf16[768,640]{1,0:T(8,128)(2,1)S(1)} %build_keys.1.near, bf16[768,640]{1,0:T(8,128)(2,1)S(1)} %collective-permute-done.2.arrived, bf16[128,640]{1,0:T(8,128)(2,1)S(1)} %get-tuple-element.36.span, ...), custom_call_target="tpu_custom_call" | custom-call | tf_op jit(solution)/shard_map/attend_1/pallas_call | solution.py:409
  46.0 6.7 %attend_2.1 = bf16[128,1152]{1,0:T(8,128)(2,1)S(1)} custom-call(bf16[8,512,128]{2,1,0:T(8,128)(2,1)S(1)} %copy-done.1, bf16[768,640]{1,0:T(8,128)(2,1)S(1)} %build_keys.1.near, bf16[768,640]{1,0:T(8,128)(2,1)S(1)} %get-tuple-element.38.arrived, bf16[128,640]{1,0:T(8,128)(2,1)S(1)} %get-tuple-element.36.span, ...), custom_call_target="tpu_custom_call" | custom-call | tf_op jit(solution)/shard_map/attend_2/pallas_call | solution.py:409
  52.6 1.9 %collective-permute-done.5.one = bf16[128,1152]{1,0:T(8,128)(2,1)S(1)} collective-permute-done((bf16[128,1152]{1,0:T(8,128)(2,1)S(1)}, bf16[128,1152]{1,0:T(8,128)(2,1)S(1)}, u32[]{:S(2)}, u32[]{:S(2)}) %collective-permute-start.5) | collective-permute-done | bytes 294944 | tf_op jit(solution)/shard_map/ppermute | solution.py:531
  54.6 7.3 %attend_3.1 = bf16[128,1152]{1,0:T(8,128)(2,1)S(1)} custom-call(bf16[8,512,128]{2,1,0:T(8,128)(2,1)S(1)} %copy-done.1, bf16[768,640]{1,0:T(8,128)(2,1)S(1)} %build_keys.1.near, bf16[768,640]{1,0:T(8,128)(2,1)S(1)} %get-tuple-element.38.arrived, bf16[128,640]{1,0:T(8,128)(2,1)S(1)} %get-tuple-element.36.span, ...), custom_call_target="tpu_custom_call" | custom-call | tf_op jit(solution)/shard_map/attend_3/pallas_call | solution.py:409
  63.0 2.0 %collective-permute-start.8 = (bf16[128,1152]{1,0:T(8,128)(2,1)S(1)}, bf16[128,1152]{1,0:T(8,128)(2,1)S(1)}, u32[]{:S(2)}, u32[]{:S(2)}) collective-permute-start(bf16[128,1152]{1,0:T(8,128)(2,1)S(1)} %attend_3.1), channel_id=1, source_target_pairs={{2,0},{4,2},{6,4},{0,6},{3,1},{5,3},{7,5},{1,7},{10,8},{12,10},{14... | collective-permute-start | bytes 884744 | tf_op jit(solution)/shard_map/ppermute | solution.py:531
  65.0 5.9 %attend_0.1.own = bf16[128,1152]{1,0:T(8,128)(2,1)S(1)} custom-call(bf16[8,512,128]{2,1,0:T(8,128)(2,1)S(1)} %copy-done.1, bf16[768,640]{1,0:T(8,128)(2,1)S(1)} %build_keys.1.near, bf16[768,640]{1,0:T(8,128)(2,1)S(1)} %get-tuple-element.38.arrived, bf16[128,640]{1,0:T(8,128)(2,1)S(1)} %get-tuple-element.36.span, bf16[1024,640]{1,0:T(8,128)(2,1)S(1)} %copy-done.9), custom_call_target="tpu_custom_call" | custom-call | tf_op jit(solution)/shard_map/attend_0/pallas_call | solution.py:409
  70.9 1.5 %project_output.1 = (f32[128,2048]{1,0:T(8,128)S(1)}, bf16[128,2048]{1,0:T(8,128)(2,1)S(1)}) custom-call(bf16[128,1152]{1,0:T(8,128)(2,1)S(1)} %attend_0.1.own, bf16[128,1152]{1,0:T(8,128)(2,1)S(1)} %collective-permute-done.5.one, bf16[128,1152]{1,0:T(8,128)(2,1)S(1)} %collective-permute-done.7.two, bf16[128,1152]{1,0:T(8,128)(2,1)S(1)} %collective-permute-done.8.three, ...), custom_call_target="tpu_custom_call" | custom-call | tf_op jit(solution)/shard_map/project_output/pallas_call | solution.py:453
  72.4 3.6 %collective-permute-start.9 = (bf16[128,2048]{1,0:T(8,128)(2,1)S(1)}, bf16[128,2048]{1,0:T(8,128)(2,1)S(1)}, u32[]{:S(2)}, u32[]{:S(2)}) collective-permute-start(bf16[128,2048]{1,0:T(8,128)(2,1)S(1)} %get-tuple-element.52), channel_id=1, source_target_pairs={{0,1},{1,0},{2,3},{3,2},{4,5},{5,4},{6,7},{7,6},{8,9},{9,8},{10,11... | collective-permute-start | bytes 1572872 | tf_op jit(solution)/shard_map/ppermute | solution.py:567
  76.0 1.5 %collective-permute-done.9.other = bf16[128,2048]{1,0:T(8,128)(2,1)S(1)} collective-permute-done((bf16[128,2048]{1,0:T(8,128)(2,1)S(1)}, bf16[128,2048]{1,0:T(8,128)(2,1)S(1)}, u32[]{:S(2)}, u32[]{:S(2)}) %collective-permute-start.9) | collective-permute-done | bytes 524320 | tf_op jit(solution)/shard_map/ppermute | solution.py:567
  77.6 2.6 %expert.1 = (f32[128,1024]{1,0:T(8,128)S(1)}, bf16[128,1024]{1,0:T(8,128)(2,1)S(1)}) custom-call(bf16[128,2048]{1,0:T(8,128)(2,1)S(1)} %copy-done.7, f32[128,2048]{1,0:T(8,128)S(1)} %get-tuple-element.51.exact, bf16[128,2048]{1,0:T(8,128)(2,1)S(1)} %collective-permute-done.9.other, bf16[2048]{0:T(1024)(128)(2,1)S(1)} %copy-done.16, ...), custom_call_target="tpu_custom_call" | custom-call | tf_op jit(solution)/shard_map/expert/pallas_call | solution.py:484
  80.6 1.2 %collective-permute-done.10 = bf16[128,1024]{1,0:T(8,128)(2,1)S(1)} collective-permute-done((bf16[128,1024]{1,0:T(8,128)(2,1)S(1)}, bf16[128,1024]{1,0:T(8,128)(2,1)S(1)}, u32[]{:S(2)}, u32[]{:S(2)}) %collective-permute-start.10) | collective-permute-done | bytes 262176 | tf_op jit(solution)/shard_map/ppermute | solution.py:577
  (51 shorter events, 6.9 us)
Async XLA Ops:
  3.9 27.5 %all-to-all-start = ((bf16[16,2,16,1152]{3,2,1,0:T(8,128)(2,1)}), bf16[16,2,16,1152]{3,2,1,0:T(8,128)(2,1)S(1)}, u32[]{:S(2)}, u32[]{:S(2)}) async-start(bf16[16,2,16,1152]{3,2,1,0:T(8,128)(2,1)} %bitcast.14), calls=%async_computation | async-start | bytes 2359296 | tf_op jit(solution)/shard_map/all_to_all | solution.py:526
  11.5 9.0 %copy-start = (bf16[8,512,128]{2,1,0:T(8,128)(2,1)S(1)}, bf16[8,512,128]{2,1,0:T(8,128)(2,1)}, u32[]{:S(2)}) copy-start(bf16[8,512,128]{2,1,0:T(8,128)(2,1)} %refs_1_.3) | copy-start | bytes 3145732
  11.6 9.0 %copy-start.18 = (bf16[512]{0:T(512)(128)(2,1)S(1)}, bf16[512]{0:T(512)(128)(2,1)}, u32[]{:S(2)}) copy-start(bf16[512]{0:T(512)(128)(2,1)} %kv_gain.1) | copy-start | bytes 3076
  11.6 19.9 %copy-start.15 = (s32[16,24,1]{1,2,0:T(1,128)S(1)}, s32[16,24,1]{1,2,0:T(1,128)}, u32[]{:S(2)}) copy-start(s32[16,24,1]{1,2,0:T(1,128)} %param.30) | copy-start | bytes 4612
  16.7 14.7 %copy-start.17 = (s32[16]{0:T(128)S(1)}, s32[16]{0:T(128)}, u32[]{:S(2)}) copy-start(s32[16]{0:T(128)} %count.3) | copy-start | bytes 196
  16.7 11.6 %collective-permute-start = (bf16[128,1536]{1,0:T(8,128)(2,1)}, bf16[128,1536]{1,0:T(8,128)(2,1)S(1)}, u32[]{:S(2)}, u32[]{:S(2)}) collective-permute-start(bf16[128,1536]{1,0:T(8,128)(2,1)} %get-tuple-element.31.query), channel_id=1, source_target_pairs={{2,0},{4,2},{6,4},{0,6},{3,1},{5,3},{7,5},{1,7},{10,8},{12,10},{14... | collective-permute-start | bytes 1179656 | tf_op jit(solution)/shard_map/ppermute | solution.py:531
  20.5 10.9 %collective-permute-start.1 = (bf16[128,1536]{1,0:T(8,128)(2,1)}, bf16[128,1536]{1,0:T(8,128)(2,1)}, u32[]{:S(2)}, u32[]{:S(2)}) collective-permute-start(bf16[128,1536]{1,0:T(8,128)(2,1)} %get-tuple-element.31.query), channel_id=1, source_target_pairs={{6,0},{0,2},{2,4},{4,6},{7,1},{1,3},{3,5},{5,7},{14,8},{8,10},{10,... | collective-permute-start | bytes 1179656 | tf_op jit(solution)/shard_map/ppermute | solution.py:531
  25.1 13.5 %copy-start.1 = (bf16[8,512,128]{2,1,0:T(8,128)(2,1)S(1)}, bf16[8,512,128]{2,1,0:T(8,128)(2,1)}, u32[]{:S(2)}) copy-start(bf16[8,512,128]{2,1,0:T(8,128)(2,1)} %value_up.7) | copy-start | bytes 3145732
  31.4 7.1 %copy-start.11 = (bf16[128,1536]{1,0:T(8,128)(2,1)S(1)}, bf16[128,1536]{1,0:T(8,128)(2,1)}, u32[]{:S(2)}) copy-start(bf16[128,1536]{1,0:T(8,128)(2,1)} %copy-done.10) | copy-start | bytes 1179652
  32.3 6.2 %collective-permute-start.2 = (bf16[768,640]{1,0:T(8,128)(2,1)S(1)}, bf16[768,640]{1,0:T(8,128)(2,1)S(1)}, u32[]{:S(2)}, u32[]{:S(2)}) collective-permute-start(bf16[768,640]{1,0:T(8,128)(2,1)S(1)} %build_keys.1.near), channel_id=1, source_target_pairs={{0,1},{1,0},{2,3},{3,2},{4,5},{5,4},{6,7},{7,6},{8,9},{9,8},{10,11... | collective-permute-start | bytes 2949128 | tf_op jit(solution)/shard_map/ppermute | solution.py:549
  35.5 9.5 %collective-permute-start.3 = (bf16[64,1536]{1,0:T(8,128)(2,1)S(1)}, bf16[64,1536]{1,0:T(8,128)(2,1)S(1)}, u32[]{:S(2)}, u32[]{:S(2)}) collective-permute-start(bf16[64,1536]{1,0:T(8,128)(2,1)S(1)} %slice.6), channel_id=1, source_target_pairs={{2,0},{4,2},{6,4},{0,6},{3,1},{5,3},{7,5},{1,7},{10,8},{12,10},{14... | collective-permute-start | bytes 589832 | tf_op jit(solution)/shard_map/ppermute | solution.py:531
  38.5 7.5 %collective-permute-start.4 = (bf16[64,1536]{1,0:T(8,128)(2,1)S(1)}, bf16[64,1536]{1,0:T(8,128)(2,1)S(1)}, u32[]{:S(2)}, u32[]{:S(2)}) collective-permute-start(bf16[64,1536]{1,0:T(8,128)(2,1)S(1)} %slice.7), channel_id=1, source_target_pairs={{6,0},{0,2},{2,4},{4,6},{7,1},{1,3},{3,5},{5,7},{14,8},{8,10},{10,... | collective-permute-start | bytes 589832 | tf_op jit(solution)/shard_map/ppermute | solution.py:531
  46.0 8.6 %collective-permute-start.5 = (bf16[128,1152]{1,0:T(8,128)(2,1)S(1)}, bf16[128,1152]{1,0:T(8,128)(2,1)S(1)}, u32[]{:S(2)}, u32[]{:S(2)}) collective-permute-start(bf16[128,1152]{1,0:T(8,128)(2,1)S(1)} %get-tuple-element.43), channel_id=1, source_target_pairs={{6,0},{0,2},{2,4},{4,6},{7,1},{1,3},{3,5},{5,7},{14,8},{8,10},{10,... | collective-permute-start | bytes 884744 | tf_op jit(solution)/shard_map/ppermute | solution.py:531
  52.6 12.3 %copy-start.9 = (bf16[1024,640]{1,0:T(8,128)(2,1)S(1)}, bf16[1024,640]{1,0:T(8,128)(2,1)}, u32[]{:S(2)}) copy-start(bf16[1024,640]{1,0:T(8,128)(2,1)} %copy-done.8) | copy-start | bytes 3932164
  54.6 7.7 %collective-permute-start.6 = (bf16[128,1152]{1,0:T(8,128)(2,1)S(1)}, bf16[128,1152]{1,0:T(8,128)(2,1)S(1)}, u32[]{:S(2)}, u32[]{:S(2)}) collective-permute-start(bf16[128,1152]{1,0:T(8,128)(2,1)S(1)} %attend_2.1), channel_id=1, source_target_pairs={{6,0},{0,2},{2,4},{4,6},{7,1},{1,3},{3,5},{5,7},{14,8},{8,10},{10,... | collective-permute-start | bytes 884744 | tf_op jit(solution)/shard_map/ppermute | solution.py:531
  54.6 23.0 %copy-start.5 = (bf16[704,2048]{1,0:T(8,128)(2,1)S(1)}, bf16[704,2048]{1,0:T(8,128)(2,1)}, u32[]{:S(2)}) copy-start(bf16[704,2048]{1,0:T(8,128)(2,1)} %w_down.1) | copy-start | bytes 8650756
  54.6 23.0 %copy-start.7 = (bf16[128,2048]{1,0:T(8,128)(2,1)S(1)}, bf16[128,2048]{1,0:T(8,128)(2,1)}, u32[]{:S(2)}) copy-start(bf16[128,2048]{1,0:T(8,128)(2,1)} %tokens.1) | copy-start | bytes 1572868
  61.9 9.0 %copy-start.2 = (bf16[1024,2048]{1,0:T(8,128)(2,1)S(1)}, bf16[1024,2048]{1,0:T(8,128)(2,1)}, u32[]{:S(2)}) copy-start(bf16[1024,2048]{1,0:T(8,128)(2,1)} %weight.1) | copy-start | bytes 12582916
  62.2 8.6 %collective-permute-start.7 = (bf16[128,1152]{1,0:T(8,128)(2,1)S(1)}, bf16[128,1152]{1,0:T(8,128)(2,1)S(1)}, u32[]{:S(2)}, u32[]{:S(2)}) collective-permute-start(bf16[128,1152]{1,0:T(8,128)(2,1)S(1)} %collective-permute-done.6), channel_id=1, source_target_pairs={{6,0},{0,2},{2,4},{4,6},{7,1},{1,3},{3,5},{5,7},{14,8},{8,10},{10,... | collective-permute-start | bytes 884744 | tf_op jit(solution)/shard_map/ppermute | solution.py:531
  63.0 7.9 %collective-permute-start.8 = (bf16[128,1152]{1,0:T(8,128)(2,1)S(1)}, bf16[128,1152]{1,0:T(8,128)(2,1)S(1)}, u32[]{:S(2)}, u32[]{:S(2)}) collective-permute-start(bf16[128,1152]{1,0:T(8,128)(2,1)S(1)} %attend_3.1), channel_id=1, source_target_pairs={{2,0},{4,2},{6,4},{0,6},{3,1},{5,3},{7,5},{1,7},{10,8},{12,10},{14... | collective-permute-start | bytes 884744 | tf_op jit(solution)/shard_map/ppermute | solution.py:531
  65.0 12.6 %copy-start.4 = (bf16[2048,704]{0,1:T(8,128)(2,1)S(1)}, bf16[2048,704]{0,1:T(8,128)(2,1)}, u32[]{:S(2)}) copy-start(bf16[2048,704]{0,1:T(8,128)(2,1)} %param.27) | copy-start | bytes 8650756
  70.8 6.7 %copy-start.3 = (bf16[2048,704]{0,1:T(8,128)(2,1)S(1)}, bf16[2048,704]{0,1:T(8,128)(2,1)}, u32[]{:S(2)}) copy-start(bf16[2048,704]{0,1:T(8,128)(2,1)} %param.26) | copy-start | bytes 8650756
  72.4 5.1 %collective-permute-start.9 = (bf16[128,2048]{1,0:T(8,128)(2,1)S(1)}, bf16[128,2048]{1,0:T(8,128)(2,1)S(1)}, u32[]{:S(2)}, u32[]{:S(2)}) collective-permute-start(bf16[128,2048]{1,0:T(8,128)(2,1)S(1)} %get-tuple-element.52), channel_id=1, source_target_pairs={{0,1},{1,0},{2,3},{3,2},{4,5},{5,4},{6,7},{7,6},{8,9},{9,8},{10,11... | collective-permute-start | bytes 1572872 | tf_op jit(solution)/shard_map/ppermute | solution.py:567
  80.2 1.6 %collective-permute-start.10 = (bf16[128,1024]{1,0:T(8,128)(2,1)S(1)}, bf16[128,1024]{1,0:T(8,128)(2,1)S(1)}, u32[]{:S(2)}, u32[]{:S(2)}) collective-permute-start(bf16[128,1024]{1,0:T(8,128)(2,1)S(1)} %get-tuple-element.54), channel_id=1, source_target_pairs={{0,1},{1,0},{2,3},{3,2},{4,5},{5,4},{6,7},{7,6},{8,9},{9,8},{10,11... | collective-permute-start | bytes 786440 | tf_op jit(solution)/shard_map/ppermute | solution.py:577
  (7 other events, 13.1 us)

commit v9 on v7

--- a/solution.py
+++ b/solution.py
@@ -298,30 +298,24 @@
         probes[at, KVR:] = jnp.where(rope_lanes < ROPE, pair, one).astype(BF16)
 
 
-def probes_kernel(key_up, ahead_src, behind_src, ahead_probes, behind_probes, ahead, behind, sems):
-    pairs = ((ahead_src, ahead), (behind_src, behind))
-    copies = [
-        pltpu.make_async_copy(src, dst, sems.at[i]) for i, (src, dst) in enumerate(pairs)
-    ]
-    for copy in copies:
-        copy.start()
-    for copy, query, probes in zip(copies, (ahead, behind), (ahead_probes, behind_probes)):
-        copy.wait()
-        fill_probes(query, key_up, probes)
-
-
-def make_probes(key_up, ahead, behind):
-    rows, width = ahead.shape
-    probes = jax.ShapeDtypeStruct((key_up.shape[0] * rows, WIDE), BF16)
+def probes_kernel(key_up, source, probes, query, sem):
+    copy = pltpu.make_async_copy(source, query, sem)
+    copy.start()
+    copy.wait()
+    fill_probes(query, key_up, probes)
+
+
+def make_probes(key_up, query):
+    rows, width = query.shape
     return pl.pallas_call(
         probes_kernel,
-        out_shape=[probes] * 2,
-        in_specs=[VMEM] + [ANY] * 2,
-        out_specs=[VMEM] * 2,
-        scratch_shapes=[pltpu.VMEM((rows, width), BF16)] * 2 + [pltpu.SemaphoreType.DMA((2,))],
+        out_shape=jax.ShapeDtypeStruct((key_up.shape[0] * rows, WIDE), BF16),
+        in_specs=[VMEM, ANY],
+        out_specs=VMEM,
+        scratch_shapes=[pltpu.VMEM((rows, width), BF16), pltpu.SemaphoreType.DMA],
         compiler_params=params(20),
         name="make_probes",
-    )(key_up, ahead, behind)
+    )(key_up, query)
 
 
 def attend_kernel(by, keep_far, value_up, near, arrived, span, *refs):
@@ -560,7 +554,7 @@
     near = build_keys(owner, fetch_count, arrived)
     far = lax.ppermute(near, "tp", swap)
 
-    next_probes, last_probes = make_probes(w_key_up, next_query, last_query)
+    next_probes = make_probes(w_key_up, next_query)
 
     def partial_for(by, far, *queries, **flags):
         return attend(by, w_value_up, near, far, span, *queries, **flags)
@@ -569,7 +563,9 @@
     one, far_low, far_high = lax.optimization_barrier((one, far_low, far_high))
     one = shift(one, -1)
     (two,) = partial_for(2, far, far_low, far_high, w_key_up)
-    two, last_probes, one = lax.optimization_barrier((two, last_probes, one))
+    two, last_query = lax.optimization_barrier((two, last_query))
+    last_probes = make_probes(w_key_up, last_query)
+    last_probes, one = lax.optimization_barrier((last_probes, one))
     two = shift(two, -1)
     (three,) = partial_for(3, far, last_probes)
     three, own_probes, two = lax.optimization_barrier((three, own_probes, two))

time: 82.1 us -> 78.7 us (0.959)
  waiting for transfers between devices: 9.78 us -> 6.08 us
    ppermute x8, waiting for transfers between devices: 7.08 us -> 3.38 us  [shift(): return lax.ppermute(value, 'section', pairs)]
    ppermute x8, starting transfers between devices: 10.8 us -> 11.7 us  [shift(): return lax.ppermute(value, 'section', pairs)]
  transfers between devices with their start and end apart: 12 -> 12, of which waited for: 5 -> 6; matrix products, arithmetic and copies ran while one was open for 0% -> 0% of each run, Pallas kernels for 39% -> 41%
where the time goes in v9:
time: 78.7 us; the launch traced here: 78.3 us
  Pallas kernels  40.5 us (51%)
  starting transfers between devices  24.4 us (31%)
  waiting for transfers between devices  6.08 us (8%)
  local copies, waits for them, and re-layouts  5.71 us (7%)
  between operations  0.88 us (1%)
    pallas_call x4, Pallas kernels, attend(): pl.pallas_call(functools.partial(attend_kernel, by, keep_far), out_shape=...  23.7 us
    ppermute x8, starting transfers between devices, shift(): return lax.ppermute(value, 'section', pairs)  11.7 us
    all_to_all x1, starting transfers between devices, on_device(): lax.all_to_all(outgoing, 'store', split_axis=0, concat_axis=0, tiled=True)  7.6 us
    unnamed x34, local copies, waits for them, and re-layouts  5.68 us
    pallas_call x1, Pallas kernels, project(): pl.pallas_call(project_kernel, out_shape=[jax.ShapeDtypeStruct((rows, col...  5.11 us
    ppermute x8, waiting for transfers between devices, shift(): return lax.ppermute(value, 'section', pairs)  3.38 us
    pallas_call x1, Pallas kernels, pack_pages(): pl.pallas_call(pack_kernel, out_shape=jax.ShapeDtypeStruct((n_store, rows...  3.3 us
    pallas_call x1, Pallas kernels, expert(): pl.pallas_call(expert_kernel, out_shape=[jax.ShapeDtypeStruct((rows, half...  2.61 us
  transfers between devices with their start and end apart: 12, of which 6 were waited for; matrix products, arithmetic and copies ran while one was open for 0% of the time, Pallas kernels for 41%

profile of v9, /device:TPU:1, one launch (start us, length us, event | category | flops | bytes accessed | tf_op | source)
XLA Modules:
  0.0 78.3 jit_solution(3196459707585158022)
XLA Ops:
  0.6 3.3 %pack_pages.1 = bf16[16,32,1152]{2,1,0:T(8,128)(2,1)} custom-call(s32[16,24]{1,0:T(8,128)} %bitcast.12, s32[16,24]{1,0:T(8,128)} %slot_src.1, bf16[8,576,256]{2,1,0:T(8,128)(2,1)} %bitcast.15), custom_call_target="tpu_custom_call" | custom-call | tf_op jit(solution)/shard_map/pack_pages/pallas_call | solution.py:126
  3.9 7.6 %all-to-all-start = ((bf16[16,2,16,1152]{3,2,1,0:T(8,128)(2,1)}), bf16[16,2,16,1152]{3,2,1,0:T(8,128)(2,1)S(1)}, u32[]{:S(2)}, u32[]{:S(2)}) async-start(bf16[16,2,16,1152]{3,2,1,0:T(8,128)(2,1)} %bitcast.14), calls=%async_computation | async-start | bytes 2359296 | tf_op jit(solution)/shard_map/all_to_all | solution.py:532
  11.6 5.1 %project.1 = (bf16[128,1536]{1,0:T(8,128)(2,1)}, bf16[128,2048]{1,0:T(8,128)(2,1)}, f32[128,128]{1,0:T(8,128)}) custom-call(s32[16]{0:T(128)} %count.3, bf16[128,2048]{1,0:T(8,128)(2,1)} %tokens.1, bf16[2048]{0:T(1024)(128)(2,1)} %gain.2, f32[6656,128]{1,0:T(8,128)} %constant.2.clone.table, bf16[2048,1536]{1,0:T(8,128)(2,1)} %w_query_src.1), custom_call_target="tpu_custom_call" | custom-call | tf_op jit(solution)/shard_map/project/pallas_call | solution.py:226
  16.7 1.7 %collective-permute-start.1 = (bf16[128,1536]{1,0:T(8,128)(2,1)}, bf16[128,1536]{1,0:T(8,128)(2,1)S(1)}, u32[]{:S(2)}, u32[]{:S(2)}) collective-permute-start(bf16[128,1536]{1,0:T(8,128)(2,1)} %get-tuple-element.32.query), channel_id=1, source_target_pairs={{6,0},{0,2},{2,4},{4,6},{7,1},{1,3},{3,5},{5,7},{14,8},{8,10},{10,... | collective-permute-start | bytes 1179656 | tf_op jit(solution)/shard_map/ppermute | solution.py:537
  18.4 2.2 %collective-permute-start = (bf16[128,1536]{1,0:T(8,128)(2,1)}, bf16[128,1536]{1,0:T(8,128)(2,1)S(1)}, u32[]{:S(2)}, u32[]{:S(2)}) collective-permute-start(bf16[128,1536]{1,0:T(8,128)(2,1)} %get-tuple-element.32.query), channel_id=1, source_target_pairs={{2,0},{4,2},{6,4},{0,6},{3,1},{5,3},{7,5},{1,7},{10,8},{12,10},{14... | collective-permute-start | bytes 1179656 | tf_op jit(solution)/shard_map/ppermute | solution.py:537
  20.6 1.7 %copy-done.6 = bf16[2048,576]{0,1:T(8,128)(2,1)S(1)} copy-done((bf16[2048,576]{0,1:T(8,128)(2,1)S(1)}, bf16[2048,576]{0,1:T(8,128)(2,1)}, u32[]{:S(2)}) %copy-start.6) | copy-done | bytes 2359320
  22.3 1.0 %copy-done.10 = bf16[128,2048]{1,0:T(8,128)(2,1)S(1)} copy-done((bf16[128,2048]{1,0:T(8,128)(2,1)S(1)}, bf16[128,2048]{1,0:T(8,128)(2,1)}, u32[]{:S(2)}) %copy-start.10) | copy-done | bytes 524312
  25.2 2.0 %project_latent.1 = (bf16[576,128]{1,0:T(8,128)(2,1)}, bf16[128,640]{1,0:T(8,128)(2,1)S(1)}, bf16[1024,640]{1,0:T(8,128)(2,1)S(1)}) custom-call(bf16[128,2048]{1,0:T(8,128)(2,1)S(1)} %copy-done.10, f32[128,128]{1,0:T(8,128)S(1)} %copy-done.12, bf16[576,2048]{1,0:T(8,128)(2,1)S(1)} %bitcast.11, bf16[512]{0:T(512)(128)(2,1)S(1)} %copy-done.16, ...), custom_call_target="tpu_custom_call" | custom-call | tf_op jit(solution)/shard_map/project_latent/pallas_call | solution.py:266
  27.2 1.1 %copy-done.8 = bf16[1024,640]{1,0:T(8,128)(2,1)} copy-done((bf16[1024,640]{1,0:T(8,128)(2,1)}, bf16[1024,640]{1,0:T(8,128)(2,1)S(1)}, u32[]{:S(2)}) %copy-start.8) | copy-done | bytes 1310744
  28.2 1.0 %collective-permute-done.1.source = bf16[128,1536]{1,0:T(8,128)(2,1)S(1)} collective-permute-done((bf16[128,1536]{1,0:T(8,128)(2,1)}, bf16[128,1536]{1,0:T(8,128)(2,1)S(1)}, u32[]{:S(2)}, u32[]{:S(2)}) %collective-permute-start.1) | collective-permute-done | bytes 393248 | tf_op jit(solution)/shard_map/ppermute | solution.py:537
  30.2 2.6 %collective-permute-start.2 = (bf16[768,640]{1,0:T(8,128)(2,1)S(1)}, bf16[768,640]{1,0:T(8,128)(2,1)S(1)}, u32[]{:S(2)}, u32[]{:S(2)}) collective-permute-start(bf16[768,640]{1,0:T(8,128)(2,1)S(1)} %build_keys.1.near), channel_id=1, source_target_pairs={{0,1},{1,0},{2,3},{3,2},{4,5},{5,4},{6,7},{7,6},{8,9},{9,8},{10,11... | collective-permute-start | bytes 2949128 | tf_op jit(solution)/shard_map/ppermute | solution.py:555
  32.8 1.7 %collective-permute-start.4 = (bf16[64,1536]{1,0:T(8,128)(2,1)S(1)}, bf16[64,1536]{1,0:T(8,128)(2,1)S(1)}, u32[]{:S(2)}, u32[]{:S(2)}) collective-permute-start(bf16[64,1536]{1,0:T(8,128)(2,1)S(1)} %slice.7), channel_id=1, source_target_pairs={{6,0},{0,2},{2,4},{4,6},{7,1},{1,3},{3,5},{5,7},{14,8},{8,10},{10,... | collective-permute-start | bytes 589832 | tf_op jit(solution)/shard_map/ppermute | solution.py:537
  34.5 2.2 %collective-permute-start.3 = (bf16[64,1536]{1,0:T(8,128)(2,1)S(1)}, bf16[64,1536]{1,0:T(8,128)(2,1)S(1)}, u32[]{:S(2)}, u32[]{:S(2)}) collective-permute-start(bf16[64,1536]{1,0:T(8,128)(2,1)S(1)} %slice.6), channel_id=1, source_target_pairs={{2,0},{4,2},{6,4},{0,6},{3,1},{5,3},{7,5},{1,7},{10,8},{12,10},{14... | collective-permute-start | bytes 589832 | tf_op jit(solution)/shard_map/ppermute | solution.py:537
  37.4 5.9 %attend_1.1 = (bf16[128,1152]{1,0:T(8,128)(2,1)S(1)}, bf16[768,640]{1,0:T(8,128)(2,1)S(1)}) custom-call(bf16[8,512,128]{2,1,0:T(8,128)(2,1)S(1)} %copy-done.1, bf16[768,640]{1,0:T(8,128)(2,1)S(1)} %build_keys.1.near, bf16[768,640]{1,0:T(8,128)(2,1)S(1)} %collective-permute-done.2.arrived, bf16[128,640]{1,0:T(8,128)(2,1)S(1)} %get-tuple-element.37.span, ...), custom_call_target="tpu_custom_call" | custom-call | tf_op jit(solution)/shard_map/attend_1/pallas_call | solution.py:415
  43.6 6.1 %attend_2.1 = bf16[128,1152]{1,0:T(8,128)(2,1)S(1)} custom-call(bf16[8,512,128]{2,1,0:T(8,128)(2,1)S(1)} %copy-done.1, bf16[768,640]{1,0:T(8,128)(2,1)S(1)} %build_keys.1.near, bf16[768,640]{1,0:T(8,128)(2,1)S(1)} %get-tuple-element.39.arrived, bf16[128,640]{1,0:T(8,128)(2,1)S(1)} %get-tuple-element.37.span, ...), custom_call_target="tpu_custom_call" | custom-call | tf_op jit(solution)/shard_map/attend_2/pallas_call | solution.py:415
  51.3 1.7 %collective-permute-done.5.one = bf16[128,1152]{1,0:T(8,128)(2,1)S(1)} collective-permute-done((bf16[128,1152]{1,0:T(8,128)(2,1)S(1)}, bf16[128,1152]{1,0:T(8,128)(2,1)S(1)}, u32[]{:S(2)}, u32[]{:S(2)}) %collective-permute-start.5) | collective-permute-done | bytes 294944 | tf_op jit(solution)/shard_map/ppermute | solution.py:537
  53.1 5.9 %attend_3.1 = bf16[128,1152]{1,0:T(8,128)(2,1)S(1)} custom-call(bf16[8,512,128]{2,1,0:T(8,128)(2,1)S(1)} %copy-done.1, bf16[768,640]{1,0:T(8,128)(2,1)S(1)} %build_keys.1.near, bf16[768,640]{1,0:T(8,128)(2,1)S(1)} %get-tuple-element.39.arrived, bf16[128,640]{1,0:T(8,128)(2,1)S(1)} %get-tuple-element.37.span, bf16[1024,640]{1,0:T(8,128)(2,1)S(1)} %make_probes.3.refs_0_), custom_call_target="tpu_custom_call" | custom-call | tf_op jit(solution)/shard_map/attend_3/pallas_call | solution.py:415
  59.5 2.7 %collective-permute-start.8 = (bf16[128,1152]{1,0:T(8,128)(2,1)S(1)}, bf16[128,1152]{1,0:T(8,128)(2,1)S(1)}, u32[]{:S(2)}, u32[]{:S(2)}) collective-permute-start(bf16[128,1152]{1,0:T(8,128)(2,1)S(1)} %attend_3.1), channel_id=1, source_target_pairs={{2,0},{4,2},{6,4},{0,6},{3,1},{5,3},{7,5},{1,7},{10,8},{12,10},{14... | collective-permute-start | bytes 884744 | tf_op jit(solution)/shard_map/ppermute | solution.py:537
  62.1 5.9 %attend_0.1.own = bf16[128,1152]{1,0:T(8,128)(2,1)S(1)} custom-call(bf16[8,512,128]{2,1,0:T(8,128)(2,1)S(1)} %copy-done.1, bf16[768,640]{1,0:T(8,128)(2,1)S(1)} %build_keys.1.near, bf16[768,640]{1,0:T(8,128)(2,1)S(1)} %get-tuple-element.39.arrived, bf16[128,640]{1,0:T(8,128)(2,1)S(1)} %get-tuple-element.37.span, bf16[1024,640]{1,0:T(8,128)(2,1)S(1)} %copy-done.9), custom_call_target="tpu_custom_call" | custom-call | tf_op jit(solution)/shard_map/attend_0/pallas_call | solution.py:415
  68.1 1.5 %project_output.1 = (f32[128,2048]{1,0:T(8,128)S(1)}, bf16[128,2048]{1,0:T(8,128)(2,1)S(1)}) custom-call(bf16[128,1152]{1,0:T(8,128)(2,1)S(1)} %attend_0.1.own, bf16[128,1152]{1,0:T(8,128)(2,1)S(1)} %collective-permute-done.5.one, bf16[128,1152]{1,0:T(8,128)(2,1)S(1)} %collective-permute-done.7.two, bf16[128,1152]{1,0:T(8,128)(2,1)S(1)} %collective-permute-done.8.three, ...), custom_call_target="tpu_custom_call" | custom-call | tf_op jit(solution)/shard_map/project_output/pallas_call | solution.py:459
  69.7 2.0 %collective-permute-start.9 = (bf16[128,2048]{1,0:T(8,128)(2,1)S(1)}, bf16[128,2048]{1,0:T(8,128)(2,1)S(1)}, u32[]{:S(2)}, u32[]{:S(2)}) collective-permute-start(bf16[128,2048]{1,0:T(8,128)(2,1)S(1)} %get-tuple-element.54), channel_id=1, source_target_pairs={{0,1},{1,0},{2,3},{3,2},{4,5},{5,4},{6,7},{7,6},{8,9},{9,8},{10,11... | collective-permute-start | bytes 1572872 | tf_op jit(solution)/shard_map/ppermute | solution.py:576
  71.7 1.5 %collective-permute-done.9.other = bf16[128,2048]{1,0:T(8,128)(2,1)S(1)} collective-permute-done((bf16[128,2048]{1,0:T(8,128)(2,1)S(1)}, bf16[128,2048]{1,0:T(8,128)(2,1)S(1)}, u32[]{:S(2)}, u32[]{:S(2)}) %collective-permute-start.9) | collective-permute-done | bytes 524320 | tf_op jit(solution)/shard_map/ppermute | solution.py:576
  73.3 2.6 %expert.1 = (f32[128,1024]{1,0:T(8,128)S(1)}, bf16[128,1024]{1,0:T(8,128)(2,1)S(1)}) custom-call(bf16[128,2048]{1,0:T(8,128)(2,1)S(1)} %copy-done.7, f32[128,2048]{1,0:T(8,128)S(1)} %get-tuple-element.53.exact, bf16[128,2048]{1,0:T(8,128)(2,1)S(1)} %collective-permute-done.9.other, bf16[2048]{0:T(1024)(128)(2,1)S(1)} %copy-done.14, ...), custom_call_target="tpu_custom_call" | custom-call | tf_op jit(solution)/shard_map/expert/pallas_call | solution.py:490
  76.4 1.2 %collective-permute-done.10 = bf16[128,1024]{1,0:T(8,128)(2,1)S(1)} collective-permute-done((bf16[128,1024]{1,0:T(8,128)(2,1)S(1)}, bf16[128,1024]{1,0:T(8,128)(2,1)S(1)}, u32[]{:S(2)}, u32[]{:S(2)}) %collective-permute-start.10) | collective-permute-done | bytes 262176 | tf_op jit(solution)/shard_map/ppermute | solution.py:586
  (49 shorter events, 7.2 us)
Async XLA Ops:
  3.9 25.3 %all-to-all-start = ((bf16[16,2,16,1152]{3,2,1,0:T(8,128)(2,1)}), bf16[16,2,16,1152]{3,2,1,0:T(8,128)(2,1)S(1)}, u32[]{:S(2)}, u32[]{:S(2)}) async-start(bf16[16,2,16,1152]{3,2,1,0:T(8,128)(2,1)} %bitcast.14), calls=%async_computation | async-start | bytes 2359296 | tf_op jit(solution)/shard_map/all_to_all | solution.py:532
  11.5 9.1 %copy-start = (bf16[8,512,128]{2,1,0:T(8,128)(2,1)S(1)}, bf16[8,512,128]{2,1,0:T(8,128)(2,1)}, u32[]{:S(2)}) copy-start(bf16[8,512,128]{2,1,0:T(8,128)(2,1)} %key_up.5) | copy-start | bytes 3145732
  11.6 9.1 %copy-start.16 = (bf16[512]{0:T(512)(128)(2,1)S(1)}, bf16[512]{0:T(512)(128)(2,1)}, u32[]{:S(2)}) copy-start(bf16[512]{0:T(512)(128)(2,1)} %kv_gain.1) | copy-start | bytes 3076
  11.6 17.7 %copy-start.13 = (s32[16,24,1]{1,2,0:T(1,128)S(1)}, s32[16,24,1]{1,2,0:T(1,128)}, u32[]{:S(2)}) copy-start(s32[16,24,1]{1,2,0:T(1,128)} %param.30) | copy-start | bytes 4612
  16.7 12.6 %copy-start.15 = (s32[16]{0:T(128)S(1)}, s32[16]{0:T(128)}, u32[]{:S(2)}) copy-start(s32[16]{0:T(128)} %count.3) | copy-start | bytes 196
  16.7 12.6 %collective-permute-start.1 = (bf16[128,1536]{1,0:T(8,128)(2,1)}, bf16[128,1536]{1,0:T(8,128)(2,1)S(1)}, u32[]{:S(2)}, u32[]{:S(2)}) collective-permute-start(bf16[128,1536]{1,0:T(8,128)(2,1)} %get-tuple-element.32.query), channel_id=1, source_target_pairs={{6,0},{0,2},{2,4},{4,6},{7,1},{1,3},{3,5},{5,7},{14,8},{8,10},{10,... | collective-permute-start | bytes 1179656 | tf_op jit(solution)/shard_map/ppermute | solution.py:537
  18.4 10.9 %collective-permute-start = (bf16[128,1536]{1,0:T(8,128)(2,1)}, bf16[128,1536]{1,0:T(8,128)(2,1)S(1)}, u32[]{:S(2)}, u32[]{:S(2)}) collective-permute-start(bf16[128,1536]{1,0:T(8,128)(2,1)} %get-tuple-element.32.query), channel_id=1, source_target_pairs={{2,0},{4,2},{6,4},{0,6},{3,1},{5,3},{7,5},{1,7},{10,8},{12,10},{14... | collective-permute-start | bytes 1179656 | tf_op jit(solution)/shard_map/ppermute | solution.py:537
  29.3 8.1 %copy-start.1 = (bf16[8,512,128]{2,1,0:T(8,128)(2,1)S(1)}, bf16[8,512,128]{2,1,0:T(8,128)(2,1)}, u32[]{:S(2)}) copy-start(bf16[8,512,128]{2,1,0:T(8,128)(2,1)} %value_up.7) | copy-start | bytes 3145732
  30.2 7.2 %collective-permute-start.2 = (bf16[768,640]{1,0:T(8,128)(2,1)S(1)}, bf16[768,640]{1,0:T(8,128)(2,1)S(1)}, u32[]{:S(2)}, u32[]{:S(2)}) collective-permute-start(bf16[768,640]{1,0:T(8,128)(2,1)S(1)} %build_keys.1.near), channel_id=1, source_target_pairs={{0,1},{1,0},{2,3},{3,2},{4,5},{5,4},{6,7},{7,6},{8,9},{9,8},{10,11... | collective-permute-start | bytes 2949128 | tf_op jit(solution)/shard_map/ppermute | solution.py:555
  32.8 10.5 %collective-permute-start.4 = (bf16[64,1536]{1,0:T(8,128)(2,1)S(1)}, bf16[64,1536]{1,0:T(8,128)(2,1)S(1)}, u32[]{:S(2)}, u32[]{:S(2)}) collective-permute-start(bf16[64,1536]{1,0:T(8,128)(2,1)S(1)} %slice.7), channel_id=1, source_target_pairs={{6,0},{0,2},{2,4},{4,6},{7,1},{1,3},{3,5},{5,7},{14,8},{8,10},{10,... | collective-permute-start | bytes 589832 | tf_op jit(solution)/shard_map/ppermute | solution.py:537
  34.5 8.8 %collective-permute-start.3 = (bf16[64,1536]{1,0:T(8,128)(2,1)S(1)}, bf16[64,1536]{1,0:T(8,128)(2,1)S(1)}, u32[]{:S(2)}, u32[]{:S(2)}) collective-permute-start(bf16[64,1536]{1,0:T(8,128)(2,1)S(1)} %slice.6), channel_id=1, source_target_pairs={{2,0},{4,2},{6,4},{0,6},{3,1},{5,3},{7,5},{1,7},{10,8},{12,10},{14... | collective-permute-start | bytes 589832 | tf_op jit(solution)/shard_map/ppermute | solution.py:537
  43.3 9.8 %collective-permute-start.5 = (bf16[128,1152]{1,0:T(8,128)(2,1)S(1)}, bf16[128,1152]{1,0:T(8,128)(2,1)S(1)}, u32[]{:S(2)}, u32[]{:S(2)}) collective-permute-start(bf16[128,1152]{1,0:T(8,128)(2,1)S(1)} %get-tuple-element.45), channel_id=1, source_target_pairs={{6,0},{0,2},{2,4},{4,6},{7,1},{1,3},{3,5},{5,7},{14,8},{8,10},{10,... | collective-permute-start | bytes 884744 | tf_op jit(solution)/shard_map/ppermute | solution.py:537
  49.7 9.8 %collective-permute-start.6 = (bf16[128,1152]{1,0:T(8,128)(2,1)S(1)}, bf16[128,1152]{1,0:T(8,128)(2,1)S(1)}, u32[]{:S(2)}, u32[]{:S(2)}) collective-permute-start(bf16[128,1152]{1,0:T(8,128)(2,1)S(1)} %attend_2.1), channel_id=1, source_target_pairs={{6,0},{0,2},{2,4},{4,6},{7,1},{1,3},{3,5},{5,7},{14,8},{8,10},{10,... | collective-permute-start | bytes 884744 | tf_op jit(solution)/shard_map/ppermute | solution.py:537
  51.3 10.8 %copy-start.9 = (bf16[1024,640]{1,0:T(8,128)(2,1)S(1)}, bf16[1024,640]{1,0:T(8,128)(2,1)}, u32[]{:S(2)}) copy-start(bf16[1024,640]{1,0:T(8,128)(2,1)} %copy-done.8) | copy-start | bytes 3932164
  53.1 20.2 %copy-start.5 = (bf16[704,2048]{1,0:T(8,128)(2,1)S(1)}, bf16[704,2048]{1,0:T(8,128)(2,1)}, u32[]{:S(2)}) copy-start(bf16[704,2048]{1,0:T(8,128)(2,1)} %w_down.1) | copy-start | bytes 8650756
  53.1 20.2 %copy-start.7 = (bf16[128,2048]{1,0:T(8,128)(2,1)S(1)}, bf16[128,2048]{1,0:T(8,128)(2,1)}, u32[]{:S(2)}) copy-start(bf16[128,2048]{1,0:T(8,128)(2,1)} %tokens.1) | copy-start | bytes 1572868
  59.5 8.7 %copy-start.2 = (bf16[1024,2048]{1,0:T(8,128)(2,1)S(1)}, bf16[1024,2048]{1,0:T(8,128)(2,1)}, u32[]{:S(2)}) copy-start(bf16[1024,2048]{1,0:T(8,128)(2,1)} %weight.1) | copy-start | bytes 12582916
  59.5 8.7 %collective-permute-start.7 = (bf16[128,1152]{1,0:T(8,128)(2,1)S(1)}, bf16[128,1152]{1,0:T(8,128)(2,1)S(1)}, u32[]{:S(2)}, u32[]{:S(2)}) collective-permute-start(bf16[128,1152]{1,0:T(8,128)(2,1)S(1)} %collective-permute-done.6), channel_id=1, source_target_pairs={{6,0},{0,2},{2,4},{4,6},{7,1},{1,3},{3,5},{5,7},{14,8},{8,10},{10,... | collective-permute-start | bytes 884744 | tf_op jit(solution)/shard_map/ppermute | solution.py:537
  59.5 8.7 %collective-permute-start.8 = (bf16[128,1152]{1,0:T(8,128)(2,1)S(1)}, bf16[128,1152]{1,0:T(8,128)(2,1)S(1)}, u32[]{:S(2)}, u32[]{:S(2)}) collective-permute-start(bf16[128,1152]{1,0:T(8,128)(2,1)S(1)} %attend_3.1), channel_id=1, source_target_pairs={{2,0},{4,2},{6,4},{0,6},{3,1},{5,3},{7,5},{1,7},{10,8},{12,10},{14... | collective-permute-start | bytes 884744 | tf_op jit(solution)/shard_map/ppermute | solution.py:537
  62.1 11.1 %copy-start.4 = (bf16[2048,704]{0,1:T(8,128)(2,1)S(1)}, bf16[2048,704]{0,1:T(8,128)(2,1)}, u32[]{:S(2)}) copy-start(bf16[2048,704]{0,1:T(8,128)(2,1)} %param.27) | copy-start | bytes 8650756
  68.0 5.3 %copy-start.3 = (bf16[2048,704]{0,1:T(8,128)(2,1)S(1)}, bf16[2048,704]{0,1:T(8,128)(2,1)}, u32[]{:S(2)}) copy-start(bf16[2048,704]{0,1:T(8,128)(2,1)} %param.26) | copy-start | bytes 8650756
  68.0 5.3 %copy-start.14 = (bf16[2048]{0:T(1024)(128)(2,1)S(1)}, bf16[2048]{0:T(1024)(128)(2,1)}, u32[]{:S(2)}) copy-start(bf16[2048]{0:T(1024)(128)(2,1)} %gain.3) | copy-start | bytes 12292
  69.7 3.6 %collective-permute-start.9 = (bf16[128,2048]{1,0:T(8,128)(2,1)S(1)}, bf16[128,2048]{1,0:T(8,128)(2,1)S(1)}, u32[]{:S(2)}, u32[]{:S(2)}) collective-permute-start(bf16[128,2048]{1,0:T(8,128)(2,1)S(1)} %get-tuple-element.54), channel_id=1, source_target_pairs={{0,1},{1,0},{2,3},{3,2},{4,5},{5,4},{6,7},{7,6},{8,9},{9,8},{10,11... | collective-permute-start | bytes 1572872 | tf_op jit(solution)/shard_map/ppermute | solution.py:576
  75.9 1.6 %collective-permute-start.10 = (bf16[128,1024]{1,0:T(8,128)(2,1)S(1)}, bf16[128,1024]{1,0:T(8,128)(2,1)S(1)}, u32[]{:S(2)}, u32[]{:S(2)}) collective-permute-start(bf16[128,1024]{1,0:T(8,128)(2,1)S(1)} %get-tuple-element.56), channel_id=1, source_target_pairs={{0,1},{1,0},{2,3},{3,2},{4,5},{5,4},{6,7},{7,6},{8,9},{9,8},{10,11... | collective-permute-start | bytes 786440 | tf_op jit(solution)/shard_map/ppermute | solution.py:586
  (5 other events, 5.6 us)
